TPU v7x, 32 devices: a whole 2x2x4 slice. The times are simulated.
32 devices in a mesh: grp: 2 (over x), gx: 16 (over z, y, core).
Axes of the slice: x: 2, y: 2, z: 4, core: 2. Of those that a mesh axis runs over, the one named last changes fastest.
Arguments:
- rhs: float32 [2048, 16, 128], P('gx', 'grp'), parts along dimension 1
- ham: bfloat16 [2048, 5, 64, 128], P('gx')
- ovl: bfloat16 [2048, 5, 64, 128], P('gx')
- sigma: bfloat16 [8192, 128, 128], P('gx'), as said below
- neighbours: int32 [2048, 5], P('gx'), may hold values from 0 to 2047, as said below
- contact: int32 [128], P('gx'), may hold values from 0 to 2047, as said below
- pole_real: float32 [16], P('grp'), parts along dimension 0, may hold values from -1 to 1
- pole_imag: float32 [16], P('grp'), parts along dimension 0, may hold values from 0.2 to 1.5
Outputs:
- solution: float32 [2048, 16, 128], P('gx', 'grp'), parts along dimension 1
- residual: float32 [2048, 16, 128], P('gx', 'grp'), parts along dimension 1
There are 2 independent parts, one for each index of `grp`. A program takes and returns all parts, laid end to end along the dimension named above; an argument that names none is the same for every part. Nothing has to cross between parts.
Inputs may be any that keep to these rules, and one draw needn't show every extreme that they name: `neighbours`: block index = x column * 16 + row. Row b lists b itself, then a block of the next x column, a block of the previous x column (columns wrap around), and two blocks of its own column. The pattern is symmetric: c stands in slot 1 of b exactly when b stands in slot 2 of c, and in slot 3 of b exactly when b stands in slot 4 of c. contact[s] is a block of x column s. sigma holds a complex symmetric matrix: part g of entry (i, j) equals part g of entry (j, i).
All inputs are finite; a program needn't handle non-finite values.
Results may differ from a plain program's by a relative error of at most 0.0058.
Values may be sent and summed in bfloat16 or wider, within the bound.
No kernel may reach another device: no remote copies, remote signals or barrier semaphores. Data moves between devices by JAX's collectives and lax.ppermute only.
A program may use at most 192 MiB of HBM per device.

v0:
```python
import functools

import jax
import jax.numpy as jnp
from jax import lax
from jax.experimental import pallas as pl
from jax.experimental.pallas import tpu as pltpu
from jax.sharding import PartitionSpec as P

BO = 64
NYB = 16
NNZ = 5
CONTACT = 128
LANES = 2 * BO
TILE = 16
FLOOR_SHARE = 0.0625
SMALL_EPS = 1e-06
F32 = jnp.float32
BF16 = jnp.bfloat16
VMEM = pl.BlockSpec(memory_space=pltpu.VMEM)
SMEM = pl.BlockSpec(memory_space=pltpu.SMEM)


def dot_nt(left, right):
    return lax.dot_general(left, right, (((1,), (1,)), ((), ())), preferred_element_type=F32)


def swap_halves(vec):
    return pltpu.roll(vec, BO, axis=vec.ndim - 1)


def half_sign(ndim):
    lane = lax.broadcasted_iota(jnp.int32, (1,) * (ndim - 1) + (LANES,), ndim - 1)
    return jnp.where(lane < BO, -1.0, 1.0).astype(F32)


def scale(factor, vec):
    fac_re = factor[0]
    fac_im = factor[1] * half_sign(2)
    return fac_re * vec + fac_im * swap_halves(vec)


def complex_mul(a, b):
    return (a[0] * b[0] - a[1] * b[1], a[0] * b[1] + a[1] * b[0])


def guarded_quotient(num, den, bound_sq):
    top = complex_mul(num, (den[0], -den[1]))
    size = jnp.maximum(den[0] * den[0] + den[1] * den[1], FLOOR_SHARE * bound_sq)
    return (top[0] / size, top[1] / size)


def spread(column):
    return jnp.broadcast_to(column, (column.shape[0], LANES))


def pack_columns(columns):
    poles = columns[0].shape[0]
    lane = lax.broadcasted_iota(jnp.int32, (poles, LANES), 1)
    packed = jnp.zeros((poles, LANES), F32)
    for index, column in enumerate(columns):
        packed = jnp.where(lane == index, column, packed)
    return packed


def take_columns(packed, count):
    return [spread(packed[:, index : index + 1]) for index in range(count)]


def lane_sum(vec):
    return jnp.sum(vec, axis=1, keepdims=True)


def store_wide(wide, start, rows, vec):
    lane = lax.broadcasted_iota(jnp.int32, (1, 1, LANES), 2)
    front = jnp.where(lane < BO, vec, -vec)
    wide[pl.ds(start, rows)] = jnp.concatenate([front, swap_halves(vec)], axis=1).astype(BF16)


def chunk_of(partner, me, count):
    slot = jnp.bitwise_xor(partner, me)
    inner = jnp.right_shift(slot, 1)
    y_bit = jnp.bitwise_and(inner, 1)
    return jnp.bitwise_and(slot, 1), y_bit * (count // 4) + jnp.right_shift(inner, 1)


def gathered_sums(near_side, far_side, row):
    total = None
    for index in range(near_side.shape[0]):
        pair = near_side[index, row] + far_side[index, row]
        total = pair if total is None else total + pair
    return total


def place_gathered(target, offset, me, near_side, far_side, cols):
    half = near_side.shape[0]
    for index in range(half):
        y_bit, z_part = index // (half // 2), index % (half // 2)
        partner = jnp.bitwise_xor(me, 2 * y_bit + 4 * z_part)
        target[pl.ds(offset + partner * cols, cols)] = near_side[index, :cols]
        partner = jnp.bitwise_xor(partner, 1)
        target[pl.ds(offset + partner * cols, cols)] = far_side[index, :cols]


def over_rows(count, step, body):
    def run(index, carry):
        body(pl.multiple_of(index * step, step))
        return carry

    lax.fori_loop(0, count // step, run, 0)


def sum_rows(count, step, body, terms, poles):
    def run(index, carry):
        parts = body(pl.multiple_of(index * step, step))
        return tuple(c + jnp.sum(p, axis=0) for c, p in zip(carry, parts))

    zero = jnp.zeros((poles, LANES), F32)
    return lax.fori_loop(0, count // step, run, (zero,) * terms)


def halo_starts(me, blocks):
    odd = jnp.bitwise_and(me, 1)
    return (1 - odd) * (NYB + blocks), odd * (NYB + blocks)


def edge_start(kind, me, blocks):
    odd = jnp.bitwise_and(me, 1)
    return (1 - odd if kind == 0 else odd) * (blocks - NYB)


def fill_extended(ext, partner, own, other, me, near_side, far_side, cols):
    blocks = own.shape[0]
    partner_start, other_start = halo_starts(me, blocks)
    ext[pl.ds(partner_start, NYB)] = partner[...]
    ext[pl.ds(other_start, NYB)] = other[...]
    ext[NYB : NYB + blocks] = own[...]
    place_gathered(ext, 2 * NYB + blocks, me, near_side, far_side, cols)


def combine(poles_ref, result):
    poles = poles_ref.shape[0]
    z = take_columns(poles_ref[...], 2)
    left = lax.broadcasted_iota(jnp.int32, (poles, LANES), 1) < BO
    top, low = result[:poles], result[poles:]
    ham_part = jnp.where(left, top, swap_halves(low))
    ovl_part = jnp.where(left, swap_halves(top), low)
    return scale(z, ovl_part) - ham_part


def ovl_base(blocks):
    return blocks * NNZ // 2


def sparse_block(mats, base, pair, index):
    half = index % 2
    return mats[base + NNZ * pair + index // 2, BO * half : BO * (half + 1)]


def sparse_group(near, poles_ref, wide, mats, blocks, image, first, count, shift=0):
    rows = 2 * image.shape[1]
    bases = (0, ovl_base(blocks))
    for pair in range(count // 2):
        b = first + 2 * pair
        vectors, matrices = [], []
        for q in range(2):
            vectors.append(jnp.concatenate([wide[near[(b + q) * NNZ + k]] for k in range(NNZ)], axis=1))
            for base in bases:
                pieces = [
                    sparse_block(mats, base, first // 2 + pair, q * NNZ + k) for k in range(NNZ)
                ]
                matrices.append(jnp.concatenate(pieces, axis=1))
        result = dot_nt(jnp.concatenate(vectors, axis=0), jnp.concatenate(matrices, axis=0))
        for q in range(2):
            image[b + q - shift] = combine(
                poles_ref, result[rows * q : rows * (q + 1), LANES * q : LANES * (q + 1)]
            )


def part_copy(source, mats, base, sem, part):
    size = source.shape[0] // sem.shape[0]
    return pltpu.make_async_copy(
        source.at[pl.ds(part * size, size)],
        mats.at[pl.ds(base + part * size, size)],
        sem.at[part],
    )


def start_sparse(ham, ovl, mats, sems):
    base = ovl_base(2 * ham.shape[0] // NNZ)
    for part in range(sems[0].shape[0]):
        part_copy(ham, mats, 0, sems[0], part).start()
        part_copy(ovl, mats, base, sems[1], part).start()


def start_sigma(sigma, mats, sem):
    base = mats.shape[0] - sigma.shape[0]
    for part in range(sem.shape[0]):
        part_copy(sigma, mats, base, sem, part).start()


def start_matrices(ham, ovl, sigma, mats, sems):
    start_sparse(ham, ovl, mats, sems)
    start_sigma(sigma, mats, sems[2])


def sparse_part(near, poles_ref, wide, ham, ovl, mats, sems, image):
    parts = sems[0].shape[0]
    blocks = image.shape[0]
    size = blocks // parts

    def step(part, carry):
        part_copy(ham, mats, 0, sems[0], part).wait()
        part_copy(ovl, mats, ovl_base(blocks), sems[1], part).wait()
        sparse_group(near, poles_ref, wide, mats, blocks, image, part * size, size)
        return carry

    lax.fori_loop(0, parts, step, 0)


def edge_part(near, poles_ref, wide, mats, image):
    blocks = image.shape[0]
    for first, slot in ((0, 2), (blocks - NYB, 1)):

        def step(group, carry, first=first, slot=slot):
            for index in range(4):
                pair = first // 2 + 4 * group + index
                for q in range(2):
                    b = 2 * pair + q
                    pieces = [
                        sparse_block(mats, base, pair, q * NNZ + slot)
                        for base in (0, ovl_base(blocks))
                    ]
                    product = dot_nt(wide[near[b * NNZ + slot]], jnp.concatenate(pieces, axis=0))
                    image[b] = image[b] + combine(poles_ref, product)
            return carry

        lax.fori_loop(0, NYB // 8, step, 0)


def contact_part(spots, wide, sigma, mats, sem, acc, image):
    blocks, poles = image.shape[0], image.shape[1]
    cols = spots.shape[0]
    first_contact = blocks + 2 * NYB
    base = blocks * NNZ
    group_rows = sigma.shape[0] // sem.shape[0]
    width = TILE * 2 * poles
    row_t = lax.broadcasted_iota(jnp.int32, (TILE, width), 0)
    col_t = lax.broadcasted_iota(jnp.int32, (TILE, width), 1) // (2 * poles)
    keep = (row_t == col_t)[None]

    def step(group, carry):
        part_copy(sigma, mats, base, sem, group).wait()
        start = base + group * group_rows
        total = None
        for pair in range(CONTACT // (2 * TILE)):
            slabs, vectors = [], []
            for side in range(2):
                first = (2 * pair + side) * TILE
                slab = mats[pl.ds(start, group_rows), first : first + TILE]
                slabs.append(slab.reshape(group_rows * TILE, LANES))
                vectors.append(
                    wide[first_contact + first : first_contact + first + TILE].reshape(width, LANES)
                )
            part = dot_nt(jnp.concatenate(slabs, axis=1), jnp.concatenate(vectors, axis=1))
            total = part if total is None else total + part
        kept = jnp.where(keep, total.reshape(group_rows, TILE, width), 0.0)
        acc[pl.ds(pl.multiple_of(group * group_rows, group_rows), group_rows)] = jnp.sum(kept, axis=1)
        return carry

    lax.fori_loop(0, sem.shape[0], step, 0)
    fold_row = lax.broadcasted_iota(jnp.int32, (2 * poles, width), 0)
    fold_col = lax.broadcasted_iota(jnp.int32, (2 * poles, width), 1) % (2 * poles)
    fold = jnp.where(fold_row == fold_col, 1.0, 0.0).astype(BF16)
    rest = acc[...]
    folded = None
    for _ in range(2):
        piece = rest.astype(BF16)
        part = dot_nt(fold, piece)
        folded = part if folded is None else folded + part
        rest = rest - piece.astype(F32)
    for l in range(cols):
        column = slice(BO * l, BO * (l + 1))
        product = jnp.concatenate([folded[:poles, column], folded[poles:, column]], axis=1)
        spot = spots[l]
        image[spot] = image[spot] - product


def apply_operator(near, spots, poles_ref, wide, ham, ovl, sigma, mats, sems, acc, image):
    sparse_part(near, poles_ref, wide, ham, ovl, mats, sems, image)
    contact_part(spots, wide, sigma, mats, sems[2], acc, image)


def store_chunk(chunk, edge_a, edge_b, me, spots, image, sums):
    cols = spots.shape[0]
    blocks = image.shape[0]
    edge_a[...] = image[pl.ds(edge_start(0, me, blocks), NYB)]
    edge_b[...] = image[pl.ds(edge_start(1, me, blocks), NYB)]
    for l in range(cols):
        chunk[l] = image[spots[l]]
    chunk[cols] = sums


def inner_terms(a, c):
    return a * c, a * swap_halves(c)


def inner_pair(re_acc, im_acc):
    return lane_sum(re_acc), lane_sum(im_acc * -half_sign(2))


def prepare_kernel(me_ref, spots, rhs, chunk, edge_a, edge_b, sem):
    blocks, poles = rhs.shape[0], rhs.shape[1]
    cols = spots.shape[0]
    copies = [pltpu.make_async_copy(rhs.at[spots[l]], chunk.at[l], sem.at[l]) for l in range(cols)]
    for kind, edge in enumerate((edge_a, edge_b)):
        here = pl.ds(edge_start(kind, me_ref[0], blocks), NYB)
        copies.append(pltpu.make_async_copy(rhs.at[here], edge, sem.at[cols + kind]))
    for copy in copies:
        copy.start()
    chunk[cols] = jnp.zeros((poles, LANES), F32)
    for copy in copies:
        copy.wait()


def own_kernel(first, near, poles_ref, own, ham, ovl, image, wide, mats, *sems):
    blocks = own.shape[0]
    parts = sems[0].shape[0]
    size = image.shape[0] // parts
    slabs = size * NNZ // 2
    start = first * NNZ // 2

    def copies(part):
        for source, base, sem in ((ham, 0, sems[0]), (ovl, ovl_base(blocks), sems[1])):
            yield pltpu.make_async_copy(
                source.at[pl.ds(start + part * slabs, slabs)],
                mats.at[pl.ds(base + start + part * slabs, slabs)],
                sem.at[part],
            )

    for part in range(parts):
        for copy in copies(part):
            copy.start()
    wide[0:NYB] = jnp.zeros((NYB, *wide.shape[1:]), BF16)
    wide[NYB + blocks : 2 * NYB + blocks] = jnp.zeros((NYB, *wide.shape[1:]), BF16)
    low = max(0, first - NYB)
    needed = min(blocks, first + image.shape[0] + NYB) - low
    over_rows(
        needed, TILE,
        lambda s: store_wide(wide, NYB + low + s, TILE, own[pl.ds(low + s, TILE)]),
    )

    def step(part, carry):
        for copy in copies(part):
            copy.wait()
        sparse_group(
            near, poles_ref, wide, mats, blocks, image, first + part * size, size, shift=first
        )
        return carry

    lax.fori_loop(0, parts, step, 0)


def first_kernel(
    me_ref, near, spots, poles_ref, own, image_front, image_back, partner, other, near_side, far_side, ham, ovl, sigma,
    rhs_ext, image, chunk, edge_a, edge_b, wide, acc, mats, *sems,
):
    blocks, poles = own.shape[0], own.shape[1]
    edge_slabs = NYB * NNZ // 2
    edges = []
    for source, base, sem in ((ham, 0, sems[0]), (ovl, ovl_base(blocks), sems[1])):
        for side, start in enumerate((0, (blocks - NYB) * NNZ // 2)):
            edges.append(
                pltpu.make_async_copy(
                    source.at[pl.ds(start, edge_slabs)],
                    mats.at[pl.ds(base + start, edge_slabs)],
                    sem.at[side],
                )
            )
    for copy in edges:
        copy.start()
    start_sigma(sigma, mats, sems[2])
    fill_extended(rhs_ext, partner, own, other, me_ref[0], near_side, far_side, spots.shape[0])
    store_wide(wide, 0, NYB, rhs_ext[0:NYB])
    over_rows(
        NYB + CONTACT, TILE,
        lambda s: store_wide(wide, NYB + blocks + s, TILE, rhs_ext[pl.ds(NYB + blocks + s, TILE)]),
    )
    image[0 : blocks // 2] = image_front[...]
    image[blocks // 2 : blocks] = image_back[...]
    for copy in edges:
        copy.wait()
    edge_part(near, poles_ref, wide, mats, image)
    contact_part(spots, wide, sigma, mats, sems[2], acc, image)

    def terms(s):
        b, v = own[pl.ds(s, TILE)], image[pl.ds(s, TILE)]
        return (b * b, *inner_terms(b, v), v * v)

    bb, bv_re, bv_im, vv = sum_rows(blocks, TILE, terms, 4, poles)
    store_chunk(
        chunk, edge_a, edge_b, me_ref[0], spots, image, pack_columns([lane_sum(bb), *inner_pair(bv_re, bv_im), lane_sum(vv)])
    )


def second_kernel(
    me_ref, near, spots, poles_ref, rhs_ext, own, partner, other, near_side, far_side, ham, ovl, sigma,
    image_ext, half_ext, turned, chunk, edge_a, edge_b, scalars, wide, acc, mats,
    *sems,
):
    start_matrices(ham, ovl, sigma, mats, sems)
    blocks, poles = own.shape[0], own.shape[1]
    cols = spots.shape[0]
    fill_extended(image_ext, partner, own, other, me_ref[0], near_side, far_side, cols)
    norm_b, bv_re, bv_im, vv = take_columns(gathered_sums(near_side, far_side, cols), 4)
    alpha = guarded_quotient((norm_b, jnp.zeros_like(norm_b)), (bv_re, bv_im), norm_b * vv)
    scalars[0] = norm_b
    scalars[1] = alpha[0]
    scalars[2] = alpha[1]

    def update(s):
        half = rhs_ext[pl.ds(s, TILE)] - scale(alpha, image_ext[pl.ds(s, TILE)])
        half_ext[pl.ds(s, TILE)] = half
        store_wide(wide, s, TILE, half)

    over_rows(half_ext.shape[0], TILE, update)
    apply_operator(near, spots, poles_ref, wide, ham, ovl, sigma, mats, sems, acc, turned)

    def terms(s):
        b = rhs_ext[pl.ds(NYB + s, TILE)]
        h = half_ext[pl.ds(NYB + s, TILE)]
        t = turned[pl.ds(s, TILE)]
        return (*inner_terms(t, h), t * t, h * h, *inner_terms(b, h), *inner_terms(b, t))

    th_re, th_im, tt, hh, bh_re, bh_im, bt_re, bt_im = sum_rows(blocks, TILE, terms, 8, poles)
    columns = [
        *inner_pair(th_re, th_im), lane_sum(tt), lane_sum(hh),
        *inner_pair(bh_re, bh_im), *inner_pair(bt_re, bt_im),
    ]
    store_chunk(chunk, edge_a, edge_b, me_ref[0], spots, turned, pack_columns(columns))


def third_kernel(
    me_ref, near, spots, poles_ref, scalars, rhs_ext, image_ext, half_ext, own, partner, other,
    near_side, far_side, ham, ovl, sigma,
    residual_own, direction_own, residual_rem, direction_rem, iterate, image, chunk, edge_a,
    edge_b, rho_out, turned_ext, wide, acc, mats, *sems,
):
    start_matrices(ham, ovl, sigma, mats, sems)
    blocks, poles = own.shape[0], own.shape[1]
    cols = spots.shape[0]
    fill_extended(turned_ext, partner, own, other, me_ref[0], near_side, far_side, cols)
    sums = take_columns(gathered_sums(near_side, far_side, cols), 8)
    th, tt, hh, bh, bt = (sums[0], sums[1]), sums[2], sums[3], (sums[4], sums[5]), (sums[6], sums[7])
    norm_b, alpha = scalars[0], (scalars[1], scalars[2])
    turned_sq = tt + SMALL_EPS
    omega = (th[0] / turned_sq, th[1] / turned_sq)
    minus = complex_mul(omega, bt)
    rho_next = (bh[0] - minus[0], bh[1] - minus[1])
    zeros = jnp.zeros_like(tt)
    inverse_omega = guarded_quotient((turned_sq, zeros), th, tt * hh)
    ratio = complex_mul(rho_next, complex_mul(alpha, inverse_omega))
    beta = (ratio[0] / norm_b, ratio[1] / norm_b)
    rho_out[0] = rho_next[0]
    rho_out[1] = rho_next[1]
    rho_out[2] = norm_b

    def update(s):
        half = half_ext[pl.ds(s, TILE)]
        residual = half - scale(omega, turned_ext[pl.ds(s, TILE)])
        old = rhs_ext[pl.ds(s, TILE)]
        direction = residual + scale(beta, old - scale(omega, image_ext[pl.ds(s, TILE)]))
        store_wide(wide, s, TILE, direction)
        return residual, direction

    def update_own(s):
        residual, direction = update(NYB + s)
        residual_own[pl.ds(s, TILE)] = residual
        direction_own[pl.ds(s, TILE)] = direction
        iterate[pl.ds(s, TILE)] = scale(alpha, rhs_ext[pl.ds(NYB + s, TILE)]) + scale(
            omega, half_ext[pl.ds(NYB + s, TILE)]
        )

    def update_rest(source, target):
        residual, direction = update(source)
        residual_rem[pl.ds(target, TILE)] = residual
        direction_rem[pl.ds(target, TILE)] = direction

    over_rows(blocks, TILE, update_own)
    update_rest(0, 0)
    over_rows(NYB + CONTACT, TILE, lambda s: update_rest(NYB + blocks + s, NYB + s))
    apply_operator(near, spots, poles_ref, wide, ham, ovl, sigma, mats, sems, acc, image)

    def terms(s):
        b, v = rhs_ext[pl.ds(NYB + s, TILE)], image[pl.ds(s, TILE)]
        return (*inner_terms(b, v), v * v)

    bv_re, bv_im, vv = sum_rows(blocks, TILE, terms, 3, poles)
    store_chunk(chunk, edge_a, edge_b, me_ref[0], spots, image, pack_columns([*inner_pair(bv_re, bv_im), lane_sum(vv)]))


def fourth_kernel(
    me_ref, near, spots, poles_ref, rho_in, residual_own, direction_own, residual_rem,
    direction_rem, iterate_in, own, partner, other, near_side, far_side, ham, ovl, sigma,
    half_own, turned, iterate, sums_out, contact_image, wide, acc, mats, *sems,
):
    start_matrices(ham, ovl, sigma, mats, sems)
    blocks, poles = own.shape[0], own.shape[1]
    cols = spots.shape[0]
    place_gathered(contact_image, 0, me_ref[0], near_side, far_side, cols)
    bv_re, bv_im, vv = take_columns(gathered_sums(near_side, far_side, cols), 3)
    norm_b = rho_in[2]
    alpha = guarded_quotient((rho_in[0], rho_in[1]), (bv_re, bv_im), norm_b * vv)

    def update_own(s):
        here = pl.ds(s, TILE)
        half = residual_own[here] - scale(alpha, own[here])
        half_own[here] = half
        iterate[here] = iterate_in[here] + scale(alpha, direction_own[here])
        store_wide(wide, NYB + s, TILE, half)

    over_rows(blocks, TILE, update_own)
    for start, image in zip(halo_starts(me_ref[0], blocks), (partner, other)):
        remote = jnp.where(start == 0, 0, NYB)
        half = residual_rem[pl.ds(remote, NYB)] - scale(alpha, image[...])
        store_wide(wide, start, NYB, half)

    def update_contact(s):
        half = residual_rem[pl.ds(2 * NYB + s, TILE)] - scale(alpha, contact_image[pl.ds(s, TILE)])
        store_wide(wide, 2 * NYB + blocks + s, TILE, half)

    over_rows(CONTACT, TILE, update_contact)
    apply_operator(near, spots, poles_ref, wide, ham, ovl, sigma, mats, sems, acc, turned)

    def terms(s):
        h, t = half_own[pl.ds(s, TILE)], turned[pl.ds(s, TILE)]
        return (*inner_terms(t, h), t * t)

    th_re, th_im, tt = sum_rows(blocks, TILE, terms, 3, poles)
    sums_out[0] = pack_columns([*inner_pair(th_re, th_im), lane_sum(tt)])


def last_kernel(near_side, far_side, half_own, turned, iterate, solution_out, residual_out):
    th_re, th_im, tt = take_columns(gathered_sums(near_side, far_side, 0), 3)
    turned_sq = tt + SMALL_EPS
    omega = (th_re / turned_sq, th_im / turned_sq)

    def update(s):
        here = pl.ds(s, TILE)
        half = half_own[here]
        solution_out[here] = iterate[here] + scale(omega, half)
        residual_out[here] = half - scale(omega, turned[here])

    over_rows(half_own.shape[0], TILE, update)


def local(rhs, ham, ovl, sigma, neighbours, contact, pole_real, pole_imag):
    blocks, poles = rhs.shape[0], rhs.shape[1]
    cols = contact.shape[0]
    count = lax.axis_size("gx")
    me = lax.axis_index("gx")
    first_block = me * blocks
    near = ((neighbours - first_block + NYB) % (blocks * count)).reshape(-1)
    spots = contact - first_block
    me_ref = jnp.reshape(me, (1,)).astype(jnp.int32)
    lane = jnp.arange(LANES)[None, :]
    poles_ref = jnp.where(lane == 0, pole_real[:, None], pole_imag[:, None])
    ext = blocks + 2 * NYB + CONTACT

    def flip(value, mask):
        return lax.ppermute(value, "gx", [(i, i ^ mask) for i in range(count)])

    def exchange(chunk, edges=None, beside=()):
        parts = [chunk] + [flip(chunk, mask) for mask in range(4, count, 4)]
        far = ()
        if edges is not None:
            other = [(i, (i + 1 if i % 2 else i - 1) % count) for i in range(count)]
            far = (lax.ppermute(edges[1], "gx", other),)
        early, line = lax.optimization_barrier((beside[:1], jnp.stack(parts)))
        plane = jnp.concatenate([line, flip(line, 2)])
        if edges is None:
            return plane, flip(plane, 1)
        far, late, plane = lax.optimization_barrier((far, beside[1:], plane))
        return (*early, *late, flip(edges[0], 1), *far, plane, flip(plane, 1))

    def vec_shape(rows):
        return jax.ShapeDtypeStruct((rows, poles, LANES), F32)

    slabs = (ham.reshape(-1, LANES, LANES), ovl.reshape(-1, LANES, LANES), sigma)
    small = pltpu.CompilerParams(vmem_limit_bytes=8 << 20)
    large = pltpu.CompilerParams(vmem_limit_bytes=43 << 20)
    wide = pltpu.VMEM((ext, 2 * poles, LANES), BF16)
    acc = pltpu.VMEM((sigma.shape[0], TILE * 2 * poles), F32)
    held = pltpu.VMEM((sum(m.shape[0] for m in slabs), LANES, LANES), BF16)
    parts = max(2, blocks // 32)
    sems = [pltpu.SemaphoreType.DMA((p,)) for p in (parts, parts, sigma.shape[0] // BO)]
    hbm = pl.BlockSpec(memory_space=pl.ANY)
    fixed = (me_ref, near, spots, poles_ref)
    remote = 2 * NYB + CONTACT
    rows = cols + 1

    def call(kernel, inputs, out_rows, scratch, name):
        scratch = [pltpu.VMEM((r, poles, LANES), F32) for r in scratch]
        return pl.pallas_call(
            kernel,
            in_specs=[SMEM] * 3 + [VMEM] * (len(inputs) - 3) + [hbm] * 3,
            out_specs=[VMEM] * len(out_rows),
            out_shape=[vec_shape(r) for r in out_rows],
            scratch_shapes=[*scratch, wide, acc, held, *sems],
            compiler_params=large,
            name=name,
        )(*inputs, *slabs)

    chunk, *edges = pl.pallas_call(
        prepare_kernel,
        in_specs=[SMEM, SMEM, pl.BlockSpec(memory_space=pl.ANY)],
        out_specs=[VMEM] * 3,
        out_shape=[vec_shape(rows), vec_shape(NYB), vec_shape(NYB)],
        scratch_shapes=[pltpu.SemaphoreType.DMA((cols + 2,))],
        compiler_params=small,
        name="prepare",
    )(me_ref, spots, rhs)
    half = blocks // 2

    def own_part(first):
        return pl.pallas_call(
            functools.partial(own_kernel, first),
            in_specs=[SMEM] + [VMEM] * 2 + [hbm] * 2,
            out_specs=VMEM,
            out_shape=vec_shape(half),
            scratch_shapes=[wide, held, *([pltpu.SemaphoreType.DMA((max(1, half // 32),))] * 2)],
            compiler_params=pltpu.CompilerParams(vmem_limit_bytes=54 << 20),
            cost_estimate=pl.CostEstimate(
                flops=2 * ham.size * 2 * poles, bytes_accessed=2 * ham.size, transcendentals=0
            ),
            name="own",
        )(near, poles_ref, rhs, *slabs[:2])

    rhs_ext, image, chunk, edge_a, edge_b = call(
        first_kernel, (*fixed, rhs, *exchange(chunk, edges, (own_part(0), own_part(half)))),
        [ext, blocks, rows, NYB, NYB], [], "first",
    )
    image_ext, half_ext, turned, chunk, edge_a, edge_b, scalars = call(
        second_kernel, (*fixed, rhs_ext, image, *exchange(chunk, (edge_a, edge_b))),
        [ext, ext, blocks, rows, NYB, NYB, 3], [], "second",
    )
    res_own, dir_own, res_rem, dir_rem, iterate, image, chunk, edge_a, edge_b, rho = call(
        third_kernel,
        (*fixed, scalars, rhs_ext, image_ext, half_ext, turned, *exchange(chunk, (edge_a, edge_b))),
        [blocks, blocks, remote, remote, blocks, blocks, rows, NYB, NYB, 3], [ext], "third",
    )
    half_own, turned, iterate, sums = call(
        fourth_kernel,
        (*fixed, rho, res_own, dir_own, res_rem, dir_rem, iterate, image,
         *exchange(chunk, (edge_a, edge_b))),
        [blocks, blocks, blocks, 1], [CONTACT], "fourth",
    )
    return tuple(
        pl.pallas_call(
            last_kernel,
            in_specs=[VMEM] * 5,
            out_specs=[VMEM] * 2,
            out_shape=[vec_shape(blocks)] * 2,
            compiler_params=small,
            name="last",
        )(*exchange(sums), half_own, turned, iterate)
    )


def solution(mesh):
    return jax.shard_map(
        local,
        mesh=mesh,
        in_specs=(
            P("gx", "grp", None),
            P("gx", None, None, None),
            P("gx", None, None, None),
            P("gx", None, None),
            P("gx", None),
            P("gx"),
            P("grp"),
            P("grp"),
        ),
        out_specs=(P("gx", "grp", None), P("gx", "grp", None)),
        check_vma=False,
    )
```

profile of v0, /device:TPU:0, one launch (start us, length us, event | category | flops | bytes accessed | tf_op | source)
XLA Modules:
  0.0 163.2 jit_solution(9831864819263243922)
XLA Ops:
  0.6 0.7 broadcast_subtract_fusion.spots
  1.3 1.0 copy-done
  2.3 0.9 prepare.1
  3.2 5.1 %collective-permute-start.2 = (f32[9,8,128]{2,1,0:T(8,128)S(1)}, f32[9,8,128]{2,1,0:T(8,128)S(1)}, u32[]{:S(2)}, u32[]{:S(2)}) collective-permute-start(f32[9,8,128]{2,1,0:T(8,128)S(1)} %get-tuple-element.42), channel_id=1, source_target_pairs={{0,12},{1,13},{2,14},{3,15},{4,8},{5,9},{6,10},{7,11},{8,4},{9,5},... | collective-permute-start | bytes 110600 | tf_op jit(solution)/shard_map/ppermute | solution.py:571
  8.3 0.6 collective-permute-start
  9.0 0.7 add_select_fusion
  9.7 1.3 broadcast_select_fusion.poles_ref
  11.0 0.1 copy.10
  11.1 0.8 reshape.24.near
  11.9 8.0 %own.5.image_front = f32[64,8,128]{2,1,0:T(8,128)} custom-call(s32[640]{0:T(1024)} %reshape.24.near, f32[8,128]{1,0:T(8,128)} %broadcast_select_fusion.poles_ref, f32[128,8,128]{2,1,0:T(8,128)} %own.9, bf16[320,128,128]{2,1,0:T(8,128)(2,1)} %bitcast.28, bf16[320,128,128]{2,1,0:T(8,128)(2,1)} %bitcast.34), custom_call_target="tpu_custom_call" | custom-call | flops 167772160 | bytes 10485760 | tf_op jit(solution)/shard_map/own/pallas_call | solution.py:626
  20.0 1.7 %collective-permute-start.4 = (f32[4,9,8,128]{3,2,1,0:T(8,128)S(1)}, f32[4,9,8,128]{3,2,1,0:T(8,128)S(1)}, u32[]{:S(2)}, u32[]{:S(2)}) collective-permute-start(f32[4,9,8,128]{3,2,1,0:T(8,128)S(1)} %pad_maximum_fusion.4), channel_id=1, source_target_pairs={{0,2},{1,3},{2,0},{3,1},{4,6},{5,7},{6,4},{7,5},{8,10},{9,11},{10,... | collective-permute-start | bytes 442376 | tf_op jit(solution)/shard_map/ppermute | solution.py:571
  21.7 1.9 %collective-permute-start.3 = (f32[16,8,128]{2,1,0:T(8,128)S(1)}, f32[16,8,128]{2,1,0:T(8,128)S(1)}, u32[]{:S(2)}, u32[]{:S(2)}) collective-permute-start(f32[16,8,128]{2,1,0:T(8,128)S(1)} %get-tuple-element.44), channel_id=1, source_target_pairs={{0,15},{1,2},{2,1},{3,4},{4,3},{5,6},{6,5},{7,8},{8,7},{9,10},{10,... | collective-permute-start | bytes 196616 | tf_op jit(solution)/shard_map/ppermute | solution.py:578
  23.6 8.0 %own.7.image_back = f32[64,8,128]{2,1,0:T(8,128)} custom-call(s32[640]{0:T(1024)} %reshape.24.near, f32[8,128]{1,0:T(8,128)} %broadcast_select_fusion.poles_ref, f32[128,8,128]{2,1,0:T(8,128)} %own.9, bf16[320,128,128]{2,1,0:T(8,128)(2,1)} %bitcast.29, bf16[320,128,128]{2,1,0:T(8,128)(2,1)} %bitcast.35), custom_call_target="tpu_custom_call" | custom-call | flops 167772160 | bytes 10485760 | tf_op jit(solution)/shard_map/own/pallas_call | solution.py:626
  31.7 0.1 collective-permute-start.6
  31.8 0.5 collective-permute-start.5
  32.3 1.2 collective-permute-done.5.partner
  33.5 0.9 copy-done.3
  34.4 12.0 %first.1 = (f32[288,8,128]{2,1,0:T(8,128)S(1)}, f32[128,8,128]{2,1,0:T(8,128)S(1)}, f32[9,8,128]{2,1,0:T(8,128)S(1)}, f32[16,8,128]{2,1,0:T(8,128)S(1)}, f32[16,8,128]{2,1,0:T(8,128)S(1)}) custom-call(s32[1]{0:T(128)} %bitcast.me_ref, s32[640]{0:T(1024)S(1)} %copy-done.5, s32[8]{0:T(128)S(1)} %broadcast_subtract_fusion.spots, f32[8,128]{1,0:T(8,128)S(1)} %copy-done.4, ...), custom_call_target="tpu_custom_call" | custom-call | tf_op jit(solution)/shard_map/first/pallas_call | solution.py:604
  46.4 2.1 %collective-permute-start.11 = (f32[9,8,128]{2,1,0:T(8,128)S(1)}, f32[9,8,128]{2,1,0:T(8,128)S(1)}, u32[]{:S(2)}, u32[]{:S(2)}) collective-permute-start(f32[9,8,128]{2,1,0:T(8,128)S(1)} %get-tuple-element.54), channel_id=1, source_target_pairs={{0,12},{1,13},{2,14},{3,15},{4,8},{5,9},{6,10},{7,11},{8,4},{9,5},... | collective-permute-start | bytes 110600 | tf_op jit(solution)/shard_map/ppermute | solution.py:571
  48.5 2.4 %collective-permute-start.9 = (f32[9,8,128]{2,1,0:T(8,128)S(1)}, f32[9,8,128]{2,1,0:T(8,128)S(1)}, u32[]{:S(2)}, u32[]{:S(2)}) collective-permute-start(f32[9,8,128]{2,1,0:T(8,128)S(1)} %get-tuple-element.54), channel_id=1, source_target_pairs={{0,4},{1,5},{2,6},{3,7},{4,0},{5,1},{6,2},{7,3},{8,12},{9,13},{10,... | collective-permute-start | bytes 110600 | tf_op jit(solution)/shard_map/ppermute | solution.py:571
  50.9 1.4 collective-permute-done.11
  52.3 1.2 collective-permute-done.10
  53.5 0.1 collective-permute-done.9
  53.6 1.1 collective-permute-start.12
  54.7 1.8 %collective-permute-start.8 = (f32[16,8,128]{2,1,0:T(8,128)S(1)}, f32[16,8,128]{2,1,0:T(8,128)S(1)}, u32[]{:S(2)}, u32[]{:S(2)}) collective-permute-start(f32[16,8,128]{2,1,0:T(8,128)S(1)} %get-tuple-element.53), channel_id=1, source_target_pairs={{0,15},{1,2},{2,1},{3,4},{4,3},{5,6},{6,5},{7,8},{8,7},{9,10},{10,... | collective-permute-start | bytes 196616 | tf_op jit(solution)/shard_map/ppermute | solution.py:578
  56.5 2.6 %collective-permute-done.12 = f32[4,9,8,128]{3,2,1,0:T(8,128)S(1)} collective-permute-done((f32[4,9,8,128]{3,2,1,0:T(8,128)S(1)}, f32[4,9,8,128]{3,2,1,0:T(8,128)S(1)}, u32[]{:S(2)}, u32[]{:S(2)}) %collective-permute-start.12) | collective-permute-done | bytes 147488 | tf_op jit(solution)/shard_map/ppermute | solution.py:571
  59.1 2.0 %collective-permute-done.8.other = f32[16,8,128]{2,1,0:T(8,128)S(1)} collective-permute-done((f32[16,8,128]{2,1,0:T(8,128)S(1)}, f32[16,8,128]{2,1,0:T(8,128)S(1)}, u32[]{:S(2)}, u32[]{:S(2)}) %collective-permute-start.8) | collective-permute-done | bytes 65568 | tf_op jit(solution)/shard_map/ppermute | solution.py:578
  61.1 0.5 collective-permute-start.7
  61.6 1.2 collective-permute-done.7.partner
  62.8 18.3 %second.1 = (f32[288,8,128]{2,1,0:T(8,128)S(1)}, f32[288,8,128]{2,1,0:T(8,128)S(1)}, f32[128,8,128]{2,1,0:T(8,128)S(1)}, f32[9,8,128]{2,1,0:T(8,128)S(1)}, f32[1...) custom-call(s32[1]{0:T(128)} %bitcast.me_ref, s32[640]{0:T(1024)S(1)} %copy-done.5, ...), custom_call_target="tpu_custom_call" | custom-call | tf_op jit(solution)/shard_map/second/pallas_call | solution.py:604
  81.1 1.3 collective-permute-start.18
  82.4 0.1 collective-permute-start.17
  82.5 3.1 %collective-permute-start.16 = (f32[9,8,128]{2,1,0:T(8,128)S(1)}, f32[9,8,128]{2,1,0:T(8,128)S(1)}, u32[]{:S(2)}, u32[]{:S(2)}) collective-permute-start(f32[9,8,128]{2,1,0:T(8,128)S(1)} %get-tuple-element.63), channel_id=1, source_target_pairs={{0,4},{1,5},{2,6},{3,7},{4,0},{5,1},{6,2},{7,3},{8,12},{9,13},{10,... | collective-permute-start | bytes 110600 | tf_op jit(solution)/shard_map/ppermute | solution.py:571
  85.5 1.4 collective-permute-done.18
  86.9 1.2 collective-permute-done.17
  88.1 0.1 collective-permute-done.16
  88.2 0.6 collective-permute-start.19
  88.8 1.1 collective-permute-start.15
  89.9 4.0 %collective-permute-done.19 = f32[4,9,8,128]{3,2,1,0:T(8,128)S(1)} collective-permute-done((f32[4,9,8,128]{3,2,1,0:T(8,128)S(1)}, f32[4,9,8,128]{3,2,1,0:T(8,128)S(1)}, u32[]{:S(2)}, u32[]{:S(2)}) %collective-permute-start.19) | collective-permute-done | bytes 147488 | tf_op jit(solution)/shard_map/ppermute | solution.py:571
  93.9 1.3 collective-permute-done.15.other
  95.3 0.5 collective-permute-start.14
  95.8 1.2 collective-permute-done.14.partner
  96.9 19.5 %third.1 = (f32[128,8,128]{2,1,0:T(8,128)S(1)}, f32[128,8,128]{2,1,0:T(8,128)S(1)}, f32[160,8,128]{2,1,0:T(8,128)S(1)}, f32[160,8,128]{2,1,0:T(8,128)S(1)}, f32[...) custom-call(s32[1]{0:T(128)} %bitcast.me_ref, ...), custom_call_target="tpu_custom_call" | custom-call | tf_op jit(solution)/shard_map/third/pallas_call | solution.py:604
  116.4 0.7 collective-permute-start.25
  117.2 1.1 collective-permute-start.24
  118.3 2.6 %collective-permute-start.23 = (f32[9,8,128]{2,1,0:T(8,128)S(1)}, f32[9,8,128]{2,1,0:T(8,128)S(1)}, u32[]{:S(2)}, u32[]{:S(2)}) collective-permute-start(f32[9,8,128]{2,1,0:T(8,128)S(1)} %get-tuple-element.75), channel_id=1, source_target_pairs={{0,4},{1,5},{2,6},{3,7},{4,0},{5,1},{6,2},{7,3},{8,12},{9,13},{10,... | collective-permute-start | bytes 110600 | tf_op jit(solution)/shard_map/ppermute | solution.py:571
  120.9 1.7 %collective-permute-done.25 = f32[9,8,128]{2,1,0:T(8,128)S(1)} collective-permute-done((f32[9,8,128]{2,1,0:T(8,128)S(1)}, f32[9,8,128]{2,1,0:T(8,128)S(1)}, u32[]{:S(2)}, u32[]{:S(2)}) %collective-permute-start.25) | collective-permute-done | bytes 36896 | tf_op jit(solution)/shard_map/ppermute | solution.py:571
  122.6 0.4 collective-permute-done.24
  123.1 1.1 collective-permute-start.26
  124.2 1.2 collective-permute-start.22
  125.4 2.9 %collective-permute-done.26 = f32[4,9,8,128]{3,2,1,0:T(8,128)S(1)} collective-permute-done((f32[4,9,8,128]{3,2,1,0:T(8,128)S(1)}, f32[4,9,8,128]{3,2,1,0:T(8,128)S(1)}, u32[]{:S(2)}, u32[]{:S(2)}) %collective-permute-start.26) | collective-permute-done | bytes 147488 | tf_op jit(solution)/shard_map/ppermute | solution.py:571
  128.3 2.3 %collective-permute-done.22.other = f32[16,8,128]{2,1,0:T(8,128)S(1)} collective-permute-done((f32[16,8,128]{2,1,0:T(8,128)S(1)}, f32[16,8,128]{2,1,0:T(8,128)S(1)}, u32[]{:S(2)}, u32[]{:S(2)}) %collective-permute-start.22) | collective-permute-done | bytes 65568 | tf_op jit(solution)/shard_map/ppermute | solution.py:578
  130.6 0.5 collective-permute-start.21
  131.1 1.2 collective-permute-done.21.partner
  132.3 18.0 %fourth.1 = (f32[128,8,128]{2,1,0:T(8,128)S(1)}, f32[128,8,128]{2,1,0:T(8,128)S(1)}, f32[128,8,128]{2,1,0:T(8,128)S(1)}, f32[1,8,128]{2,1,0:T(8,128)S(1)}) custom-call(s32[1]{0:T(128)} %bitcast.me_ref, s32[640]{0:T(1024)S(1)} %copy-done.5, s32[8]{0:T(128)S(1)} %broadcast_subtract_fusion.spots, f32[8,128]{1,0:T(8,128)S(1)} %copy-done.4, ...), custom_call_target="tpu_custom_call" | custom-call | tf_op jit(solution)/shard_map/fourth/pallas_call | solution.py:604
  150.3 0.7 collective-permute-start.30
  151.0 1.1 collective-permute-start.29
  152.2 2.6 %collective-permute-start.28 = (f32[1,8,128]{2,1,0:T(8,128)S(1)}, f32[1,8,128]{2,1,0:T(8,128)S(1)}, u32[]{:S(2)}, u32[]{:S(2)}) collective-permute-start(f32[1,8,128]{2,1,0:T(8,128)S(1)} %get-tuple-element.78), channel_id=1, source_target_pairs={{0,4},{1,5},{2,6},{3,7},{4,0},{5,1},{6,2},{7,3},{8,12},{9,13},{10,... | collective-permute-start | bytes 12296 | tf_op jit(solution)/shard_map/ppermute | solution.py:571
  154.7 1.0 collective-permute-done.30
  155.8 0.6 collective-permute-done.28
  156.3 1.5 collective-permute-start.31
  157.8 2.3 %collective-permute-done.31 = f32[4,1,8,128]{3,2,1,0:T(8,128)S(1)} collective-permute-done((f32[4,1,8,128]{3,2,1,0:T(8,128)S(1)}, f32[4,1,8,128]{3,2,1,0:T(8,128)S(1)}, u32[]{:S(2)}, u32[]{:S(2)}) %collective-permute-start.31) | collective-permute-done | bytes 16416 | tf_op jit(solution)/shard_map/ppermute | solution.py:571
  160.1 1.2 collective-permute-done.32.far_side
  161.3 1.9 %last.1 = (f32[128,8,128]{2,1,0:T(8,128)}, f32[128,8,128]{2,1,0:T(8,128)}) custom-call(f32[8,1,8,128]{3,2,1,0:T(8,128)S(1)} %pad_maximum_fusion.8.near_side, f32[8,1,8,128]{3,2,1,0:T(8,128)S(1)} %collective-permute-done.32.far_side, f32[128,8,128]{2,1,0:T(8,128)S(1)} %get-tuple-element.79.half_own, f32[128,8,128]{2,1,0:T(8,128)S(1)} %get-tuple-element.80.turned, ...), custom_call_target="tpu_custom_call" | custom-call | tf_op jit(solution)/shard_map/last/pallas_call | solution.py:659
  (38 shorter events, 0.2 us)
Async XLA Ops:
  1.3 1.0 copy-start
  3.2 16.7 %collective-permute-start.2 = (f32[9,8,128]{2,1,0:T(8,128)S(1)}, f32[9,8,128]{2,1,0:T(8,128)S(1)}, u32[]{:S(2)}, u32[]{:S(2)}) collective-permute-start(f32[9,8,128]{2,1,0:T(8,128)S(1)} %get-tuple-element.42), channel_id=1, source_target_pairs={{0,12},{1,13},{2,14},{3,15},{4,8},{5,9},{6,10},{7,11},{8,4},{9,5},... | collective-permute-start | bytes 110600 | tf_op jit(solution)/shard_map/ppermute | solution.py:571
  8.3 11.6 %collective-permute-start.1 = (f32[9,8,128]{2,1,0:T(8,128)S(1)}, f32[9,8,128]{2,1,0:T(8,128)S(1)}, u32[]{:S(2)}, u32[]{:S(2)}) collective-permute-start(f32[9,8,128]{2,1,0:T(8,128)S(1)} %get-tuple-element.42), channel_id=1, source_target_pairs={{0,8},{1,9},{2,10},{3,11},{4,12},{5,13},{6,14},{7,15},{8,0},{9,1},... | collective-permute-start | bytes 110600 | tf_op jit(solution)/shard_map/ppermute | solution.py:571
  8.3 11.6 %collective-permute-start = (f32[9,8,128]{2,1,0:T(8,128)S(1)}, f32[9,8,128]{2,1,0:T(8,128)S(1)}, u32[]{:S(2)}, u32[]{:S(2)}) collective-permute-start(f32[9,8,128]{2,1,0:T(8,128)S(1)} %get-tuple-element.42), channel_id=1, source_target_pairs={{0,4},{1,5},{2,6},{3,7},{4,0},{5,1},{6,2},{7,3},{8,12},{9,13},{10,... | collective-permute-start | bytes 110600 | tf_op jit(solution)/shard_map/ppermute | solution.py:571
  20.0 11.7 %collective-permute-start.4 = (f32[4,9,8,128]{3,2,1,0:T(8,128)S(1)}, f32[4,9,8,128]{3,2,1,0:T(8,128)S(1)}, u32[]{:S(2)}, u32[]{:S(2)}) collective-permute-start(f32[4,9,8,128]{3,2,1,0:T(8,128)S(1)} %pad_maximum_fusion.4), channel_id=1, source_target_pairs={{0,2},{1,3},{2,0},{3,1},{4,6},{5,7},{6,4},{7,5},{8,10},{9,11},{10,... | collective-permute-start | bytes 442376 | tf_op jit(solution)/shard_map/ppermute | solution.py:571
  21.7 11.7 %copy-start.1 = (f32[128,8,128]{2,1,0:T(8,128)S(1)}, f32[128,8,128]{2,1,0:T(8,128)}, u32[]{:S(2)}) copy-start(f32[128,8,128]{2,1,0:T(8,128)} %own.9) | copy-start | bytes 1572868
  21.7 11.7 %copy-start.2 = (f32[64,8,128]{2,1,0:T(8,128)S(1)}, f32[64,8,128]{2,1,0:T(8,128)}, u32[]{:S(2)}) copy-start(f32[64,8,128]{2,1,0:T(8,128)} %own.5.image_front) | copy-start | bytes 786436
  21.7 11.7 %copy-start.4 = (f32[8,128]{1,0:T(8,128)S(1)}, f32[8,128]{1,0:T(8,128)}, u32[]{:S(2)}) copy-start(f32[8,128]{1,0:T(8,128)} %broadcast_select_fusion.poles_ref) | copy-start | bytes 12292
  21.7 11.8 %copy-start.5 = (s32[640]{0:T(1024)S(1)}, s32[640]{0:T(1024)}, u32[]{:S(2)}) copy-start(s32[640]{0:T(1024)} %reshape.24.near) | copy-start | bytes 7684
  21.7 10.0 %collective-permute-start.3 = (f32[16,8,128]{2,1,0:T(8,128)S(1)}, f32[16,8,128]{2,1,0:T(8,128)S(1)}, u32[]{:S(2)}, u32[]{:S(2)}) collective-permute-start(f32[16,8,128]{2,1,0:T(8,128)S(1)} %get-tuple-element.44), channel_id=1, source_target_pairs={{0,15},{1,2},{2,1},{3,4},{4,3},{5,6},{6,5},{7,8},{8,7},{9,10},{10,... | collective-permute-start | bytes 196616 | tf_op jit(solution)/shard_map/ppermute | solution.py:578
  31.7 1.7 %collective-permute-start.6 = (f32[8,9,8,128]{3,2,1,0:T(8,128)S(1)}, f32[8,9,8,128]{3,2,1,0:T(8,128)S(1)}, u32[]{:S(2)}, u32[]{:S(2)}) collective-permute-start(f32[8,9,8,128]{3,2,1,0:T(8,128)S(1)} %pad_maximum_fusion.near_side), channel_id=1, source_target_pairs={{0,1},{1,0},{2,3},{3,2},{4,5},{5,4},{6,7},{7,6},{8,9},{9,8},{10,11... | collective-permute-start | bytes 884744 | tf_op jit(solution)/shard_map/ppermute | solution.py:571
  31.8 1.7 %collective-permute-start.5 = (f32[16,8,128]{2,1,0:T(8,128)S(1)}, f32[16,8,128]{2,1,0:T(8,128)S(1)}, u32[]{:S(2)}, u32[]{:S(2)}) collective-permute-start(f32[16,8,128]{2,1,0:T(8,128)S(1)} %get-tuple-element.47), channel_id=1, source_target_pairs={{0,1},{1,0},{2,3},{3,2},{4,5},{5,4},{6,7},{7,6},{8,9},{9,8},{10,11... | collective-permute-start | bytes 196616 | tf_op jit(solution)/shard_map/ppermute | solution.py:571
  33.5 1.0 copy-start.3
  46.4 5.8 %collective-permute-start.11 = (f32[9,8,128]{2,1,0:T(8,128)S(1)}, f32[9,8,128]{2,1,0:T(8,128)S(1)}, u32[]{:S(2)}, u32[]{:S(2)}) collective-permute-start(f32[9,8,128]{2,1,0:T(8,128)S(1)} %get-tuple-element.54), channel_id=1, source_target_pairs={{0,12},{1,13},{2,14},{3,15},{4,8},{5,9},{6,10},{7,11},{8,4},{9,5},... | collective-permute-start | bytes 110600 | tf_op jit(solution)/shard_map/ppermute | solution.py:571
  48.5 5.0 %collective-permute-start.10 = (f32[9,8,128]{2,1,0:T(8,128)S(1)}, f32[9,8,128]{2,1,0:T(8,128)S(1)}, u32[]{:S(2)}, u32[]{:S(2)}) collective-permute-start(f32[9,8,128]{2,1,0:T(8,128)S(1)} %get-tuple-element.54), channel_id=1, source_target_pairs={{0,8},{1,9},{2,10},{3,11},{4,12},{5,13},{6,14},{7,15},{8,0},{9,1},... | collective-permute-start | bytes 110600 | tf_op jit(solution)/shard_map/ppermute | solution.py:571
  48.5 5.1 %collective-permute-start.9 = (f32[9,8,128]{2,1,0:T(8,128)S(1)}, f32[9,8,128]{2,1,0:T(8,128)S(1)}, u32[]{:S(2)}, u32[]{:S(2)}) collective-permute-start(f32[9,8,128]{2,1,0:T(8,128)S(1)} %get-tuple-element.54), channel_id=1, source_target_pairs={{0,4},{1,5},{2,6},{3,7},{4,0},{5,1},{6,2},{7,3},{8,12},{9,13},{10,... | collective-permute-start | bytes 110600 | tf_op jit(solution)/shard_map/ppermute | solution.py:571
  53.6 5.5 %collective-permute-start.12 = (f32[4,9,8,128]{3,2,1,0:T(8,128)S(1)}, f32[4,9,8,128]{3,2,1,0:T(8,128)S(1)}, u32[]{:S(2)}, u32[]{:S(2)}) collective-permute-start(f32[4,9,8,128]{3,2,1,0:T(8,128)S(1)} %pad_maximum_fusion.5), channel_id=1, source_target_pairs={{0,2},{1,3},{2,0},{3,1},{4,6},{5,7},{6,4},{7,5},{8,10},{9,11},{10,... | collective-permute-start | bytes 442376 | tf_op jit(solution)/shard_map/ppermute | solution.py:571
  54.7 6.4 %collective-permute-start.8 = (f32[16,8,128]{2,1,0:T(8,128)S(1)}, f32[16,8,128]{2,1,0:T(8,128)S(1)}, u32[]{:S(2)}, u32[]{:S(2)}) collective-permute-start(f32[16,8,128]{2,1,0:T(8,128)S(1)} %get-tuple-element.53), channel_id=1, source_target_pairs={{0,15},{1,2},{2,1},{3,4},{4,3},{5,6},{6,5},{7,8},{8,7},{9,10},{10,... | collective-permute-start | bytes 196616 | tf_op jit(solution)/shard_map/ppermute | solution.py:578
  61.1 1.7 %collective-permute-start.13 = (f32[8,9,8,128]{3,2,1,0:T(8,128)S(1)}, f32[8,9,8,128]{3,2,1,0:T(8,128)S(1)}, u32[]{:S(2)}, u32[]{:S(2)}) collective-permute-start(f32[8,9,8,128]{3,2,1,0:T(8,128)S(1)} %pad_maximum_fusion.1.near_side), channel_id=1, source_target_pairs={{0,1},{1,0},{2,3},{3,2},{4,5},{5,4},{6,7},{7,6},{8,9},{9,8},{10,11... | collective-permute-start | bytes 884744 | tf_op jit(solution)/shard_map/ppermute | solution.py:571
  61.1 1.7 %collective-permute-start.7 = (f32[16,8,128]{2,1,0:T(8,128)S(1)}, f32[16,8,128]{2,1,0:T(8,128)S(1)}, u32[]{:S(2)}, u32[]{:S(2)}) collective-permute-start(f32[16,8,128]{2,1,0:T(8,128)S(1)} %get-tuple-element.52), channel_id=1, source_target_pairs={{0,1},{1,0},{2,3},{3,2},{4,5},{5,4},{6,7},{7,6},{8,9},{9,8},{10,11... | collective-permute-start | bytes 196616 | tf_op jit(solution)/shard_map/ppermute | solution.py:571
  81.1 5.9 %collective-permute-start.18 = (f32[9,8,128]{2,1,0:T(8,128)S(1)}, f32[9,8,128]{2,1,0:T(8,128)S(1)}, u32[]{:S(2)}, u32[]{:S(2)}) collective-permute-start(f32[9,8,128]{2,1,0:T(8,128)S(1)} %get-tuple-element.63), channel_id=1, source_target_pairs={{0,12},{1,13},{2,14},{3,15},{4,8},{5,9},{6,10},{7,11},{8,4},{9,5},... | collective-permute-start | bytes 110600 | tf_op jit(solution)/shard_map/ppermute | solution.py:571
  82.4 5.7 %collective-permute-start.17 = (f32[9,8,128]{2,1,0:T(8,128)S(1)}, f32[9,8,128]{2,1,0:T(8,128)S(1)}, u32[]{:S(2)}, u32[]{:S(2)}) collective-permute-start(f32[9,8,128]{2,1,0:T(8,128)S(1)} %get-tuple-element.63), channel_id=1, source_target_pairs={{0,8},{1,9},{2,10},{3,11},{4,12},{5,13},{6,14},{7,15},{8,0},{9,1},... | collective-permute-start | bytes 110600 | tf_op jit(solution)/shard_map/ppermute | solution.py:571
  82.5 5.7 %collective-permute-start.16 = (f32[9,8,128]{2,1,0:T(8,128)S(1)}, f32[9,8,128]{2,1,0:T(8,128)S(1)}, u32[]{:S(2)}, u32[]{:S(2)}) collective-permute-start(f32[9,8,128]{2,1,0:T(8,128)S(1)} %get-tuple-element.63), channel_id=1, source_target_pairs={{0,4},{1,5},{2,6},{3,7},{4,0},{5,1},{6,2},{7,3},{8,12},{9,13},{10,... | collective-permute-start | bytes 110600 | tf_op jit(solution)/shard_map/ppermute | solution.py:571
  88.2 5.7 %collective-permute-start.19 = (f32[4,9,8,128]{3,2,1,0:T(8,128)S(1)}, f32[4,9,8,128]{3,2,1,0:T(8,128)S(1)}, u32[]{:S(2)}, u32[]{:S(2)}) collective-permute-start(f32[4,9,8,128]{3,2,1,0:T(8,128)S(1)} %pad_maximum_fusion.6), channel_id=1, source_target_pairs={{0,2},{1,3},{2,0},{3,1},{4,6},{5,7},{6,4},{7,5},{8,10},{9,11},{10,... | collective-permute-start | bytes 442376 | tf_op jit(solution)/shard_map/ppermute | solution.py:571
  88.8 6.5 %collective-permute-start.15 = (f32[16,8,128]{2,1,0:T(8,128)S(1)}, f32[16,8,128]{2,1,0:T(8,128)S(1)}, u32[]{:S(2)}, u32[]{:S(2)}) collective-permute-start(f32[16,8,128]{2,1,0:T(8,128)S(1)} %get-tuple-element.62), channel_id=1, source_target_pairs={{0,15},{1,2},{2,1},{3,4},{4,3},{5,6},{6,5},{7,8},{8,7},{9,10},{10,... | collective-permute-start | bytes 196616 | tf_op jit(solution)/shard_map/ppermute | solution.py:578
  95.3 1.7 %collective-permute-start.20 = (f32[8,9,8,128]{3,2,1,0:T(8,128)S(1)}, f32[8,9,8,128]{3,2,1,0:T(8,128)S(1)}, u32[]{:S(2)}, u32[]{:S(2)}) collective-permute-start(f32[8,9,8,128]{3,2,1,0:T(8,128)S(1)} %pad_maximum_fusion.2.near_side), channel_id=1, source_target_pairs={{0,1},{1,0},{2,3},{3,2},{4,5},{5,4},{6,7},{7,6},{8,9},{9,8},{10,11... | collective-permute-start | bytes 884744 | tf_op jit(solution)/shard_map/ppermute | solution.py:571
  95.3 1.7 %collective-permute-start.14 = (f32[16,8,128]{2,1,0:T(8,128)S(1)}, f32[16,8,128]{2,1,0:T(8,128)S(1)}, u32[]{:S(2)}, u32[]{:S(2)}) collective-permute-start(f32[16,8,128]{2,1,0:T(8,128)S(1)} %get-tuple-element.61), channel_id=1, source_target_pairs={{0,1},{1,0},{2,3},{3,2},{4,5},{5,4},{6,7},{7,6},{8,9},{9,8},{10,11... | collective-permute-start | bytes 196616 | tf_op jit(solution)/shard_map/ppermute | solution.py:571
  116.4 6.2 %collective-permute-start.25 = (f32[9,8,128]{2,1,0:T(8,128)S(1)}, f32[9,8,128]{2,1,0:T(8,128)S(1)}, u32[]{:S(2)}, u32[]{:S(2)}) collective-permute-start(f32[9,8,128]{2,1,0:T(8,128)S(1)} %get-tuple-element.75), channel_id=1, source_target_pairs={{0,12},{1,13},{2,14},{3,15},{4,8},{5,9},{6,10},{7,11},{8,4},{9,5},... | collective-permute-start | bytes 110600 | tf_op jit(solution)/shard_map/ppermute | solution.py:571
  117.2 5.9 %collective-permute-start.24 = (f32[9,8,128]{2,1,0:T(8,128)S(1)}, f32[9,8,128]{2,1,0:T(8,128)S(1)}, u32[]{:S(2)}, u32[]{:S(2)}) collective-permute-start(f32[9,8,128]{2,1,0:T(8,128)S(1)} %get-tuple-element.75), channel_id=1, source_target_pairs={{0,8},{1,9},{2,10},{3,11},{4,12},{5,13},{6,14},{7,15},{8,0},{9,1},... | collective-permute-start | bytes 110600 | tf_op jit(solution)/shard_map/ppermute | solution.py:571
  118.3 4.8 %collective-permute-start.23 = (f32[9,8,128]{2,1,0:T(8,128)S(1)}, f32[9,8,128]{2,1,0:T(8,128)S(1)}, u32[]{:S(2)}, u32[]{:S(2)}) collective-permute-start(f32[9,8,128]{2,1,0:T(8,128)S(1)} %get-tuple-element.75), channel_id=1, source_target_pairs={{0,4},{1,5},{2,6},{3,7},{4,0},{5,1},{6,2},{7,3},{8,12},{9,13},{10,... | collective-permute-start | bytes 110600 | tf_op jit(solution)/shard_map/ppermute | solution.py:571
  123.1 5.2 %collective-permute-start.26 = (f32[4,9,8,128]{3,2,1,0:T(8,128)S(1)}, f32[4,9,8,128]{3,2,1,0:T(8,128)S(1)}, u32[]{:S(2)}, u32[]{:S(2)}) collective-permute-start(f32[4,9,8,128]{3,2,1,0:T(8,128)S(1)} %pad_maximum_fusion.7), channel_id=1, source_target_pairs={{0,2},{1,3},{2,0},{3,1},{4,6},{5,7},{6,4},{7,5},{8,10},{9,11},{10,... | collective-permute-start | bytes 442376 | tf_op jit(solution)/shard_map/ppermute | solution.py:571
  124.2 6.4 %collective-permute-start.22 = (f32[16,8,128]{2,1,0:T(8,128)S(1)}, f32[16,8,128]{2,1,0:T(8,128)S(1)}, u32[]{:S(2)}, u32[]{:S(2)}) collective-permute-start(f32[16,8,128]{2,1,0:T(8,128)S(1)} %get-tuple-element.74), channel_id=1, source_target_pairs={{0,15},{1,2},{2,1},{3,4},{4,3},{5,6},{6,5},{7,8},{8,7},{9,10},{10,... | collective-permute-start | bytes 196616 | tf_op jit(solution)/shard_map/ppermute | solution.py:578
  130.6 1.7 %collective-permute-start.27 = (f32[8,9,8,128]{3,2,1,0:T(8,128)S(1)}, f32[8,9,8,128]{3,2,1,0:T(8,128)S(1)}, u32[]{:S(2)}, u32[]{:S(2)}) collective-permute-start(f32[8,9,8,128]{3,2,1,0:T(8,128)S(1)} %pad_maximum_fusion.3.near_side), channel_id=1, source_target_pairs={{0,1},{1,0},{2,3},{3,2},{4,5},{5,4},{6,7},{7,6},{8,9},{9,8},{10,11... | collective-permute-start | bytes 884744 | tf_op jit(solution)/shard_map/ppermute | solution.py:571
  130.6 1.7 %collective-permute-start.21 = (f32[16,8,128]{2,1,0:T(8,128)S(1)}, f32[16,8,128]{2,1,0:T(8,128)S(1)}, u32[]{:S(2)}, u32[]{:S(2)}) collective-permute-start(f32[16,8,128]{2,1,0:T(8,128)S(1)} %get-tuple-element.73), channel_id=1, source_target_pairs={{0,1},{1,0},{2,3},{3,2},{4,5},{5,4},{6,7},{7,6},{8,9},{9,8},{10,11... | collective-permute-start | bytes 196616 | tf_op jit(solution)/shard_map/ppermute | solution.py:571
  150.3 5.5 %collective-permute-start.30 = (f32[1,8,128]{2,1,0:T(8,128)S(1)}, f32[1,8,128]{2,1,0:T(8,128)S(1)}, u32[]{:S(2)}, u32[]{:S(2)}) collective-permute-start(f32[1,8,128]{2,1,0:T(8,128)S(1)} %get-tuple-element.78), channel_id=1, source_target_pairs={{0,12},{1,13},{2,14},{3,15},{4,8},{5,9},{6,10},{7,11},{8,4},{9,5},... | collective-permute-start | bytes 12296 | tf_op jit(solution)/shard_map/ppermute | solution.py:571
  151.0 4.7 %collective-permute-start.29 = (f32[1,8,128]{2,1,0:T(8,128)S(1)}, f32[1,8,128]{2,1,0:T(8,128)S(1)}, u32[]{:S(2)}, u32[]{:S(2)}) collective-permute-start(f32[1,8,128]{2,1,0:T(8,128)S(1)} %get-tuple-element.78), channel_id=1, source_target_pairs={{0,8},{1,9},{2,10},{3,11},{4,12},{5,13},{6,14},{7,15},{8,0},{9,1},... | collective-permute-start | bytes 12296 | tf_op jit(solution)/shard_map/ppermute | solution.py:571
  152.2 4.2 %collective-permute-start.28 = (f32[1,8,128]{2,1,0:T(8,128)S(1)}, f32[1,8,128]{2,1,0:T(8,128)S(1)}, u32[]{:S(2)}, u32[]{:S(2)}) collective-permute-start(f32[1,8,128]{2,1,0:T(8,128)S(1)} %get-tuple-element.78), channel_id=1, source_target_pairs={{0,4},{1,5},{2,6},{3,7},{4,0},{5,1},{6,2},{7,3},{8,12},{9,13},{10,... | collective-permute-start | bytes 12296 | tf_op jit(solution)/shard_map/ppermute | solution.py:571
  156.3 3.7 %collective-permute-start.31 = (f32[4,1,8,128]{3,2,1,0:T(8,128)S(1)}, f32[4,1,8,128]{3,2,1,0:T(8,128)S(1)}, u32[]{:S(2)}, u32[]{:S(2)}) collective-permute-start(f32[4,1,8,128]{3,2,1,0:T(8,128)S(1)} %pad_maximum_fusion.9), channel_id=1, source_target_pairs={{0,2},{1,3},{2,0},{3,1},{4,6},{5,7},{6,4},{7,5},{8,10},{9,11},{10,... | collective-permute-start | bytes 49160 | tf_op jit(solution)/shard_map/ppermute | solution.py:571
  160.1 1.2 collective-permute-start.32
where the time goes:
time: 163 us
  Pallas kernels  86.5 us (53%)
  starting transfers between devices  37.7 us (23%)
  waiting for transfers between devices  32.3 us (20%)
  local copies, waits for them, and re-layouts  2.91 us (2%)
  other arithmetic  2.83 us (2%)
    pallas_call x4, Pallas kernels, call(): pl.pallas_call(kernel, in_specs=[SMEM] * 3 + [VMEM] * (len(inputs) - 3) +...  67.8 us
    ppermute x29, starting transfers between devices, flip(): return lax.ppermute(value, 'gx', [(i, i ^ mask) for i in range(count)])  31.7 us
    ppermute x29, waiting for transfers between devices, flip(): return lax.ppermute(value, 'gx', [(i, i ^ mask) for i in range(count)])  26.7 us
    pallas_call x2, Pallas kernels, own_part(): pl.pallas_call(functools.partial(own_kernel, first), in_specs=[SMEM] + [V...  16 us
    ppermute x4, starting transfers between devices, exchange(): far = (lax.ppermute(edges[1], 'gx', other),)  6.07 us
    ppermute x4, waiting for transfers between devices, exchange(): far = (lax.ppermute(edges[1], 'gx', other),)  5.58 us
  transfers between devices with their start and end apart: 33, of which 22 were waited for; matrix products, arithmetic and copies ran while one was open for 2% of the time, Pallas kernels for 10%

commit v1 on v0

--- a/solution.py
+++ b/solution.py
@@ -119,6 +119,10 @@
     return lax.fori_loop(0, count // step, run, (zero,) * terms)
 
 
+def contact_spots(contact, me, blocks):
+    return [contact[l] - me * blocks for l in range(contact.shape[0])]
+
+
 def halo_starts(me, blocks):
     odd = jnp.bitwise_and(me, 1)
     return (1 - odd) * (NYB + blocks), odd * (NYB + blocks)
@@ -138,9 +142,17 @@
     place_gathered(ext, 2 * NYB + blocks, me, near_side, far_side, cols)
 
 
-def combine(poles_ref, result):
-    poles = poles_ref.shape[0]
-    z = take_columns(poles_ref[...], 2)
+def pole_factor(values):
+    poles = values.shape[0]
+    row = lax.broadcasted_iota(jnp.int32, (poles, LANES), 0)
+    factor = jnp.zeros((poles, LANES), F32)
+    for pole in range(poles):
+        factor = jnp.where(row == pole, values[pole], factor)
+    return factor
+
+
+def combine(z, result):
+    poles = z[0].shape[0]
     left = lax.broadcasted_iota(jnp.int32, (poles, LANES), 1) < BO
     top, low = result[:poles], result[poles:]
     ham_part = jnp.where(left, top, swap_halves(low))
@@ -157,7 +169,7 @@
     return mats[base + NNZ * pair + index // 2, BO * half : BO * (half + 1)]
 
 
-def sparse_group(near, poles_ref, wide, mats, blocks, image, first, count, shift=0):
+def sparse_group(near, z, wide, mats, blocks, image, first, count, shift=0):
     rows = 2 * image.shape[1]
     bases = (0, ovl_base(blocks))
     for pair in range(count // 2):
@@ -173,7 +185,7 @@
         result = dot_nt(jnp.concatenate(vectors, axis=0), jnp.concatenate(matrices, axis=0))
         for q in range(2):
             image[b + q - shift] = combine(
-                poles_ref, result[rows * q : rows * (q + 1), LANES * q : LANES * (q + 1)]
+                z, result[rows * q : rows * (q + 1), LANES * q : LANES * (q + 1)]
             )
 
 
@@ -204,7 +216,7 @@
     start_sigma(sigma, mats, sems[2])
 
 
-def sparse_part(near, poles_ref, wide, ham, ovl, mats, sems, image):
+def sparse_part(near, z, wide, ham, ovl, mats, sems, image):
     parts = sems[0].shape[0]
     blocks = image.shape[0]
     size = blocks // parts
@@ -212,13 +224,13 @@
     def step(part, carry):
         part_copy(ham, mats, 0, sems[0], part).wait()
         part_copy(ovl, mats, ovl_base(blocks), sems[1], part).wait()
-        sparse_group(near, poles_ref, wide, mats, blocks, image, part * size, size)
+        sparse_group(near, z, wide, mats, blocks, image, part * size, size)
         return carry
 
     lax.fori_loop(0, parts, step, 0)
 
 
-def edge_part(near, poles_ref, wide, mats, image):
+def edge_part(near, z, wide, mats, image):
     blocks = image.shape[0]
     for first, slot in ((0, 2), (blocks - NYB, 1)):
 
@@ -232,7 +244,7 @@
                         for base in (0, ovl_base(blocks))
                     ]
                     product = dot_nt(wide[near[b * NNZ + slot]], jnp.concatenate(pieces, axis=0))
-                    image[b] = image[b] + combine(poles_ref, product)
+                    image[b] = image[b] + combine(z, product)
             return carry
 
         lax.fori_loop(0, NYB // 8, step, 0)
@@ -240,7 +252,7 @@
 
 def contact_part(spots, wide, sigma, mats, sem, acc, image):
     blocks, poles = image.shape[0], image.shape[1]
-    cols = spots.shape[0]
+    cols = len(spots)
     first_contact = blocks + 2 * NYB
     base = blocks * NNZ
     group_rows = sigma.shape[0] // sem.shape[0]
@@ -286,13 +298,13 @@
         image[spot] = image[spot] - product
 
 
-def apply_operator(near, spots, poles_ref, wide, ham, ovl, sigma, mats, sems, acc, image):
-    sparse_part(near, poles_ref, wide, ham, ovl, mats, sems, image)
+def apply_operator(near, spots, z, wide, ham, ovl, sigma, mats, sems, acc, image):
+    sparse_part(near, z, wide, ham, ovl, mats, sems, image)
     contact_part(spots, wide, sigma, mats, sems[2], acc, image)
 
 
 def store_chunk(chunk, edge_a, edge_b, me, spots, image, sums):
-    cols = spots.shape[0]
+    cols = len(spots)
     blocks = image.shape[0]
     edge_a[...] = image[pl.ds(edge_start(0, me, blocks), NYB)]
     edge_b[...] = image[pl.ds(edge_start(1, me, blocks), NYB)]
@@ -309,9 +321,10 @@
     return lane_sum(re_acc), lane_sum(im_acc * -half_sign(2))
 
 
-def prepare_kernel(me_ref, spots, rhs, chunk, edge_a, edge_b, sem):
+def prepare_kernel(me_ref, contact, rhs, chunk, edge_a, edge_b, sem):
     blocks, poles = rhs.shape[0], rhs.shape[1]
-    cols = spots.shape[0]
+    spots = contact_spots(contact, me_ref[0], blocks)
+    cols = len(spots)
     copies = [pltpu.make_async_copy(rhs.at[spots[l]], chunk.at[l], sem.at[l]) for l in range(cols)]
     for kind, edge in enumerate((edge_a, edge_b)):
         here = pl.ds(edge_start(kind, me_ref[0], blocks), NYB)
@@ -323,7 +336,8 @@
         copy.wait()
 
 
-def own_kernel(first, near, poles_ref, own, ham, ovl, image, wide, mats, *sems):
+def own_kernel(first, near, pole_re, pole_im, own, ham, ovl, image, wide, mats, *sems):
+    z = (pole_factor(pole_re), pole_factor(pole_im))
     blocks = own.shape[0]
     parts = sems[0].shape[0]
     size = image.shape[0] // parts
@@ -354,7 +368,7 @@
         for copy in copies(part):
             copy.wait()
         sparse_group(
-            near, poles_ref, wide, mats, blocks, image, first + part * size, size, shift=first
+            near, z, wide, mats, blocks, image, first + part * size, size, shift=first
         )
         return carry
 
@@ -362,10 +376,12 @@
 
 
 def first_kernel(
-    me_ref, near, spots, poles_ref, own, image_front, image_back, partner, other, near_side, far_side, ham, ovl, sigma,
+    me_ref, near, contact, pole_re, pole_im, own, image_in, partner, other, near_side, far_side, ham, ovl, sigma,
     rhs_ext, image, chunk, edge_a, edge_b, wide, acc, mats, *sems,
 ):
     blocks, poles = own.shape[0], own.shape[1]
+    z = (pole_factor(pole_re), pole_factor(pole_im))
+    spots = contact_spots(contact, me_ref[0], blocks)
     edge_slabs = NYB * NNZ // 2
     edges = []
     for source, base, sem in ((ham, 0, sems[0]), (ovl, ovl_base(blocks), sems[1])):
@@ -380,37 +396,38 @@
     for copy in edges:
         copy.start()
     start_sigma(sigma, mats, sems[2])
-    fill_extended(rhs_ext, partner, own, other, me_ref[0], near_side, far_side, spots.shape[0])
+    fill_extended(rhs_ext, partner, own, other, me_ref[0], near_side, far_side, len(spots))
     store_wide(wide, 0, NYB, rhs_ext[0:NYB])
     over_rows(
         NYB + CONTACT, TILE,
         lambda s: store_wide(wide, NYB + blocks + s, TILE, rhs_ext[pl.ds(NYB + blocks + s, TILE)]),
     )
-    image[0 : blocks // 2] = image_front[...]
-    image[blocks // 2 : blocks] = image_back[...]
+    image[...] = image_in[...]
     for copy in edges:
         copy.wait()
-    edge_part(near, poles_ref, wide, mats, image)
+    edge_part(near, z, wide, mats, image)
     contact_part(spots, wide, sigma, mats, sems[2], acc, image)
 
     def terms(s):
-        b, v = own[pl.ds(s, TILE)], image[pl.ds(s, TILE)]
+        b, v = own[pl.ds(s, 2 * TILE)], image[pl.ds(s, 2 * TILE)]
         return (b * b, *inner_terms(b, v), v * v)
 
-    bb, bv_re, bv_im, vv = sum_rows(blocks, TILE, terms, 4, poles)
+    bb, bv_re, bv_im, vv = sum_rows(blocks, 2 * TILE, terms, 4, poles)
     store_chunk(
         chunk, edge_a, edge_b, me_ref[0], spots, image, pack_columns([lane_sum(bb), *inner_pair(bv_re, bv_im), lane_sum(vv)])
     )
 
 
 def second_kernel(
-    me_ref, near, spots, poles_ref, rhs_ext, own, partner, other, near_side, far_side, ham, ovl, sigma,
+    me_ref, near, contact, pole_re, pole_im, rhs_ext, own, partner, other, near_side, far_side, ham, ovl, sigma,
     image_ext, half_ext, turned, chunk, edge_a, edge_b, scalars, wide, acc, mats,
     *sems,
 ):
     start_matrices(ham, ovl, sigma, mats, sems)
     blocks, poles = own.shape[0], own.shape[1]
-    cols = spots.shape[0]
+    z = (pole_factor(pole_re), pole_factor(pole_im))
+    spots = contact_spots(contact, me_ref[0], blocks)
+    cols = len(spots)
     fill_extended(image_ext, partner, own, other, me_ref[0], near_side, far_side, cols)
     norm_b, bv_re, bv_im, vv = take_columns(gathered_sums(near_side, far_side, cols), 4)
     alpha = guarded_quotient((norm_b, jnp.zeros_like(norm_b)), (bv_re, bv_im), norm_b * vv)
@@ -419,20 +436,21 @@
     scalars[2] = alpha[1]
 
     def update(s):
-        half = rhs_ext[pl.ds(s, TILE)] - scale(alpha, image_ext[pl.ds(s, TILE)])
-        half_ext[pl.ds(s, TILE)] = half
-        store_wide(wide, s, TILE, half)
-
-    over_rows(half_ext.shape[0], TILE, update)
-    apply_operator(near, spots, poles_ref, wide, ham, ovl, sigma, mats, sems, acc, turned)
+        here = pl.ds(s, 2 * TILE)
+        half = rhs_ext[here] - scale(alpha, image_ext[here])
+        half_ext[here] = half
+        store_wide(wide, s, 2 * TILE, half)
+
+    over_rows(half_ext.shape[0], 2 * TILE, update)
+    apply_operator(near, spots, z, wide, ham, ovl, sigma, mats, sems, acc, turned)
 
     def terms(s):
-        b = rhs_ext[pl.ds(NYB + s, TILE)]
-        h = half_ext[pl.ds(NYB + s, TILE)]
-        t = turned[pl.ds(s, TILE)]
+        b = rhs_ext[pl.ds(NYB + s, 2 * TILE)]
+        h = half_ext[pl.ds(NYB + s, 2 * TILE)]
+        t = turned[pl.ds(s, 2 * TILE)]
         return (*inner_terms(t, h), t * t, h * h, *inner_terms(b, h), *inner_terms(b, t))
 
-    th_re, th_im, tt, hh, bh_re, bh_im, bt_re, bt_im = sum_rows(blocks, TILE, terms, 8, poles)
+    th_re, th_im, tt, hh, bh_re, bh_im, bt_re, bt_im = sum_rows(blocks, 2 * TILE, terms, 8, poles)
     columns = [
         *inner_pair(th_re, th_im), lane_sum(tt), lane_sum(hh),
         *inner_pair(bh_re, bh_im), *inner_pair(bt_re, bt_im),
@@ -441,14 +459,16 @@
 
 
 def third_kernel(
-    me_ref, near, spots, poles_ref, scalars, rhs_ext, image_ext, half_ext, own, partner, other,
+    me_ref, near, contact, pole_re, pole_im, scalars, rhs_ext, image_ext, half_ext, own, partner, other,
     near_side, far_side, ham, ovl, sigma,
     residual_own, direction_own, residual_rem, direction_rem, iterate, image, chunk, edge_a,
     edge_b, rho_out, turned_ext, wide, acc, mats, *sems,
 ):
     start_matrices(ham, ovl, sigma, mats, sems)
     blocks, poles = own.shape[0], own.shape[1]
-    cols = spots.shape[0]
+    z = (pole_factor(pole_re), pole_factor(pole_im))
+    spots = contact_spots(contact, me_ref[0], blocks)
+    cols = len(spots)
     fill_extended(turned_ext, partner, own, other, me_ref[0], near_side, far_side, cols)
     sums = take_columns(gathered_sums(near_side, far_side, cols), 8)
     th, tt, hh, bh, bt = (sums[0], sums[1]), sums[2], sums[3], (sums[4], sums[5]), (sums[6], sums[7])
@@ -489,24 +509,26 @@
     over_rows(blocks, TILE, update_own)
     update_rest(0, 0)
     over_rows(NYB + CONTACT, TILE, lambda s: update_rest(NYB + blocks + s, NYB + s))
-    apply_operator(near, spots, poles_ref, wide, ham, ovl, sigma, mats, sems, acc, image)
+    apply_operator(near, spots, z, wide, ham, ovl, sigma, mats, sems, acc, image)
 
     def terms(s):
-        b, v = rhs_ext[pl.ds(NYB + s, TILE)], image[pl.ds(s, TILE)]
+        b, v = rhs_ext[pl.ds(NYB + s, 2 * TILE)], image[pl.ds(s, 2 * TILE)]
         return (*inner_terms(b, v), v * v)
 
-    bv_re, bv_im, vv = sum_rows(blocks, TILE, terms, 3, poles)
+    bv_re, bv_im, vv = sum_rows(blocks, 2 * TILE, terms, 3, poles)
     store_chunk(chunk, edge_a, edge_b, me_ref[0], spots, image, pack_columns([*inner_pair(bv_re, bv_im), lane_sum(vv)]))
 
 
 def fourth_kernel(
-    me_ref, near, spots, poles_ref, rho_in, residual_own, direction_own, residual_rem,
+    me_ref, near, contact, pole_re, pole_im, rho_in, residual_own, direction_own, residual_rem,
     direction_rem, iterate_in, own, partner, other, near_side, far_side, ham, ovl, sigma,
     half_own, turned, iterate, sums_out, contact_image, wide, acc, mats, *sems,
 ):
     start_matrices(ham, ovl, sigma, mats, sems)
     blocks, poles = own.shape[0], own.shape[1]
-    cols = spots.shape[0]
+    z = (pole_factor(pole_re), pole_factor(pole_im))
+    spots = contact_spots(contact, me_ref[0], blocks)
+    cols = len(spots)
     place_gathered(contact_image, 0, me_ref[0], near_side, far_side, cols)
     bv_re, bv_im, vv = take_columns(gathered_sums(near_side, far_side, cols), 3)
     norm_b = rho_in[2]
@@ -530,13 +552,13 @@
         store_wide(wide, 2 * NYB + blocks + s, TILE, half)
 
     over_rows(CONTACT, TILE, update_contact)
-    apply_operator(near, spots, poles_ref, wide, ham, ovl, sigma, mats, sems, acc, turned)
+    apply_operator(near, spots, z, wide, ham, ovl, sigma, mats, sems, acc, turned)
 
     def terms(s):
-        h, t = half_own[pl.ds(s, TILE)], turned[pl.ds(s, TILE)]
+        h, t = half_own[pl.ds(s, 2 * TILE)], turned[pl.ds(s, 2 * TILE)]
         return (*inner_terms(t, h), t * t)
 
-    th_re, th_im, tt = sum_rows(blocks, TILE, terms, 3, poles)
+    th_re, th_im, tt = sum_rows(blocks, 2 * TILE, terms, 3, poles)
     sums_out[0] = pack_columns([*inner_pair(th_re, th_im), lane_sum(tt)])
 
 
@@ -561,27 +583,28 @@
     me = lax.axis_index("gx")
     first_block = me * blocks
     near = ((neighbours - first_block + NYB) % (blocks * count)).reshape(-1)
-    spots = contact - first_block
     me_ref = jnp.reshape(me, (1,)).astype(jnp.int32)
-    lane = jnp.arange(LANES)[None, :]
-    poles_ref = jnp.where(lane == 0, pole_real[:, None], pole_imag[:, None])
     ext = blocks + 2 * NYB + CONTACT
 
     def flip(value, mask):
         return lax.ppermute(value, "gx", [(i, i ^ mask) for i in range(count)])
 
-    def exchange(chunk, edges=None, beside=()):
+    def exchange(chunk, edges=None, beside=None):
         parts = [chunk] + [flip(chunk, mask) for mask in range(4, count, 4)]
         far = ()
         if edges is not None:
             other = [(i, (i + 1 if i % 2 else i - 1) % count) for i in range(count)]
             far = (lax.ppermute(edges[1], "gx", other),)
-        early, line = lax.optimization_barrier((beside[:1], jnp.stack(parts)))
+        line = jnp.stack(parts)
+        extra = ()
+        if beside is not None:
+            after, line = lax.optimization_barrier((near, line))
+            extra = (beside(after),)
         plane = jnp.concatenate([line, flip(line, 2)])
         if edges is None:
             return plane, flip(plane, 1)
-        far, late, plane = lax.optimization_barrier((far, beside[1:], plane))
-        return (*early, *late, flip(edges[0], 1), *far, plane, flip(plane, 1))
+        far, extra, plane = lax.optimization_barrier((far, extra, plane))
+        return (*extra, flip(edges[0], 1), *far, plane, flip(plane, 1))
 
     def vec_shape(rows):
         return jax.ShapeDtypeStruct((rows, poles, LANES), F32)
@@ -593,9 +616,9 @@
     acc = pltpu.VMEM((sigma.shape[0], TILE * 2 * poles), F32)
     held = pltpu.VMEM((sum(m.shape[0] for m in slabs), LANES, LANES), BF16)
     parts = max(2, blocks // 32)
-    sems = [pltpu.SemaphoreType.DMA((p,)) for p in (parts, parts, sigma.shape[0] // BO)]
+    sems = [pltpu.SemaphoreType.DMA((p,)) for p in (parts, parts, max(1, sigma.shape[0] // 128))]
     hbm = pl.BlockSpec(memory_space=pl.ANY)
-    fixed = (me_ref, near, spots, poles_ref)
+    fixed = (me_ref, near, contact, pole_real, pole_imag)
     remote = 2 * NYB + CONTACT
     rows = cols + 1
 
@@ -603,7 +626,7 @@
         scratch = [pltpu.VMEM((r, poles, LANES), F32) for r in scratch]
         return pl.pallas_call(
             kernel,
-            in_specs=[SMEM] * 3 + [VMEM] * (len(inputs) - 3) + [hbm] * 3,
+            in_specs=[SMEM] * 5 + [VMEM] * (len(inputs) - 5) + [hbm] * 3,
             out_specs=[VMEM] * len(out_rows),
             out_shape=[vec_shape(r) for r in out_rows],
             scratch_shapes=[*scratch, wide, acc, held, *sems],
@@ -619,25 +642,23 @@
         scratch_shapes=[pltpu.SemaphoreType.DMA((cols + 2,))],
         compiler_params=small,
         name="prepare",
-    )(me_ref, spots, rhs)
-    half = blocks // 2
-
-    def own_part(first):
+    )(me_ref, contact, rhs)
+    def own_part(near):
         return pl.pallas_call(
-            functools.partial(own_kernel, first),
-            in_specs=[SMEM] + [VMEM] * 2 + [hbm] * 2,
+            functools.partial(own_kernel, 0),
+            in_specs=[SMEM] * 3 + [VMEM] + [hbm] * 2,
             out_specs=VMEM,
-            out_shape=vec_shape(half),
-            scratch_shapes=[wide, held, *([pltpu.SemaphoreType.DMA((max(1, half // 32),))] * 2)],
-            compiler_params=pltpu.CompilerParams(vmem_limit_bytes=54 << 20),
+            out_shape=vec_shape(blocks),
+            scratch_shapes=[wide, held, *([pltpu.SemaphoreType.DMA((parts,))] * 2)],
+            compiler_params=pltpu.CompilerParams(vmem_limit_bytes=50 << 20),
             cost_estimate=pl.CostEstimate(
-                flops=2 * ham.size * 2 * poles, bytes_accessed=2 * ham.size, transcendentals=0
+                flops=4 * ham.size * 2 * poles, bytes_accessed=4 * ham.size, transcendentals=0
             ),
             name="own",
-        )(near, poles_ref, rhs, *slabs[:2])
+        )(near, pole_real, pole_imag, rhs, *slabs[:2])
 
     rhs_ext, image, chunk, edge_a, edge_b = call(
-        first_kernel, (*fixed, rhs, *exchange(chunk, edges, (own_part(0), own_part(half)))),
+        first_kernel, (*fixed, rhs, *exchange(chunk, edges, own_part)),
         [ext, blocks, rows, NYB, NYB], [], "first",
     )
     image_ext, half_ext, turned, chunk, edge_a, edge_b, scalars = call(

time: 163 us -> 151 us (0.926)
  Pallas kernels: 86.5 us -> 76 us
  waiting for transfers between devices: 32.3 us -> 25 us
  starting transfers between devices: 37.7 us -> 43.6 us
  other arithmetic: 2.83 us -> 0.78 us
    pallas_call x6 -> x5, Pallas kernels: 83.8 us -> 73.3 us  [the longest x4 62.7 us: call(): pl.pallas_call(kernel, in_specs=[SMEM] * 5 + [VMEM] * (len(inputs) - 5) +...]
    ppermute x4, waiting for transfers between devices: 5.58 us -> 0.01 us  [exchange(): far = (lax.ppermute(edges[1], 'gx', other),)]
    ppermute x29, starting transfers between devices: 31.7 us -> 35.4 us  [flip(): return lax.ppermute(value, 'gx', [(i, i ^ mask) for i in range(count)])]
    unnamed x12 -> x32, local copies, waits for them, and re-layouts: 2 us -> 4.11 us
    ppermute x4, starting transfers between devices: 6.07 us -> 8.17 us  [exchange(): far = (lax.ppermute(edges[1], 'gx', other),)]
    ppermute x29, waiting for transfers between devices: 26.7 us -> 25 us  [flip(): return lax.ppermute(value, 'gx', [(i, i ^ mask) for i in range(count)])]
  transfers between devices with their start and end apart: 33 -> 33, of which waited for: 22 -> 15; matrix products, arithmetic and copies ran while one was open for 2% -> 1% of each run, Pallas kernels for 10% -> 7%
where the time goes in v1:
time: 151 us
  Pallas kernels  76 us (50%)
  starting transfers between devices  43.6 us (29%)
  waiting for transfers between devices  25 us (17%)
  local copies, waits for them, and re-layouts  4.46 us (3%)
    pallas_call x4, Pallas kernels, call(): pl.pallas_call(kernel, in_specs=[SMEM] * 5 + [VMEM] * (len(inputs) - 5) +...  62.7 us
    ppermute x29, starting transfers between devices, flip(): return lax.ppermute(value, 'gx', [(i, i ^ mask) for i in range(count)])  35.4 us
    ppermute x29, waiting for transfers between devices, flip(): return lax.ppermute(value, 'gx', [(i, i ^ mask) for i in range(count)])  25 us
    pallas_call x1, Pallas kernels, own_part(): pl.pallas_call(functools.partial(own_kernel, 0), in_specs=[SMEM] * 3 + [V...  10.5 us
    ppermute x4, starting transfers between devices, exchange(): far = (lax.ppermute(edges[1], 'gx', other),)  8.17 us
    unnamed x32, local copies, waits for them, and re-layouts  4.11 us
  transfers between devices with their start and end apart: 33, of which 15 were waited for; matrix products, arithmetic and copies ran while one was open for 1% of the time, Pallas kernels for 7%

profile of v1, /device:TPU:0, one launch (start us, length us, event | category | flops | bytes accessed | tf_op | source)
XLA Modules:
  0.0 150.7 jit_solution(16746929776968971575)
XLA Ops:
  0.6 0.0 copy-start
  0.6 1.0 copy-done
  1.7 0.7 copy-done.6
  2.3 0.9 prepare.1
  3.2 5.1 %collective-permute-start.3 = (f32[9,8,128]{2,1,0:T(8,128)S(1)}, f32[9,8,128]{2,1,0:T(8,128)S(1)}, u32[]{:S(2)}, u32[]{:S(2)}) collective-permute-start(f32[9,8,128]{2,1,0:T(8,128)S(1)} %get-tuple-element.43), channel_id=1, source_target_pairs={{0,12},{1,13},{2,14},{3,15},{4,8},{5,9},{6,10},{7,11},{8,4},{9,5},... | collective-permute-start | bytes 110600 | tf_op jit(solution)/shard_map/ppermute | solution.py:590
  8.3 0.0 collective-permute-start.2
  8.3 0.6 collective-permute-start.1
  9.0 0.7 add_select_fusion
  9.7 0.1 copy.10
  9.8 0.2 reshape.17.near
  10.0 0.3 collective-permute-done.3
  10.3 2.9 %collective-permute-done.2 = f32[9,8,128]{2,1,0:T(8,128)S(1)} collective-permute-done((f32[9,8,128]{2,1,0:T(8,128)S(1)}, f32[9,8,128]{2,1,0:T(8,128)S(1)}, u32[]{:S(2)}, u32[]{:S(2)}) %collective-permute-start.2) | collective-permute-done | bytes 36896 | tf_op jit(solution)/shard_map/ppermute | solution.py:590
  13.2 1.6 %collective-permute-start.4 = (f32[4,9,8,128]{3,2,1,0:T(8,128)S(1)}, f32[4,9,8,128]{3,2,1,0:T(8,128)S(1)}, u32[]{:S(2)}, u32[]{:S(2)}) collective-permute-start(f32[4,9,8,128]{3,2,1,0:T(8,128)S(1)} %pad_maximum_fusion.1), channel_id=1, source_target_pairs={{0,2},{1,3},{2,0},{3,1},{4,6},{5,7},{6,4},{7,5},{8,10},{9,11},{10,... | collective-permute-start | bytes 442376 | tf_op jit(solution)/shard_map/ppermute | solution.py:590
  14.8 0.0 collective-permute-start
  14.8 1.0 copy-done.1
  15.9 0.7 copy-done.2
  16.5 0.7 copy-done.4
  17.2 10.5 %own.3.image_in = f32[128,8,128]{2,1,0:T(8,128)S(1)} custom-call(s32[640]{0:T(1024)S(1)} %reshape.17.near, f32[8]{0:T(128)S(1)} %copy-done.2, f32[8]{0:T(128)S(1)} %copy-done.4, f32[128,8,128]{2,1,0:T(8,128)S(1)} %copy-done.1, bf16[320,128,128]{2,1,0:T(8,128)(2,1)} %bitcast.44, bf16[320,128,128]{2,1,0:T(8,128)(2,1)} %bitcast.49), custom_call_target="tpu_custom_call" | custom-call | flops 335544320 | bytes 20971520 | tf_op jit(solution)/shard_map/own/pallas_call | solution.py:647
  27.7 0.7 collective-permute-start.6
  28.4 0.1 collective-permute-start.5
  28.5 1.2 collective-permute-done.5.partner
  29.7 0.0 collective-permute-done.6.far_side
  29.7 10.9 %first.1 = (f32[288,8,128]{2,1,0:T(8,128)S(1)}, f32[128,8,128]{2,1,0:T(8,128)S(1)}, f32[9,8,128]{2,1,0:T(8,128)S(1)}, f32[16,8,128]{2,1,0:T(8,128)S(1)}, f32[16,8,128]{2,1,0:T(8,128)S(1)}) custom-call(s32[1]{0:T(128)} %bitcast.me_ref, s32[640]{0:T(1024)S(1)} %reshape.17.near, s32[8]{0:T(128)S(1)} %copy-done.7, f32[8]{0:T(128)S(1)} %copy-done.2, ...), custom_call_target="tpu_custom_call" | custom-call | tf_op jit(solution)/shard_map/first/pallas_call | solution.py:627
  40.6 1.6 %collective-permute-start.11 = (f32[9,8,128]{2,1,0:T(8,128)S(1)}, f32[9,8,128]{2,1,0:T(8,128)S(1)}, u32[]{:S(2)}, u32[]{:S(2)}) collective-permute-start(f32[9,8,128]{2,1,0:T(8,128)S(1)} %get-tuple-element.54), channel_id=1, source_target_pairs={{0,12},{1,13},{2,14},{3,15},{4,8},{5,9},{6,10},{7,11},{8,4},{9,5},... | collective-permute-start | bytes 110600 | tf_op jit(solution)/shard_map/ppermute | solution.py:590
  42.2 0.6 collective-permute-start.10
  42.8 2.3 %collective-permute-start.9 = (f32[9,8,128]{2,1,0:T(8,128)S(1)}, f32[9,8,128]{2,1,0:T(8,128)S(1)}, u32[]{:S(2)}, u32[]{:S(2)}) collective-permute-start(f32[9,8,128]{2,1,0:T(8,128)S(1)} %get-tuple-element.54), channel_id=1, source_target_pairs={{0,4},{1,5},{2,6},{3,7},{4,0},{5,1},{6,2},{7,3},{8,12},{9,13},{10,... | collective-permute-start | bytes 110600 | tf_op jit(solution)/shard_map/ppermute | solution.py:590
  45.1 3.3 %collective-permute-start.8 = (f32[16,8,128]{2,1,0:T(8,128)S(1)}, f32[16,8,128]{2,1,0:T(8,128)S(1)}, u32[]{:S(2)}, u32[]{:S(2)}) collective-permute-start(f32[16,8,128]{2,1,0:T(8,128)S(1)} %get-tuple-element.53), channel_id=1, source_target_pairs={{0,15},{1,2},{2,1},{3,4},{4,3},{5,6},{6,5},{7,8},{8,7},{9,10},{10,... | collective-permute-start | bytes 196616 | tf_op jit(solution)/shard_map/ppermute | solution.py:597
  48.5 2.0 %collective-permute-start.12 = (f32[4,9,8,128]{3,2,1,0:T(8,128)S(1)}, f32[4,9,8,128]{3,2,1,0:T(8,128)S(1)}, u32[]{:S(2)}, u32[]{:S(2)}) collective-permute-start(f32[4,9,8,128]{3,2,1,0:T(8,128)S(1)} %pad_maximum_fusion.2), channel_id=1, source_target_pairs={{0,2},{1,3},{2,0},{3,1},{4,6},{5,7},{6,4},{7,5},{8,10},{9,11},{10,... | collective-permute-start | bytes 442376 | tf_op jit(solution)/shard_map/ppermute | solution.py:590
  50.4 3.7 %collective-permute-done.12 = f32[4,9,8,128]{3,2,1,0:T(8,128)S(1)} collective-permute-done((f32[4,9,8,128]{3,2,1,0:T(8,128)S(1)}, f32[4,9,8,128]{3,2,1,0:T(8,128)S(1)}, u32[]{:S(2)}, u32[]{:S(2)}) %collective-permute-start.12) | collective-permute-done | bytes 147488 | tf_op jit(solution)/shard_map/ppermute | solution.py:590
  54.2 0.1 collective-permute-start.13
  54.3 0.5 collective-permute-start.7
  54.8 1.2 collective-permute-done.7.partner
  56.0 16.7 %second.1 = (f32[288,8,128]{2,1,0:T(8,128)S(1)}, f32[288,8,128]{2,1,0:T(8,128)S(1)}, f32[128,8,128]{2,1,0:T(8,128)S(1)}, f32[9,8,128]{2,1,0:T(8,128)S(1)}, f32[1...) custom-call(s32[1]{0:T(128)} %bitcast.me_ref, s32[640]{0:T(1024)S(1)} %reshape.17.near, ...), custom_call_target="tpu_custom_call" | custom-call | tf_op jit(solution)/shard_map/second/pallas_call | solution.py:627
  72.7 1.7 %collective-permute-start.18 = (f32[9,8,128]{2,1,0:T(8,128)S(1)}, f32[9,8,128]{2,1,0:T(8,128)S(1)}, u32[]{:S(2)}, u32[]{:S(2)}) collective-permute-start(f32[9,8,128]{2,1,0:T(8,128)S(1)} %get-tuple-element.63), channel_id=1, source_target_pairs={{0,12},{1,13},{2,14},{3,15},{4,8},{5,9},{6,10},{7,11},{8,4},{9,5},... | collective-permute-start | bytes 110600 | tf_op jit(solution)/shard_map/ppermute | solution.py:590
  74.4 0.2 collective-permute-start.17
  74.6 2.5 %collective-permute-start.16 = (f32[9,8,128]{2,1,0:T(8,128)S(1)}, f32[9,8,128]{2,1,0:T(8,128)S(1)}, u32[]{:S(2)}, u32[]{:S(2)}) collective-permute-start(f32[9,8,128]{2,1,0:T(8,128)S(1)} %get-tuple-element.63), channel_id=1, source_target_pairs={{0,4},{1,5},{2,6},{3,7},{4,0},{5,1},{6,2},{7,3},{8,12},{9,13},{10,... | collective-permute-start | bytes 110600 | tf_op jit(solution)/shard_map/ppermute | solution.py:590
  77.2 2.1 %collective-permute-start.15 = (f32[16,8,128]{2,1,0:T(8,128)S(1)}, f32[16,8,128]{2,1,0:T(8,128)S(1)}, u32[]{:S(2)}, u32[]{:S(2)}) collective-permute-start(f32[16,8,128]{2,1,0:T(8,128)S(1)} %get-tuple-element.62), channel_id=1, source_target_pairs={{0,15},{1,2},{2,1},{3,4},{4,3},{5,6},{6,5},{7,8},{8,7},{9,10},{10,... | collective-permute-start | bytes 196616 | tf_op jit(solution)/shard_map/ppermute | solution.py:597
  79.3 0.3 collective-permute-done.17
  79.6 0.1 collective-permute-done.16
  79.7 2.1 %collective-permute-start.19 = (f32[4,9,8,128]{3,2,1,0:T(8,128)S(1)}, f32[4,9,8,128]{3,2,1,0:T(8,128)S(1)}, u32[]{:S(2)}, u32[]{:S(2)}) collective-permute-start(f32[4,9,8,128]{3,2,1,0:T(8,128)S(1)} %pad_maximum_fusion.3), channel_id=1, source_target_pairs={{0,2},{1,3},{2,0},{3,1},{4,6},{5,7},{6,4},{7,5},{8,10},{9,11},{10,... | collective-permute-start | bytes 442376 | tf_op jit(solution)/shard_map/ppermute | solution.py:590
  81.9 3.7 %collective-permute-done.19 = f32[4,9,8,128]{3,2,1,0:T(8,128)S(1)} collective-permute-done((f32[4,9,8,128]{3,2,1,0:T(8,128)S(1)}, f32[4,9,8,128]{3,2,1,0:T(8,128)S(1)}, u32[]{:S(2)}, u32[]{:S(2)}) %collective-permute-start.19) | collective-permute-done | bytes 147488 | tf_op jit(solution)/shard_map/ppermute | solution.py:590
  85.7 0.1 collective-permute-start.20
  85.7 0.5 collective-permute-start.14
  86.2 1.2 collective-permute-done.14.partner
  87.4 18.3 %third.1 = (f32[128,8,128]{2,1,0:T(8,128)S(1)}, f32[128,8,128]{2,1,0:T(8,128)S(1)}, f32[160,8,128]{2,1,0:T(8,128)S(1)}, f32[160,8,128]{2,1,0:T(8,128)S(1)}, f32[...) custom-call(s32[1]{0:T(128)} %bitcast.me_ref, ...), custom_call_target="tpu_custom_call" | custom-call | tf_op jit(solution)/shard_map/third/pallas_call | solution.py:627
  105.8 2.2 %collective-permute-start.25 = (f32[9,8,128]{2,1,0:T(8,128)S(1)}, f32[9,8,128]{2,1,0:T(8,128)S(1)}, u32[]{:S(2)}, u32[]{:S(2)}) collective-permute-start(f32[9,8,128]{2,1,0:T(8,128)S(1)} %get-tuple-element.75), channel_id=1, source_target_pairs={{0,12},{1,13},{2,14},{3,15},{4,8},{5,9},{6,10},{7,11},{8,4},{9,5},... | collective-permute-start | bytes 110600 | tf_op jit(solution)/shard_map/ppermute | solution.py:590
  108.0 0.0 collective-permute-start.24
  108.0 2.2 %collective-permute-start.23 = (f32[9,8,128]{2,1,0:T(8,128)S(1)}, f32[9,8,128]{2,1,0:T(8,128)S(1)}, u32[]{:S(2)}, u32[]{:S(2)}) collective-permute-start(f32[9,8,128]{2,1,0:T(8,128)S(1)} %get-tuple-element.75), channel_id=1, source_target_pairs={{0,4},{1,5},{2,6},{3,7},{4,0},{5,1},{6,2},{7,3},{8,12},{9,13},{10,... | collective-permute-start | bytes 110600 | tf_op jit(solution)/shard_map/ppermute | solution.py:590
  110.2 2.7 %collective-permute-start.22 = (f32[16,8,128]{2,1,0:T(8,128)S(1)}, f32[16,8,128]{2,1,0:T(8,128)S(1)}, u32[]{:S(2)}, u32[]{:S(2)}) collective-permute-start(f32[16,8,128]{2,1,0:T(8,128)S(1)} %get-tuple-element.74), channel_id=1, source_target_pairs={{0,15},{1,2},{2,1},{3,4},{4,3},{5,6},{6,5},{7,8},{8,7},{9,10},{10,... | collective-permute-start | bytes 196616 | tf_op jit(solution)/shard_map/ppermute | solution.py:597
  112.9 2.2 %collective-permute-start.26 = (f32[4,9,8,128]{3,2,1,0:T(8,128)S(1)}, f32[4,9,8,128]{3,2,1,0:T(8,128)S(1)}, u32[]{:S(2)}, u32[]{:S(2)}) collective-permute-start(f32[4,9,8,128]{3,2,1,0:T(8,128)S(1)} %pad_maximum_fusion.4), channel_id=1, source_target_pairs={{0,2},{1,3},{2,0},{3,1},{4,6},{5,7},{6,4},{7,5},{8,10},{9,11},{10,... | collective-permute-start | bytes 442376 | tf_op jit(solution)/shard_map/ppermute | solution.py:590
  115.1 3.7 %collective-permute-done.26 = f32[4,9,8,128]{3,2,1,0:T(8,128)S(1)} collective-permute-done((f32[4,9,8,128]{3,2,1,0:T(8,128)S(1)}, f32[4,9,8,128]{3,2,1,0:T(8,128)S(1)}, u32[]{:S(2)}, u32[]{:S(2)}) %collective-permute-start.26) | collective-permute-done | bytes 147488 | tf_op jit(solution)/shard_map/ppermute | solution.py:590
  118.9 0.1 collective-permute-start.27
  119.0 0.5 collective-permute-start.21
  119.5 1.2 collective-permute-done.21.partner
  120.6 16.8 %fourth.1 = (f32[128,8,128]{2,1,0:T(8,128)S(1)}, f32[128,8,128]{2,1,0:T(8,128)S(1)}, f32[128,8,128]{2,1,0:T(8,128)S(1)}, f32[1,8,128]{2,1,0:T(8,128)S(1)}) custom-call(s32[1]{0:T(128)} %bitcast.me_ref, s32[640]{0:T(1024)S(1)} %reshape.17.near, s32[8]{0:T(128)S(1)} %copy-done.7, f32[8]{0:T(128)S(1)} %copy-done.3, f32[8]{0:T(128)S(1)} %copy-done.5, ...), custom_call_target="tpu_custom_call" | custom-call | tf_op jit(solution)/shard_map/fourth/pallas_call | solution.py:627
  137.4 1.9 %collective-permute-start.30 = (f32[1,8,128]{2,1,0:T(8,128)S(1)}, f32[1,8,128]{2,1,0:T(8,128)S(1)}, u32[]{:S(2)}, u32[]{:S(2)}) collective-permute-start(f32[1,8,128]{2,1,0:T(8,128)S(1)} %get-tuple-element.78), channel_id=1, source_target_pairs={{0,12},{1,13},{2,14},{3,15},{4,8},{5,9},{6,10},{7,11},{8,4},{9,5},... | collective-permute-start | bytes 12296 | tf_op jit(solution)/shard_map/ppermute | solution.py:590
  139.4 0.2 collective-permute-start.29
  139.5 2.4 %collective-permute-start.28 = (f32[1,8,128]{2,1,0:T(8,128)S(1)}, f32[1,8,128]{2,1,0:T(8,128)S(1)}, u32[]{:S(2)}, u32[]{:S(2)}) collective-permute-start(f32[1,8,128]{2,1,0:T(8,128)S(1)} %get-tuple-element.78), channel_id=1, source_target_pairs={{0,4},{1,5},{2,6},{3,7},{4,0},{5,1},{6,2},{7,3},{8,12},{9,13},{10,... | collective-permute-start | bytes 12296 | tf_op jit(solution)/shard_map/ppermute | solution.py:590
  141.9 1.0 collective-permute-done.30
  142.9 1.0 collective-permute-done.29
  143.9 1.5 %collective-permute-start.31 = (f32[4,1,8,128]{3,2,1,0:T(8,128)S(1)}, f32[4,1,8,128]{3,2,1,0:T(8,128)S(1)}, u32[]{:S(2)}, u32[]{:S(2)}) collective-permute-start(f32[4,1,8,128]{3,2,1,0:T(8,128)S(1)} %pad_maximum_fusion.5), channel_id=1, source_target_pairs={{0,2},{1,3},{2,0},{3,1},{4,6},{5,7},{6,4},{7,5},{8,10},{9,11},{10,... | collective-permute-start | bytes 49160 | tf_op jit(solution)/shard_map/ppermute | solution.py:590
  145.4 2.2 %collective-permute-done.31 = f32[4,1,8,128]{3,2,1,0:T(8,128)S(1)} collective-permute-done((f32[4,1,8,128]{3,2,1,0:T(8,128)S(1)}, f32[4,1,8,128]{3,2,1,0:T(8,128)S(1)}, u32[]{:S(2)}, u32[]{:S(2)}) %collective-permute-start.31) | collective-permute-done | bytes 16416 | tf_op jit(solution)/shard_map/ppermute | solution.py:590
  147.6 1.2 collective-permute-done.32.far_side
  148.8 1.9 %last.1 = (f32[128,8,128]{2,1,0:T(8,128)}, f32[128,8,128]{2,1,0:T(8,128)}) custom-call(f32[8,1,8,128]{3,2,1,0:T(8,128)S(1)} %constant_dynamic-update-slice_fusion.15.near_side, f32[8,1,8,128]{3,2,1,0:T(8,128)S(1)} %collective-permute-done.32.far_side, f32[128,8,128]{2,1,0:T(8,128)S(1)} %get-tuple-element.79.half_own, ...), custom_call_target="tpu_custom_call" | custom-call | tf_op jit(solution)/shard_map/last/pallas_call | solution.py:680
  (54 shorter events, 0.2 us)
Async XLA Ops:
  0.6 1.0 copy-start
  1.7 0.7 copy-start.6
  3.2 7.1 %collective-permute-start.3 = (f32[9,8,128]{2,1,0:T(8,128)S(1)}, f32[9,8,128]{2,1,0:T(8,128)S(1)}, u32[]{:S(2)}, u32[]{:S(2)}) collective-permute-start(f32[9,8,128]{2,1,0:T(8,128)S(1)} %get-tuple-element.43), channel_id=1, source_target_pairs={{0,12},{1,13},{2,14},{3,15},{4,8},{5,9},{6,10},{7,11},{8,4},{9,5},... | collective-permute-start | bytes 110600 | tf_op jit(solution)/shard_map/ppermute | solution.py:590
  8.3 4.9 %collective-permute-start.2 = (f32[9,8,128]{2,1,0:T(8,128)S(1)}, f32[9,8,128]{2,1,0:T(8,128)S(1)}, u32[]{:S(2)}, u32[]{:S(2)}) collective-permute-start(f32[9,8,128]{2,1,0:T(8,128)S(1)} %get-tuple-element.43), channel_id=1, source_target_pairs={{0,8},{1,9},{2,10},{3,11},{4,12},{5,13},{6,14},{7,15},{8,0},{9,1},... | collective-permute-start | bytes 110600 | tf_op jit(solution)/shard_map/ppermute | solution.py:590
  8.3 4.9 %collective-permute-start.1 = (f32[9,8,128]{2,1,0:T(8,128)S(1)}, f32[9,8,128]{2,1,0:T(8,128)S(1)}, u32[]{:S(2)}, u32[]{:S(2)}) collective-permute-start(f32[9,8,128]{2,1,0:T(8,128)S(1)} %get-tuple-element.43), channel_id=1, source_target_pairs={{0,4},{1,5},{2,6},{3,7},{4,0},{5,1},{6,2},{7,3},{8,12},{9,13},{10,... | collective-permute-start | bytes 110600 | tf_op jit(solution)/shard_map/ppermute | solution.py:590
  13.2 14.5 %collective-permute-start.4 = (f32[4,9,8,128]{3,2,1,0:T(8,128)S(1)}, f32[4,9,8,128]{3,2,1,0:T(8,128)S(1)}, u32[]{:S(2)}, u32[]{:S(2)}) collective-permute-start(f32[4,9,8,128]{3,2,1,0:T(8,128)S(1)} %pad_maximum_fusion.1), channel_id=1, source_target_pairs={{0,2},{1,3},{2,0},{3,1},{4,6},{5,7},{6,4},{7,5},{8,10},{9,11},{10,... | collective-permute-start | bytes 442376 | tf_op jit(solution)/shard_map/ppermute | solution.py:590
  14.8 12.9 %collective-permute-start = (f32[16,8,128]{2,1,0:T(8,128)S(1)}, f32[16,8,128]{2,1,0:T(8,128)S(1)}, u32[]{:S(2)}, u32[]{:S(2)}) collective-permute-start(f32[16,8,128]{2,1,0:T(8,128)S(1)} %get-tuple-element.42), channel_id=1, source_target_pairs={{0,15},{1,2},{2,1},{3,4},{4,3},{5,6},{6,5},{7,8},{8,7},{9,10},{10,... | collective-permute-start | bytes 196616 | tf_op jit(solution)/shard_map/ppermute | solution.py:597
  14.8 1.0 copy-start.1
  15.9 0.7 copy-start.2
  16.5 0.7 copy-start.4
  17.2 12.6 %copy-start.7 = (s32[8]{0:T(128)S(1)}, s32[8]{0:T(128)}, u32[]{:S(2)}) copy-start(s32[8]{0:T(128)} %contact.9) | copy-start | bytes 100
  27.7 2.0 %collective-permute-start.6 = (f32[8,9,8,128]{3,2,1,0:T(8,128)S(1)}, f32[8,9,8,128]{3,2,1,0:T(8,128)S(1)}, u32[]{:S(2)}, u32[]{:S(2)}) collective-permute-start(f32[8,9,8,128]{3,2,1,0:T(8,128)S(1)} %pad_maximum_fusion.near_side), channel_id=1, source_target_pairs={{0,1},{1,0},{2,3},{3,2},{4,5},{5,4},{6,7},{7,6},{8,9},{9,8},{10,11... | collective-permute-start | bytes 884744 | tf_op jit(solution)/shard_map/ppermute | solution.py:590
  28.4 1.3 collective-permute-start.5
  40.6 7.8 %collective-permute-start.11 = (f32[9,8,128]{2,1,0:T(8,128)S(1)}, f32[9,8,128]{2,1,0:T(8,128)S(1)}, u32[]{:S(2)}, u32[]{:S(2)}) collective-permute-start(f32[9,8,128]{2,1,0:T(8,128)S(1)} %get-tuple-element.54), channel_id=1, source_target_pairs={{0,12},{1,13},{2,14},{3,15},{4,8},{5,9},{6,10},{7,11},{8,4},{9,5},... | collective-permute-start | bytes 110600 | tf_op jit(solution)/shard_map/ppermute | solution.py:590
  42.2 6.3 %collective-permute-start.10 = (f32[9,8,128]{2,1,0:T(8,128)S(1)}, f32[9,8,128]{2,1,0:T(8,128)S(1)}, u32[]{:S(2)}, u32[]{:S(2)}) collective-permute-start(f32[9,8,128]{2,1,0:T(8,128)S(1)} %get-tuple-element.54), channel_id=1, source_target_pairs={{0,8},{1,9},{2,10},{3,11},{4,12},{5,13},{6,14},{7,15},{8,0},{9,1},... | collective-permute-start | bytes 110600 | tf_op jit(solution)/shard_map/ppermute | solution.py:590
  42.8 5.6 %collective-permute-start.9 = (f32[9,8,128]{2,1,0:T(8,128)S(1)}, f32[9,8,128]{2,1,0:T(8,128)S(1)}, u32[]{:S(2)}, u32[]{:S(2)}) collective-permute-start(f32[9,8,128]{2,1,0:T(8,128)S(1)} %get-tuple-element.54), channel_id=1, source_target_pairs={{0,4},{1,5},{2,6},{3,7},{4,0},{5,1},{6,2},{7,3},{8,12},{9,13},{10,... | collective-permute-start | bytes 110600 | tf_op jit(solution)/shard_map/ppermute | solution.py:590
  45.1 9.1 %collective-permute-start.8 = (f32[16,8,128]{2,1,0:T(8,128)S(1)}, f32[16,8,128]{2,1,0:T(8,128)S(1)}, u32[]{:S(2)}, u32[]{:S(2)}) collective-permute-start(f32[16,8,128]{2,1,0:T(8,128)S(1)} %get-tuple-element.53), channel_id=1, source_target_pairs={{0,15},{1,2},{2,1},{3,4},{4,3},{5,6},{6,5},{7,8},{8,7},{9,10},{10,... | collective-permute-start | bytes 196616 | tf_op jit(solution)/shard_map/ppermute | solution.py:597
  48.5 5.7 %collective-permute-start.12 = (f32[4,9,8,128]{3,2,1,0:T(8,128)S(1)}, f32[4,9,8,128]{3,2,1,0:T(8,128)S(1)}, u32[]{:S(2)}, u32[]{:S(2)}) collective-permute-start(f32[4,9,8,128]{3,2,1,0:T(8,128)S(1)} %pad_maximum_fusion.2), channel_id=1, source_target_pairs={{0,2},{1,3},{2,0},{3,1},{4,6},{5,7},{6,4},{7,5},{8,10},{9,11},{10,... | collective-permute-start | bytes 442376 | tf_op jit(solution)/shard_map/ppermute | solution.py:590
  54.2 1.7 %collective-permute-start.13 = (f32[8,9,8,128]{3,2,1,0:T(8,128)S(1)}, f32[8,9,8,128]{3,2,1,0:T(8,128)S(1)}, u32[]{:S(2)}, u32[]{:S(2)}) collective-permute-start(f32[8,9,8,128]{3,2,1,0:T(8,128)S(1)} %constant_dynamic-update-slice_fusion.near_side), channel_id=1, source_target_pairs={{0,1},{1,0},{2,3},{3,2},{4,5},{5,4},{6,7},{7,6},{8,9},{9,8},{10,11... | collective-permute-start | bytes 884744 | tf_op jit(solution)/shard_map/ppermute | solution.py:590
  54.3 1.7 %collective-permute-start.7 = (f32[16,8,128]{2,1,0:T(8,128)S(1)}, f32[16,8,128]{2,1,0:T(8,128)S(1)}, u32[]{:S(2)}, u32[]{:S(2)}) collective-permute-start(f32[16,8,128]{2,1,0:T(8,128)S(1)} %get-tuple-element.52), channel_id=1, source_target_pairs={{0,1},{1,0},{2,3},{3,2},{4,5},{5,4},{6,7},{7,6},{8,9},{9,8},{10,11... | collective-permute-start | bytes 196616 | tf_op jit(solution)/shard_map/ppermute | solution.py:590
  56.0 31.4 %copy-start.3 = (f32[8]{0:T(128)S(1)}, f32[8]{0:T(128)}, u32[]{:S(2)}) copy-start(f32[8]{0:T(128)} %pole_re.9) | copy-start | bytes 100
  56.0 31.4 %copy-start.5 = (f32[8]{0:T(128)S(1)}, f32[8]{0:T(128)}, u32[]{:S(2)}) copy-start(f32[8]{0:T(128)} %pole_im.9) | copy-start | bytes 100
  72.7 6.6 %collective-permute-start.18 = (f32[9,8,128]{2,1,0:T(8,128)S(1)}, f32[9,8,128]{2,1,0:T(8,128)S(1)}, u32[]{:S(2)}, u32[]{:S(2)}) collective-permute-start(f32[9,8,128]{2,1,0:T(8,128)S(1)} %get-tuple-element.63), channel_id=1, source_target_pairs={{0,12},{1,13},{2,14},{3,15},{4,8},{5,9},{6,10},{7,11},{8,4},{9,5},... | collective-permute-start | bytes 110600 | tf_op jit(solution)/shard_map/ppermute | solution.py:590
  74.4 5.2 %collective-permute-start.17 = (f32[9,8,128]{2,1,0:T(8,128)S(1)}, f32[9,8,128]{2,1,0:T(8,128)S(1)}, u32[]{:S(2)}, u32[]{:S(2)}) collective-permute-start(f32[9,8,128]{2,1,0:T(8,128)S(1)} %get-tuple-element.63), channel_id=1, source_target_pairs={{0,8},{1,9},{2,10},{3,11},{4,12},{5,13},{6,14},{7,15},{8,0},{9,1},... | collective-permute-start | bytes 110600 | tf_op jit(solution)/shard_map/ppermute | solution.py:590
  74.6 5.1 %collective-permute-start.16 = (f32[9,8,128]{2,1,0:T(8,128)S(1)}, f32[9,8,128]{2,1,0:T(8,128)S(1)}, u32[]{:S(2)}, u32[]{:S(2)}) collective-permute-start(f32[9,8,128]{2,1,0:T(8,128)S(1)} %get-tuple-element.63), channel_id=1, source_target_pairs={{0,4},{1,5},{2,6},{3,7},{4,0},{5,1},{6,2},{7,3},{8,12},{9,13},{10,... | collective-permute-start | bytes 110600 | tf_op jit(solution)/shard_map/ppermute | solution.py:590
  77.2 8.5 %collective-permute-start.15 = (f32[16,8,128]{2,1,0:T(8,128)S(1)}, f32[16,8,128]{2,1,0:T(8,128)S(1)}, u32[]{:S(2)}, u32[]{:S(2)}) collective-permute-start(f32[16,8,128]{2,1,0:T(8,128)S(1)} %get-tuple-element.62), channel_id=1, source_target_pairs={{0,15},{1,2},{2,1},{3,4},{4,3},{5,6},{6,5},{7,8},{8,7},{9,10},{10,... | collective-permute-start | bytes 196616 | tf_op jit(solution)/shard_map/ppermute | solution.py:597
  79.7 5.9 %collective-permute-start.19 = (f32[4,9,8,128]{3,2,1,0:T(8,128)S(1)}, f32[4,9,8,128]{3,2,1,0:T(8,128)S(1)}, u32[]{:S(2)}, u32[]{:S(2)}) collective-permute-start(f32[4,9,8,128]{3,2,1,0:T(8,128)S(1)} %pad_maximum_fusion.3), channel_id=1, source_target_pairs={{0,2},{1,3},{2,0},{3,1},{4,6},{5,7},{6,4},{7,5},{8,10},{9,11},{10,... | collective-permute-start | bytes 442376 | tf_op jit(solution)/shard_map/ppermute | solution.py:590
  85.7 1.7 %collective-permute-start.20 = (f32[8,9,8,128]{3,2,1,0:T(8,128)S(1)}, f32[8,9,8,128]{3,2,1,0:T(8,128)S(1)}, u32[]{:S(2)}, u32[]{:S(2)}) collective-permute-start(f32[8,9,8,128]{3,2,1,0:T(8,128)S(1)} %constant_dynamic-update-slice_fusion.5.near_side), channel_id=1, source_target_pairs={{0,1},{1,0},{2,3},{3,2},{4,5},{5,4},{6,7},{7,6},{8,9},{9,8},{10,11... | collective-permute-start | bytes 884744 | tf_op jit(solution)/shard_map/ppermute | solution.py:590
  85.7 1.7 %collective-permute-start.14 = (f32[16,8,128]{2,1,0:T(8,128)S(1)}, f32[16,8,128]{2,1,0:T(8,128)S(1)}, u32[]{:S(2)}, u32[]{:S(2)}) collective-permute-start(f32[16,8,128]{2,1,0:T(8,128)S(1)} %get-tuple-element.61), channel_id=1, source_target_pairs={{0,1},{1,0},{2,3},{3,2},{4,5},{5,4},{6,7},{7,6},{8,9},{9,8},{10,11... | collective-permute-start | bytes 196616 | tf_op jit(solution)/shard_map/ppermute | solution.py:590
  105.8 7.1 %collective-permute-start.25 = (f32[9,8,128]{2,1,0:T(8,128)S(1)}, f32[9,8,128]{2,1,0:T(8,128)S(1)}, u32[]{:S(2)}, u32[]{:S(2)}) collective-permute-start(f32[9,8,128]{2,1,0:T(8,128)S(1)} %get-tuple-element.75), channel_id=1, source_target_pairs={{0,12},{1,13},{2,14},{3,15},{4,8},{5,9},{6,10},{7,11},{8,4},{9,5},... | collective-permute-start | bytes 110600 | tf_op jit(solution)/shard_map/ppermute | solution.py:590
  108.0 4.9 %collective-permute-start.24 = (f32[9,8,128]{2,1,0:T(8,128)S(1)}, f32[9,8,128]{2,1,0:T(8,128)S(1)}, u32[]{:S(2)}, u32[]{:S(2)}) collective-permute-start(f32[9,8,128]{2,1,0:T(8,128)S(1)} %get-tuple-element.75), channel_id=1, source_target_pairs={{0,8},{1,9},{2,10},{3,11},{4,12},{5,13},{6,14},{7,15},{8,0},{9,1},... | collective-permute-start | bytes 110600 | tf_op jit(solution)/shard_map/ppermute | solution.py:590
  108.0 4.9 %collective-permute-start.23 = (f32[9,8,128]{2,1,0:T(8,128)S(1)}, f32[9,8,128]{2,1,0:T(8,128)S(1)}, u32[]{:S(2)}, u32[]{:S(2)}) collective-permute-start(f32[9,8,128]{2,1,0:T(8,128)S(1)} %get-tuple-element.75), channel_id=1, source_target_pairs={{0,4},{1,5},{2,6},{3,7},{4,0},{5,1},{6,2},{7,3},{8,12},{9,13},{10,... | collective-permute-start | bytes 110600 | tf_op jit(solution)/shard_map/ppermute | solution.py:590
  110.2 8.7 %collective-permute-start.22 = (f32[16,8,128]{2,1,0:T(8,128)S(1)}, f32[16,8,128]{2,1,0:T(8,128)S(1)}, u32[]{:S(2)}, u32[]{:S(2)}) collective-permute-start(f32[16,8,128]{2,1,0:T(8,128)S(1)} %get-tuple-element.74), channel_id=1, source_target_pairs={{0,15},{1,2},{2,1},{3,4},{4,3},{5,6},{6,5},{7,8},{8,7},{9,10},{10,... | collective-permute-start | bytes 196616 | tf_op jit(solution)/shard_map/ppermute | solution.py:597
  112.9 5.9 %collective-permute-start.26 = (f32[4,9,8,128]{3,2,1,0:T(8,128)S(1)}, f32[4,9,8,128]{3,2,1,0:T(8,128)S(1)}, u32[]{:S(2)}, u32[]{:S(2)}) collective-permute-start(f32[4,9,8,128]{3,2,1,0:T(8,128)S(1)} %pad_maximum_fusion.4), channel_id=1, source_target_pairs={{0,2},{1,3},{2,0},{3,1},{4,6},{5,7},{6,4},{7,5},{8,10},{9,11},{10,... | collective-permute-start | bytes 442376 | tf_op jit(solution)/shard_map/ppermute | solution.py:590
  118.9 1.7 %collective-permute-start.27 = (f32[8,9,8,128]{3,2,1,0:T(8,128)S(1)}, f32[8,9,8,128]{3,2,1,0:T(8,128)S(1)}, u32[]{:S(2)}, u32[]{:S(2)}) collective-permute-start(f32[8,9,8,128]{3,2,1,0:T(8,128)S(1)} %constant_dynamic-update-slice_fusion.10.near_side), channel_id=1, source_target_pairs={{0,1},{1,0},{2,3},{3,2},{4,5},{5,4},{6,7},{7,6},{8,9},{9,8},{10,11... | collective-permute-start | bytes 884744 | tf_op jit(solution)/shard_map/ppermute | solution.py:590
  119.0 1.7 %collective-permute-start.21 = (f32[16,8,128]{2,1,0:T(8,128)S(1)}, f32[16,8,128]{2,1,0:T(8,128)S(1)}, u32[]{:S(2)}, u32[]{:S(2)}) collective-permute-start(f32[16,8,128]{2,1,0:T(8,128)S(1)} %get-tuple-element.73), channel_id=1, source_target_pairs={{0,1},{1,0},{2,3},{3,2},{4,5},{5,4},{6,7},{7,6},{8,9},{9,8},{10,11... | collective-permute-start | bytes 196616 | tf_op jit(solution)/shard_map/ppermute | solution.py:590
  137.4 5.5 %collective-permute-start.30 = (f32[1,8,128]{2,1,0:T(8,128)S(1)}, f32[1,8,128]{2,1,0:T(8,128)S(1)}, u32[]{:S(2)}, u32[]{:S(2)}) collective-permute-start(f32[1,8,128]{2,1,0:T(8,128)S(1)} %get-tuple-element.78), channel_id=1, source_target_pairs={{0,12},{1,13},{2,14},{3,15},{4,8},{5,9},{6,10},{7,11},{8,4},{9,5},... | collective-permute-start | bytes 12296 | tf_op jit(solution)/shard_map/ppermute | solution.py:590
  139.4 4.5 %collective-permute-start.29 = (f32[1,8,128]{2,1,0:T(8,128)S(1)}, f32[1,8,128]{2,1,0:T(8,128)S(1)}, u32[]{:S(2)}, u32[]{:S(2)}) collective-permute-start(f32[1,8,128]{2,1,0:T(8,128)S(1)} %get-tuple-element.78), channel_id=1, source_target_pairs={{0,8},{1,9},{2,10},{3,11},{4,12},{5,13},{6,14},{7,15},{8,0},{9,1},... | collective-permute-start | bytes 12296 | tf_op jit(solution)/shard_map/ppermute | solution.py:590
  139.5 4.4 %collective-permute-start.28 = (f32[1,8,128]{2,1,0:T(8,128)S(1)}, f32[1,8,128]{2,1,0:T(8,128)S(1)}, u32[]{:S(2)}, u32[]{:S(2)}) collective-permute-start(f32[1,8,128]{2,1,0:T(8,128)S(1)} %get-tuple-element.78), channel_id=1, source_target_pairs={{0,4},{1,5},{2,6},{3,7},{4,0},{5,1},{6,2},{7,3},{8,12},{9,13},{10,... | collective-permute-start | bytes 12296 | tf_op jit(solution)/shard_map/ppermute | solution.py:590
  143.9 3.7 %collective-permute-start.31 = (f32[4,1,8,128]{3,2,1,0:T(8,128)S(1)}, f32[4,1,8,128]{3,2,1,0:T(8,128)S(1)}, u32[]{:S(2)}, u32[]{:S(2)}) collective-permute-start(f32[4,1,8,128]{3,2,1,0:T(8,128)S(1)} %pad_maximum_fusion.5), channel_id=1, source_target_pairs={{0,2},{1,3},{2,0},{3,1},{4,6},{5,7},{6,4},{7,5},{8,10},{9,11},{10,... | collective-permute-start | bytes 49160 | tf_op jit(solution)/shard_map/ppermute | solution.py:590
  147.6 1.2 collective-permute-start.32

commit v2 on v1

--- a/solution.py
+++ b/solution.py
@@ -485,30 +485,31 @@
     rho_out[1] = rho_next[1]
     rho_out[2] = norm_b
 
-    def update(s):
-        half = half_ext[pl.ds(s, TILE)]
-        residual = half - scale(omega, turned_ext[pl.ds(s, TILE)])
-        old = rhs_ext[pl.ds(s, TILE)]
-        direction = residual + scale(beta, old - scale(omega, image_ext[pl.ds(s, TILE)]))
-        store_wide(wide, s, TILE, direction)
+    def update(s, size):
+        here = pl.ds(s, size)
+        half = half_ext[here]
+        residual = half - scale(omega, turned_ext[here])
+        old = rhs_ext[here]
+        direction = residual + scale(beta, old - scale(omega, image_ext[here]))
+        store_wide(wide, s, size, direction)
         return residual, direction
 
     def update_own(s):
-        residual, direction = update(NYB + s)
-        residual_own[pl.ds(s, TILE)] = residual
-        direction_own[pl.ds(s, TILE)] = direction
-        iterate[pl.ds(s, TILE)] = scale(alpha, rhs_ext[pl.ds(NYB + s, TILE)]) + scale(
-            omega, half_ext[pl.ds(NYB + s, TILE)]
-        )
-
-    def update_rest(source, target):
-        residual, direction = update(source)
-        residual_rem[pl.ds(target, TILE)] = residual
-        direction_rem[pl.ds(target, TILE)] = direction
-
-    over_rows(blocks, TILE, update_own)
-    update_rest(0, 0)
-    over_rows(NYB + CONTACT, TILE, lambda s: update_rest(NYB + blocks + s, NYB + s))
+        residual, direction = update(NYB + s, 2 * TILE)
+        residual_own[pl.ds(s, 2 * TILE)] = residual
+        direction_own[pl.ds(s, 2 * TILE)] = direction
+        here = pl.ds(NYB + s, 2 * TILE)
+        iterate[pl.ds(s, 2 * TILE)] = scale(alpha, rhs_ext[here]) + scale(omega, half_ext[here])
+
+    def update_rest(source, target, size):
+        residual, direction = update(source, size)
+        residual_rem[pl.ds(target, size)] = residual
+        direction_rem[pl.ds(target, size)] = direction
+
+    over_rows(blocks, 2 * TILE, update_own)
+    update_rest(0, 0, NYB)
+    update_rest(NYB + blocks, NYB, NYB)
+    over_rows(CONTACT, 2 * TILE, lambda s: update_rest(2 * NYB + blocks + s, 2 * NYB + s, 2 * TILE))
     apply_operator(near, spots, z, wide, ham, ovl, sigma, mats, sems, acc, image)
 
     def terms(s):
@@ -535,23 +536,24 @@
     alpha = guarded_quotient((rho_in[0], rho_in[1]), (bv_re, bv_im), norm_b * vv)
 
     def update_own(s):
-        here = pl.ds(s, TILE)
+        here = pl.ds(s, 2 * TILE)
         half = residual_own[here] - scale(alpha, own[here])
         half_own[here] = half
         iterate[here] = iterate_in[here] + scale(alpha, direction_own[here])
-        store_wide(wide, NYB + s, TILE, half)
-
-    over_rows(blocks, TILE, update_own)
+        store_wide(wide, NYB + s, 2 * TILE, half)
+
+    over_rows(blocks, 2 * TILE, update_own)
     for start, image in zip(halo_starts(me_ref[0], blocks), (partner, other)):
         remote = jnp.where(start == 0, 0, NYB)
         half = residual_rem[pl.ds(remote, NYB)] - scale(alpha, image[...])
         store_wide(wide, start, NYB, half)
 
     def update_contact(s):
-        half = residual_rem[pl.ds(2 * NYB + s, TILE)] - scale(alpha, contact_image[pl.ds(s, TILE)])
-        store_wide(wide, 2 * NYB + blocks + s, TILE, half)
-
-    over_rows(CONTACT, TILE, update_contact)
+        here = pl.ds(2 * NYB + s, 2 * TILE)
+        half = residual_rem[here] - scale(alpha, contact_image[pl.ds(s, 2 * TILE)])
+        store_wide(wide, 2 * NYB + blocks + s, 2 * TILE, half)
+
+    over_rows(CONTACT, 2 * TILE, update_contact)
     apply_operator(near, spots, z, wide, ham, ovl, sigma, mats, sems, acc, turned)
 
     def terms(s):
@@ -568,12 +570,12 @@
     omega = (th_re / turned_sq, th_im / turned_sq)
 
     def update(s):
-        here = pl.ds(s, TILE)
+        here = pl.ds(s, 2 * TILE)
         half = half_own[here]
         solution_out[here] = iterate[here] + scale(omega, half)
         residual_out[here] = half - scale(omega, turned[here])
 
-    over_rows(half_own.shape[0], TILE, update)
+    over_rows(half_own.shape[0], 2 * TILE, update)
 
 
 def local(rhs, ham, ovl, sigma, neighbours, contact, pole_real, pole_imag):

time: 151 us -> 149 us (0.987)
  Pallas kernels: 76 us -> 73.9 us
    pallas_call x4, Pallas kernels: 62.7 us -> 61 us  [call(): pl.pallas_call(kernel, in_specs=[SMEM] * 5 + [VMEM] * (len(inputs) - 5) +...]
where the time goes in v2:
time: 149 us
  Pallas kernels  73.9 us (50%)
  starting transfers between devices  43.6 us (29%)
  waiting for transfers between devices  25 us (17%)
  local copies, waits for them, and re-layouts  4.46 us (3%)
    pallas_call x4, Pallas kernels, call(): pl.pallas_call(kernel, in_specs=[SMEM] * 5 + [VMEM] * (len(inputs) - 5) +...  61 us
    ppermute x29, starting transfers between devices, flip(): return lax.ppermute(value, 'gx', [(i, i ^ mask) for i in range(count)])  35.4 us
    ppermute x29, waiting for transfers between devices, flip(): return lax.ppermute(value, 'gx', [(i, i ^ mask) for i in range(count)])  24.9 us
    pallas_call x1, Pallas kernels, own_part(): pl.pallas_call(functools.partial(own_kernel, 0), in_specs=[SMEM] * 3 + [V...  10.5 us
    ppermute x4, starting transfers between devices, exchange(): far = (lax.ppermute(edges[1], 'gx', other),)  8.15 us
    unnamed x32, local copies, waits for them, and re-layouts  4.11 us
  transfers between devices with their start and end apart: 33, of which 15 were waited for; matrix products, arithmetic and copies ran while one was open for 1% of the time, Pallas kernels for 7%

profile of v2, /device:TPU:0, one launch (start us, length us, event | category | flops | bytes accessed | tf_op | source)
XLA Modules:
  0.0 148.6 jit_solution(16089363506300018941)
XLA Ops:
  0.6 0.0 copy-start
  0.6 1.0 copy-done
  1.7 0.7 copy-done.6
  2.3 0.9 prepare.1
  3.2 5.1 %collective-permute-start.3 = (f32[9,8,128]{2,1,0:T(8,128)S(1)}, f32[9,8,128]{2,1,0:T(8,128)S(1)}, u32[]{:S(2)}, u32[]{:S(2)}) collective-permute-start(f32[9,8,128]{2,1,0:T(8,128)S(1)} %get-tuple-element.43), channel_id=1, source_target_pairs={{0,12},{1,13},{2,14},{3,15},{4,8},{5,9},{6,10},{7,11},{8,4},{9,5},... | collective-permute-start | bytes 110600 | tf_op jit(solution)/shard_map/ppermute | solution.py:592
  8.3 0.0 collective-permute-start.2
  8.3 0.6 collective-permute-start.1
  9.0 0.7 add_select_fusion
  9.7 0.1 copy.10
  9.8 0.2 reshape.17.near
  10.0 0.3 collective-permute-done.3
  10.3 2.9 %collective-permute-done.2 = f32[9,8,128]{2,1,0:T(8,128)S(1)} collective-permute-done((f32[9,8,128]{2,1,0:T(8,128)S(1)}, f32[9,8,128]{2,1,0:T(8,128)S(1)}, u32[]{:S(2)}, u32[]{:S(2)}) %collective-permute-start.2) | collective-permute-done | bytes 36896 | tf_op jit(solution)/shard_map/ppermute | solution.py:592
  13.2 1.6 %collective-permute-start.4 = (f32[4,9,8,128]{3,2,1,0:T(8,128)S(1)}, f32[4,9,8,128]{3,2,1,0:T(8,128)S(1)}, u32[]{:S(2)}, u32[]{:S(2)}) collective-permute-start(f32[4,9,8,128]{3,2,1,0:T(8,128)S(1)} %pad_maximum_fusion.1), channel_id=1, source_target_pairs={{0,2},{1,3},{2,0},{3,1},{4,6},{5,7},{6,4},{7,5},{8,10},{9,11},{10,... | collective-permute-start | bytes 442376 | tf_op jit(solution)/shard_map/ppermute | solution.py:592
  14.8 0.0 collective-permute-start
  14.8 1.0 copy-done.1
  15.9 0.7 copy-done.2
  16.5 0.7 copy-done.4
  17.2 10.5 %own.3.image_in = f32[128,8,128]{2,1,0:T(8,128)S(1)} custom-call(s32[640]{0:T(1024)S(1)} %reshape.17.near, f32[8]{0:T(128)S(1)} %copy-done.2, f32[8]{0:T(128)S(1)} %copy-done.4, f32[128,8,128]{2,1,0:T(8,128)S(1)} %copy-done.1, bf16[320,128,128]{2,1,0:T(8,128)(2,1)} %bitcast.44, bf16[320,128,128]{2,1,0:T(8,128)(2,1)} %bitcast.49), custom_call_target="tpu_custom_call" | custom-call | flops 335544320 | bytes 20971520 | tf_op jit(solution)/shard_map/own/pallas_call | solution.py:649
  27.7 0.7 collective-permute-start.6
  28.4 0.1 collective-permute-start.5
  28.5 1.2 collective-permute-done.5.partner
  29.7 0.0 collective-permute-done.6.far_side
  29.7 10.9 %first.1 = (f32[288,8,128]{2,1,0:T(8,128)S(1)}, f32[128,8,128]{2,1,0:T(8,128)S(1)}, f32[9,8,128]{2,1,0:T(8,128)S(1)}, f32[16,8,128]{2,1,0:T(8,128)S(1)}, f32[16,8,128]{2,1,0:T(8,128)S(1)}) custom-call(s32[1]{0:T(128)} %bitcast.me_ref, s32[640]{0:T(1024)S(1)} %reshape.17.near, s32[8]{0:T(128)S(1)} %copy-done.7, f32[8]{0:T(128)S(1)} %copy-done.2, ...), custom_call_target="tpu_custom_call" | custom-call | tf_op jit(solution)/shard_map/first/pallas_call | solution.py:629
  40.6 1.5 %collective-permute-start.11 = (f32[9,8,128]{2,1,0:T(8,128)S(1)}, f32[9,8,128]{2,1,0:T(8,128)S(1)}, u32[]{:S(2)}, u32[]{:S(2)}) collective-permute-start(f32[9,8,128]{2,1,0:T(8,128)S(1)} %get-tuple-element.54), channel_id=1, source_target_pairs={{0,12},{1,13},{2,14},{3,15},{4,8},{5,9},{6,10},{7,11},{8,4},{9,5},... | collective-permute-start | bytes 110600 | tf_op jit(solution)/shard_map/ppermute | solution.py:592
  42.2 0.6 collective-permute-start.10
  42.8 2.3 %collective-permute-start.9 = (f32[9,8,128]{2,1,0:T(8,128)S(1)}, f32[9,8,128]{2,1,0:T(8,128)S(1)}, u32[]{:S(2)}, u32[]{:S(2)}) collective-permute-start(f32[9,8,128]{2,1,0:T(8,128)S(1)} %get-tuple-element.54), channel_id=1, source_target_pairs={{0,4},{1,5},{2,6},{3,7},{4,0},{5,1},{6,2},{7,3},{8,12},{9,13},{10,... | collective-permute-start | bytes 110600 | tf_op jit(solution)/shard_map/ppermute | solution.py:592
  45.1 3.3 %collective-permute-start.8 = (f32[16,8,128]{2,1,0:T(8,128)S(1)}, f32[16,8,128]{2,1,0:T(8,128)S(1)}, u32[]{:S(2)}, u32[]{:S(2)}) collective-permute-start(f32[16,8,128]{2,1,0:T(8,128)S(1)} %get-tuple-element.53), channel_id=1, source_target_pairs={{0,15},{1,2},{2,1},{3,4},{4,3},{5,6},{6,5},{7,8},{8,7},{9,10},{10,... | collective-permute-start | bytes 196616 | tf_op jit(solution)/shard_map/ppermute | solution.py:599
  48.5 2.0 %collective-permute-start.12 = (f32[4,9,8,128]{3,2,1,0:T(8,128)S(1)}, f32[4,9,8,128]{3,2,1,0:T(8,128)S(1)}, u32[]{:S(2)}, u32[]{:S(2)}) collective-permute-start(f32[4,9,8,128]{3,2,1,0:T(8,128)S(1)} %pad_maximum_fusion.2), channel_id=1, source_target_pairs={{0,2},{1,3},{2,0},{3,1},{4,6},{5,7},{6,4},{7,5},{8,10},{9,11},{10,... | collective-permute-start | bytes 442376 | tf_op jit(solution)/shard_map/ppermute | solution.py:592
  50.4 3.7 %collective-permute-done.12 = f32[4,9,8,128]{3,2,1,0:T(8,128)S(1)} collective-permute-done((f32[4,9,8,128]{3,2,1,0:T(8,128)S(1)}, f32[4,9,8,128]{3,2,1,0:T(8,128)S(1)}, u32[]{:S(2)}, u32[]{:S(2)}) %collective-permute-start.12) | collective-permute-done | bytes 147488 | tf_op jit(solution)/shard_map/ppermute | solution.py:592
  54.2 0.1 collective-permute-start.13
  54.3 0.5 collective-permute-start.7
  54.8 1.2 collective-permute-done.7.partner
  56.0 16.7 %second.1 = (f32[288,8,128]{2,1,0:T(8,128)S(1)}, f32[288,8,128]{2,1,0:T(8,128)S(1)}, f32[128,8,128]{2,1,0:T(8,128)S(1)}, f32[9,8,128]{2,1,0:T(8,128)S(1)}, f32[1...) custom-call(s32[1]{0:T(128)} %bitcast.me_ref, s32[640]{0:T(1024)S(1)} %reshape.17.near, ...), custom_call_target="tpu_custom_call" | custom-call | tf_op jit(solution)/shard_map/second/pallas_call | solution.py:629
  72.7 1.7 %collective-permute-start.18 = (f32[9,8,128]{2,1,0:T(8,128)S(1)}, f32[9,8,128]{2,1,0:T(8,128)S(1)}, u32[]{:S(2)}, u32[]{:S(2)}) collective-permute-start(f32[9,8,128]{2,1,0:T(8,128)S(1)} %get-tuple-element.63), channel_id=1, source_target_pairs={{0,12},{1,13},{2,14},{3,15},{4,8},{5,9},{6,10},{7,11},{8,4},{9,5},... | collective-permute-start | bytes 110600 | tf_op jit(solution)/shard_map/ppermute | solution.py:592
  74.4 0.2 collective-permute-start.17
  74.6 2.5 %collective-permute-start.16 = (f32[9,8,128]{2,1,0:T(8,128)S(1)}, f32[9,8,128]{2,1,0:T(8,128)S(1)}, u32[]{:S(2)}, u32[]{:S(2)}) collective-permute-start(f32[9,8,128]{2,1,0:T(8,128)S(1)} %get-tuple-element.63), channel_id=1, source_target_pairs={{0,4},{1,5},{2,6},{3,7},{4,0},{5,1},{6,2},{7,3},{8,12},{9,13},{10,... | collective-permute-start | bytes 110600 | tf_op jit(solution)/shard_map/ppermute | solution.py:592
  77.1 2.1 %collective-permute-start.15 = (f32[16,8,128]{2,1,0:T(8,128)S(1)}, f32[16,8,128]{2,1,0:T(8,128)S(1)}, u32[]{:S(2)}, u32[]{:S(2)}) collective-permute-start(f32[16,8,128]{2,1,0:T(8,128)S(1)} %get-tuple-element.62), channel_id=1, source_target_pairs={{0,15},{1,2},{2,1},{3,4},{4,3},{5,6},{6,5},{7,8},{8,7},{9,10},{10,... | collective-permute-start | bytes 196616 | tf_op jit(solution)/shard_map/ppermute | solution.py:599
  79.3 0.4 collective-permute-done.17
  79.6 0.1 collective-permute-done.16
  79.7 2.2 %collective-permute-start.19 = (f32[4,9,8,128]{3,2,1,0:T(8,128)S(1)}, f32[4,9,8,128]{3,2,1,0:T(8,128)S(1)}, u32[]{:S(2)}, u32[]{:S(2)}) collective-permute-start(f32[4,9,8,128]{3,2,1,0:T(8,128)S(1)} %pad_maximum_fusion.3), channel_id=1, source_target_pairs={{0,2},{1,3},{2,0},{3,1},{4,6},{5,7},{6,4},{7,5},{8,10},{9,11},{10,... | collective-permute-start | bytes 442376 | tf_op jit(solution)/shard_map/ppermute | solution.py:592
  81.9 3.7 %collective-permute-done.19 = f32[4,9,8,128]{3,2,1,0:T(8,128)S(1)} collective-permute-done((f32[4,9,8,128]{3,2,1,0:T(8,128)S(1)}, f32[4,9,8,128]{3,2,1,0:T(8,128)S(1)}, u32[]{:S(2)}, u32[]{:S(2)}) %collective-permute-start.19) | collective-permute-done | bytes 147488 | tf_op jit(solution)/shard_map/ppermute | solution.py:592
  85.7 0.1 collective-permute-start.20
  85.7 0.5 collective-permute-start.14
  86.2 1.2 collective-permute-done.14.partner
  87.4 16.8 %third.1 = (f32[128,8,128]{2,1,0:T(8,128)S(1)}, f32[128,8,128]{2,1,0:T(8,128)S(1)}, f32[160,8,128]{2,1,0:T(8,128)S(1)}, f32[160,8,128]{2,1,0:T(8,128)S(1)}, f32[...) custom-call(s32[1]{0:T(128)} %bitcast.me_ref, ...), custom_call_target="tpu_custom_call" | custom-call | tf_op jit(solution)/shard_map/third/pallas_call | solution.py:629
  104.2 2.2 %collective-permute-start.25 = (f32[9,8,128]{2,1,0:T(8,128)S(1)}, f32[9,8,128]{2,1,0:T(8,128)S(1)}, u32[]{:S(2)}, u32[]{:S(2)}) collective-permute-start(f32[9,8,128]{2,1,0:T(8,128)S(1)} %get-tuple-element.75), channel_id=1, source_target_pairs={{0,12},{1,13},{2,14},{3,15},{4,8},{5,9},{6,10},{7,11},{8,4},{9,5},... | collective-permute-start | bytes 110600 | tf_op jit(solution)/shard_map/ppermute | solution.py:592
  106.4 0.0 collective-permute-start.24
  106.4 2.2 %collective-permute-start.23 = (f32[9,8,128]{2,1,0:T(8,128)S(1)}, f32[9,8,128]{2,1,0:T(8,128)S(1)}, u32[]{:S(2)}, u32[]{:S(2)}) collective-permute-start(f32[9,8,128]{2,1,0:T(8,128)S(1)} %get-tuple-element.75), channel_id=1, source_target_pairs={{0,4},{1,5},{2,6},{3,7},{4,0},{5,1},{6,2},{7,3},{8,12},{9,13},{10,... | collective-permute-start | bytes 110600 | tf_op jit(solution)/shard_map/ppermute | solution.py:592
  108.7 2.7 %collective-permute-start.22 = (f32[16,8,128]{2,1,0:T(8,128)S(1)}, f32[16,8,128]{2,1,0:T(8,128)S(1)}, u32[]{:S(2)}, u32[]{:S(2)}) collective-permute-start(f32[16,8,128]{2,1,0:T(8,128)S(1)} %get-tuple-element.74), channel_id=1, source_target_pairs={{0,15},{1,2},{2,1},{3,4},{4,3},{5,6},{6,5},{7,8},{8,7},{9,10},{10,... | collective-permute-start | bytes 196616 | tf_op jit(solution)/shard_map/ppermute | solution.py:599
  111.4 2.2 %collective-permute-start.26 = (f32[4,9,8,128]{3,2,1,0:T(8,128)S(1)}, f32[4,9,8,128]{3,2,1,0:T(8,128)S(1)}, u32[]{:S(2)}, u32[]{:S(2)}) collective-permute-start(f32[4,9,8,128]{3,2,1,0:T(8,128)S(1)} %pad_maximum_fusion.4), channel_id=1, source_target_pairs={{0,2},{1,3},{2,0},{3,1},{4,6},{5,7},{6,4},{7,5},{8,10},{9,11},{10,... | collective-permute-start | bytes 442376 | tf_op jit(solution)/shard_map/ppermute | solution.py:592
  113.6 3.7 %collective-permute-done.26 = f32[4,9,8,128]{3,2,1,0:T(8,128)S(1)} collective-permute-done((f32[4,9,8,128]{3,2,1,0:T(8,128)S(1)}, f32[4,9,8,128]{3,2,1,0:T(8,128)S(1)}, u32[]{:S(2)}, u32[]{:S(2)}) %collective-permute-start.26) | collective-permute-done | bytes 147488 | tf_op jit(solution)/shard_map/ppermute | solution.py:592
  117.3 0.1 collective-permute-start.27
  117.4 0.5 collective-permute-start.21
  117.9 1.2 collective-permute-done.21.partner
  119.1 16.6 %fourth.1 = (f32[128,8,128]{2,1,0:T(8,128)S(1)}, f32[128,8,128]{2,1,0:T(8,128)S(1)}, f32[128,8,128]{2,1,0:T(8,128)S(1)}, f32[1,8,128]{2,1,0:T(8,128)S(1)}) custom-call(s32[1]{0:T(128)} %bitcast.me_ref, s32[640]{0:T(1024)S(1)} %reshape.17.near, s32[8]{0:T(128)S(1)} %copy-done.7, f32[8]{0:T(128)S(1)} %copy-done.3, f32[8]{0:T(128)S(1)} %copy-done.5, ...), custom_call_target="tpu_custom_call" | custom-call | tf_op jit(solution)/shard_map/fourth/pallas_call | solution.py:629
  135.6 1.9 %collective-permute-start.30 = (f32[1,8,128]{2,1,0:T(8,128)S(1)}, f32[1,8,128]{2,1,0:T(8,128)S(1)}, u32[]{:S(2)}, u32[]{:S(2)}) collective-permute-start(f32[1,8,128]{2,1,0:T(8,128)S(1)} %get-tuple-element.78), channel_id=1, source_target_pairs={{0,12},{1,13},{2,14},{3,15},{4,8},{5,9},{6,10},{7,11},{8,4},{9,5},... | collective-permute-start | bytes 12296 | tf_op jit(solution)/shard_map/ppermute | solution.py:592
  137.6 0.2 collective-permute-start.29
  137.7 2.4 %collective-permute-start.28 = (f32[1,8,128]{2,1,0:T(8,128)S(1)}, f32[1,8,128]{2,1,0:T(8,128)S(1)}, u32[]{:S(2)}, u32[]{:S(2)}) collective-permute-start(f32[1,8,128]{2,1,0:T(8,128)S(1)} %get-tuple-element.78), channel_id=1, source_target_pairs={{0,4},{1,5},{2,6},{3,7},{4,0},{5,1},{6,2},{7,3},{8,12},{9,13},{10,... | collective-permute-start | bytes 12296 | tf_op jit(solution)/shard_map/ppermute | solution.py:592
  140.1 1.0 collective-permute-done.30
  141.1 1.0 collective-permute-done.29
  142.1 1.5 %collective-permute-start.31 = (f32[4,1,8,128]{3,2,1,0:T(8,128)S(1)}, f32[4,1,8,128]{3,2,1,0:T(8,128)S(1)}, u32[]{:S(2)}, u32[]{:S(2)}) collective-permute-start(f32[4,1,8,128]{3,2,1,0:T(8,128)S(1)} %pad_maximum_fusion.5), channel_id=1, source_target_pairs={{0,2},{1,3},{2,0},{3,1},{4,6},{5,7},{6,4},{7,5},{8,10},{9,11},{10,... | collective-permute-start | bytes 49160 | tf_op jit(solution)/shard_map/ppermute | solution.py:592
  143.6 2.2 %collective-permute-done.31 = f32[4,1,8,128]{3,2,1,0:T(8,128)S(1)} collective-permute-done((f32[4,1,8,128]{3,2,1,0:T(8,128)S(1)}, f32[4,1,8,128]{3,2,1,0:T(8,128)S(1)}, u32[]{:S(2)}, u32[]{:S(2)}) %collective-permute-start.31) | collective-permute-done | bytes 16416 | tf_op jit(solution)/shard_map/ppermute | solution.py:592
  145.8 1.2 collective-permute-done.32.far_side
  147.0 1.6 %last.1 = (f32[128,8,128]{2,1,0:T(8,128)}, f32[128,8,128]{2,1,0:T(8,128)}) custom-call(f32[8,1,8,128]{3,2,1,0:T(8,128)S(1)} %constant_dynamic-update-slice_fusion.15.near_side, f32[8,1,8,128]{3,2,1,0:T(8,128)S(1)} %collective-permute-done.32.far_side, f32[128,8,128]{2,1,0:T(8,128)S(1)} %get-tuple-element.79.half_own, ...), custom_call_target="tpu_custom_call" | custom-call | tf_op jit(solution)/shard_map/last/pallas_call | solution.py:682
  (54 shorter events, 0.2 us)
Async XLA Ops:
  0.6 1.0 copy-start
  1.7 0.7 copy-start.6
  3.2 7.1 %collective-permute-start.3 = (f32[9,8,128]{2,1,0:T(8,128)S(1)}, f32[9,8,128]{2,1,0:T(8,128)S(1)}, u32[]{:S(2)}, u32[]{:S(2)}) collective-permute-start(f32[9,8,128]{2,1,0:T(8,128)S(1)} %get-tuple-element.43), channel_id=1, source_target_pairs={{0,12},{1,13},{2,14},{3,15},{4,8},{5,9},{6,10},{7,11},{8,4},{9,5},... | collective-permute-start | bytes 110600 | tf_op jit(solution)/shard_map/ppermute | solution.py:592
  8.3 4.9 %collective-permute-start.2 = (f32[9,8,128]{2,1,0:T(8,128)S(1)}, f32[9,8,128]{2,1,0:T(8,128)S(1)}, u32[]{:S(2)}, u32[]{:S(2)}) collective-permute-start(f32[9,8,128]{2,1,0:T(8,128)S(1)} %get-tuple-element.43), channel_id=1, source_target_pairs={{0,8},{1,9},{2,10},{3,11},{4,12},{5,13},{6,14},{7,15},{8,0},{9,1},... | collective-permute-start | bytes 110600 | tf_op jit(solution)/shard_map/ppermute | solution.py:592
  8.3 4.9 %collective-permute-start.1 = (f32[9,8,128]{2,1,0:T(8,128)S(1)}, f32[9,8,128]{2,1,0:T(8,128)S(1)}, u32[]{:S(2)}, u32[]{:S(2)}) collective-permute-start(f32[9,8,128]{2,1,0:T(8,128)S(1)} %get-tuple-element.43), channel_id=1, source_target_pairs={{0,4},{1,5},{2,6},{3,7},{4,0},{5,1},{6,2},{7,3},{8,12},{9,13},{10,... | collective-permute-start | bytes 110600 | tf_op jit(solution)/shard_map/ppermute | solution.py:592
  13.2 14.5 %collective-permute-start.4 = (f32[4,9,8,128]{3,2,1,0:T(8,128)S(1)}, f32[4,9,8,128]{3,2,1,0:T(8,128)S(1)}, u32[]{:S(2)}, u32[]{:S(2)}) collective-permute-start(f32[4,9,8,128]{3,2,1,0:T(8,128)S(1)} %pad_maximum_fusion.1), channel_id=1, source_target_pairs={{0,2},{1,3},{2,0},{3,1},{4,6},{5,7},{6,4},{7,5},{8,10},{9,11},{10,... | collective-permute-start | bytes 442376 | tf_op jit(solution)/shard_map/ppermute | solution.py:592
  14.8 12.9 %collective-permute-start = (f32[16,8,128]{2,1,0:T(8,128)S(1)}, f32[16,8,128]{2,1,0:T(8,128)S(1)}, u32[]{:S(2)}, u32[]{:S(2)}) collective-permute-start(f32[16,8,128]{2,1,0:T(8,128)S(1)} %get-tuple-element.42), channel_id=1, source_target_pairs={{0,15},{1,2},{2,1},{3,4},{4,3},{5,6},{6,5},{7,8},{8,7},{9,10},{10,... | collective-permute-start | bytes 196616 | tf_op jit(solution)/shard_map/ppermute | solution.py:599
  14.8 1.0 copy-start.1
  15.9 0.7 copy-start.2
  16.5 0.7 copy-start.4
  17.2 12.6 %copy-start.7 = (s32[8]{0:T(128)S(1)}, s32[8]{0:T(128)}, u32[]{:S(2)}) copy-start(s32[8]{0:T(128)} %contact.9) | copy-start | bytes 100
  27.7 2.0 %collective-permute-start.6 = (f32[8,9,8,128]{3,2,1,0:T(8,128)S(1)}, f32[8,9,8,128]{3,2,1,0:T(8,128)S(1)}, u32[]{:S(2)}, u32[]{:S(2)}) collective-permute-start(f32[8,9,8,128]{3,2,1,0:T(8,128)S(1)} %pad_maximum_fusion.near_side), channel_id=1, source_target_pairs={{0,1},{1,0},{2,3},{3,2},{4,5},{5,4},{6,7},{7,6},{8,9},{9,8},{10,11... | collective-permute-start | bytes 884744 | tf_op jit(solution)/shard_map/ppermute | solution.py:592
  28.4 1.3 collective-permute-start.5
  40.6 7.8 %collective-permute-start.11 = (f32[9,8,128]{2,1,0:T(8,128)S(1)}, f32[9,8,128]{2,1,0:T(8,128)S(1)}, u32[]{:S(2)}, u32[]{:S(2)}) collective-permute-start(f32[9,8,128]{2,1,0:T(8,128)S(1)} %get-tuple-element.54), channel_id=1, source_target_pairs={{0,12},{1,13},{2,14},{3,15},{4,8},{5,9},{6,10},{7,11},{8,4},{9,5},... | collective-permute-start | bytes 110600 | tf_op jit(solution)/shard_map/ppermute | solution.py:592
  42.2 6.3 %collective-permute-start.10 = (f32[9,8,128]{2,1,0:T(8,128)S(1)}, f32[9,8,128]{2,1,0:T(8,128)S(1)}, u32[]{:S(2)}, u32[]{:S(2)}) collective-permute-start(f32[9,8,128]{2,1,0:T(8,128)S(1)} %get-tuple-element.54), channel_id=1, source_target_pairs={{0,8},{1,9},{2,10},{3,11},{4,12},{5,13},{6,14},{7,15},{8,0},{9,1},... | collective-permute-start | bytes 110600 | tf_op jit(solution)/shard_map/ppermute | solution.py:592
  42.8 5.6 %collective-permute-start.9 = (f32[9,8,128]{2,1,0:T(8,128)S(1)}, f32[9,8,128]{2,1,0:T(8,128)S(1)}, u32[]{:S(2)}, u32[]{:S(2)}) collective-permute-start(f32[9,8,128]{2,1,0:T(8,128)S(1)} %get-tuple-element.54), channel_id=1, source_target_pairs={{0,4},{1,5},{2,6},{3,7},{4,0},{5,1},{6,2},{7,3},{8,12},{9,13},{10,... | collective-permute-start | bytes 110600 | tf_op jit(solution)/shard_map/ppermute | solution.py:592
  45.1 9.1 %collective-permute-start.8 = (f32[16,8,128]{2,1,0:T(8,128)S(1)}, f32[16,8,128]{2,1,0:T(8,128)S(1)}, u32[]{:S(2)}, u32[]{:S(2)}) collective-permute-start(f32[16,8,128]{2,1,0:T(8,128)S(1)} %get-tuple-element.53), channel_id=1, source_target_pairs={{0,15},{1,2},{2,1},{3,4},{4,3},{5,6},{6,5},{7,8},{8,7},{9,10},{10,... | collective-permute-start | bytes 196616 | tf_op jit(solution)/shard_map/ppermute | solution.py:599
  48.5 5.7 %collective-permute-start.12 = (f32[4,9,8,128]{3,2,1,0:T(8,128)S(1)}, f32[4,9,8,128]{3,2,1,0:T(8,128)S(1)}, u32[]{:S(2)}, u32[]{:S(2)}) collective-permute-start(f32[4,9,8,128]{3,2,1,0:T(8,128)S(1)} %pad_maximum_fusion.2), channel_id=1, source_target_pairs={{0,2},{1,3},{2,0},{3,1},{4,6},{5,7},{6,4},{7,5},{8,10},{9,11},{10,... | collective-permute-start | bytes 442376 | tf_op jit(solution)/shard_map/ppermute | solution.py:592
  54.2 1.7 %collective-permute-start.13 = (f32[8,9,8,128]{3,2,1,0:T(8,128)S(1)}, f32[8,9,8,128]{3,2,1,0:T(8,128)S(1)}, u32[]{:S(2)}, u32[]{:S(2)}) collective-permute-start(f32[8,9,8,128]{3,2,1,0:T(8,128)S(1)} %constant_dynamic-update-slice_fusion.near_side), channel_id=1, source_target_pairs={{0,1},{1,0},{2,3},{3,2},{4,5},{5,4},{6,7},{7,6},{8,9},{9,8},{10,11... | collective-permute-start | bytes 884744 | tf_op jit(solution)/shard_map/ppermute | solution.py:592
  54.3 1.7 %collective-permute-start.7 = (f32[16,8,128]{2,1,0:T(8,128)S(1)}, f32[16,8,128]{2,1,0:T(8,128)S(1)}, u32[]{:S(2)}, u32[]{:S(2)}) collective-permute-start(f32[16,8,128]{2,1,0:T(8,128)S(1)} %get-tuple-element.52), channel_id=1, source_target_pairs={{0,1},{1,0},{2,3},{3,2},{4,5},{5,4},{6,7},{7,6},{8,9},{9,8},{10,11... | collective-permute-start | bytes 196616 | tf_op jit(solution)/shard_map/ppermute | solution.py:592
  56.0 31.5 %copy-start.3 = (f32[8]{0:T(128)S(1)}, f32[8]{0:T(128)}, u32[]{:S(2)}) copy-start(f32[8]{0:T(128)} %pole_re.9) | copy-start | bytes 100
  56.0 31.5 %copy-start.5 = (f32[8]{0:T(128)S(1)}, f32[8]{0:T(128)}, u32[]{:S(2)}) copy-start(f32[8]{0:T(128)} %pole_im.9) | copy-start | bytes 100
  72.7 6.6 %collective-permute-start.18 = (f32[9,8,128]{2,1,0:T(8,128)S(1)}, f32[9,8,128]{2,1,0:T(8,128)S(1)}, u32[]{:S(2)}, u32[]{:S(2)}) collective-permute-start(f32[9,8,128]{2,1,0:T(8,128)S(1)} %get-tuple-element.63), channel_id=1, source_target_pairs={{0,12},{1,13},{2,14},{3,15},{4,8},{5,9},{6,10},{7,11},{8,4},{9,5},... | collective-permute-start | bytes 110600 | tf_op jit(solution)/shard_map/ppermute | solution.py:592
  74.4 5.2 %collective-permute-start.17 = (f32[9,8,128]{2,1,0:T(8,128)S(1)}, f32[9,8,128]{2,1,0:T(8,128)S(1)}, u32[]{:S(2)}, u32[]{:S(2)}) collective-permute-start(f32[9,8,128]{2,1,0:T(8,128)S(1)} %get-tuple-element.63), channel_id=1, source_target_pairs={{0,8},{1,9},{2,10},{3,11},{4,12},{5,13},{6,14},{7,15},{8,0},{9,1},... | collective-permute-start | bytes 110600 | tf_op jit(solution)/shard_map/ppermute | solution.py:592
  74.6 5.1 %collective-permute-start.16 = (f32[9,8,128]{2,1,0:T(8,128)S(1)}, f32[9,8,128]{2,1,0:T(8,128)S(1)}, u32[]{:S(2)}, u32[]{:S(2)}) collective-permute-start(f32[9,8,128]{2,1,0:T(8,128)S(1)} %get-tuple-element.63), channel_id=1, source_target_pairs={{0,4},{1,5},{2,6},{3,7},{4,0},{5,1},{6,2},{7,3},{8,12},{9,13},{10,... | collective-permute-start | bytes 110600 | tf_op jit(solution)/shard_map/ppermute | solution.py:592
  77.1 8.5 %collective-permute-start.15 = (f32[16,8,128]{2,1,0:T(8,128)S(1)}, f32[16,8,128]{2,1,0:T(8,128)S(1)}, u32[]{:S(2)}, u32[]{:S(2)}) collective-permute-start(f32[16,8,128]{2,1,0:T(8,128)S(1)} %get-tuple-element.62), channel_id=1, source_target_pairs={{0,15},{1,2},{2,1},{3,4},{4,3},{5,6},{6,5},{7,8},{8,7},{9,10},{10,... | collective-permute-start | bytes 196616 | tf_op jit(solution)/shard_map/ppermute | solution.py:599
  79.7 5.9 %collective-permute-start.19 = (f32[4,9,8,128]{3,2,1,0:T(8,128)S(1)}, f32[4,9,8,128]{3,2,1,0:T(8,128)S(1)}, u32[]{:S(2)}, u32[]{:S(2)}) collective-permute-start(f32[4,9,8,128]{3,2,1,0:T(8,128)S(1)} %pad_maximum_fusion.3), channel_id=1, source_target_pairs={{0,2},{1,3},{2,0},{3,1},{4,6},{5,7},{6,4},{7,5},{8,10},{9,11},{10,... | collective-permute-start | bytes 442376 | tf_op jit(solution)/shard_map/ppermute | solution.py:592
  85.7 1.7 %collective-permute-start.20 = (f32[8,9,8,128]{3,2,1,0:T(8,128)S(1)}, f32[8,9,8,128]{3,2,1,0:T(8,128)S(1)}, u32[]{:S(2)}, u32[]{:S(2)}) collective-permute-start(f32[8,9,8,128]{3,2,1,0:T(8,128)S(1)} %constant_dynamic-update-slice_fusion.5.near_side), channel_id=1, source_target_pairs={{0,1},{1,0},{2,3},{3,2},{4,5},{5,4},{6,7},{7,6},{8,9},{9,8},{10,11... | collective-permute-start | bytes 884744 | tf_op jit(solution)/shard_map/ppermute | solution.py:592
  85.7 1.7 %collective-permute-start.14 = (f32[16,8,128]{2,1,0:T(8,128)S(1)}, f32[16,8,128]{2,1,0:T(8,128)S(1)}, u32[]{:S(2)}, u32[]{:S(2)}) collective-permute-start(f32[16,8,128]{2,1,0:T(8,128)S(1)} %get-tuple-element.61), channel_id=1, source_target_pairs={{0,1},{1,0},{2,3},{3,2},{4,5},{5,4},{6,7},{7,6},{8,9},{9,8},{10,11... | collective-permute-start | bytes 196616 | tf_op jit(solution)/shard_map/ppermute | solution.py:592
  104.2 7.1 %collective-permute-start.25 = (f32[9,8,128]{2,1,0:T(8,128)S(1)}, f32[9,8,128]{2,1,0:T(8,128)S(1)}, u32[]{:S(2)}, u32[]{:S(2)}) collective-permute-start(f32[9,8,128]{2,1,0:T(8,128)S(1)} %get-tuple-element.75), channel_id=1, source_target_pairs={{0,12},{1,13},{2,14},{3,15},{4,8},{5,9},{6,10},{7,11},{8,4},{9,5},... | collective-permute-start | bytes 110600 | tf_op jit(solution)/shard_map/ppermute | solution.py:592
  106.4 4.9 %collective-permute-start.24 = (f32[9,8,128]{2,1,0:T(8,128)S(1)}, f32[9,8,128]{2,1,0:T(8,128)S(1)}, u32[]{:S(2)}, u32[]{:S(2)}) collective-permute-start(f32[9,8,128]{2,1,0:T(8,128)S(1)} %get-tuple-element.75), channel_id=1, source_target_pairs={{0,8},{1,9},{2,10},{3,11},{4,12},{5,13},{6,14},{7,15},{8,0},{9,1},... | collective-permute-start | bytes 110600 | tf_op jit(solution)/shard_map/ppermute | solution.py:592
  106.4 4.9 %collective-permute-start.23 = (f32[9,8,128]{2,1,0:T(8,128)S(1)}, f32[9,8,128]{2,1,0:T(8,128)S(1)}, u32[]{:S(2)}, u32[]{:S(2)}) collective-permute-start(f32[9,8,128]{2,1,0:T(8,128)S(1)} %get-tuple-element.75), channel_id=1, source_target_pairs={{0,4},{1,5},{2,6},{3,7},{4,0},{5,1},{6,2},{7,3},{8,12},{9,13},{10,... | collective-permute-start | bytes 110600 | tf_op jit(solution)/shard_map/ppermute | solution.py:592
  108.7 8.7 %collective-permute-start.22 = (f32[16,8,128]{2,1,0:T(8,128)S(1)}, f32[16,8,128]{2,1,0:T(8,128)S(1)}, u32[]{:S(2)}, u32[]{:S(2)}) collective-permute-start(f32[16,8,128]{2,1,0:T(8,128)S(1)} %get-tuple-element.74), channel_id=1, source_target_pairs={{0,15},{1,2},{2,1},{3,4},{4,3},{5,6},{6,5},{7,8},{8,7},{9,10},{10,... | collective-permute-start | bytes 196616 | tf_op jit(solution)/shard_map/ppermute | solution.py:599
  111.4 5.9 %collective-permute-start.26 = (f32[4,9,8,128]{3,2,1,0:T(8,128)S(1)}, f32[4,9,8,128]{3,2,1,0:T(8,128)S(1)}, u32[]{:S(2)}, u32[]{:S(2)}) collective-permute-start(f32[4,9,8,128]{3,2,1,0:T(8,128)S(1)} %pad_maximum_fusion.4), channel_id=1, source_target_pairs={{0,2},{1,3},{2,0},{3,1},{4,6},{5,7},{6,4},{7,5},{8,10},{9,11},{10,... | collective-permute-start | bytes 442376 | tf_op jit(solution)/shard_map/ppermute | solution.py:592
  117.3 1.7 %collective-permute-start.27 = (f32[8,9,8,128]{3,2,1,0:T(8,128)S(1)}, f32[8,9,8,128]{3,2,1,0:T(8,128)S(1)}, u32[]{:S(2)}, u32[]{:S(2)}) collective-permute-start(f32[8,9,8,128]{3,2,1,0:T(8,128)S(1)} %constant_dynamic-update-slice_fusion.10.near_side), channel_id=1, source_target_pairs={{0,1},{1,0},{2,3},{3,2},{4,5},{5,4},{6,7},{7,6},{8,9},{9,8},{10,11... | collective-permute-start | bytes 884744 | tf_op jit(solution)/shard_map/ppermute | solution.py:592
  117.4 1.7 %collective-permute-start.21 = (f32[16,8,128]{2,1,0:T(8,128)S(1)}, f32[16,8,128]{2,1,0:T(8,128)S(1)}, u32[]{:S(2)}, u32[]{:S(2)}) collective-permute-start(f32[16,8,128]{2,1,0:T(8,128)S(1)} %get-tuple-element.73), channel_id=1, source_target_pairs={{0,1},{1,0},{2,3},{3,2},{4,5},{5,4},{6,7},{7,6},{8,9},{9,8},{10,11... | collective-permute-start | bytes 196616 | tf_op jit(solution)/shard_map/ppermute | solution.py:592
  135.6 5.5 %collective-permute-start.30 = (f32[1,8,128]{2,1,0:T(8,128)S(1)}, f32[1,8,128]{2,1,0:T(8,128)S(1)}, u32[]{:S(2)}, u32[]{:S(2)}) collective-permute-start(f32[1,8,128]{2,1,0:T(8,128)S(1)} %get-tuple-element.78), channel_id=1, source_target_pairs={{0,12},{1,13},{2,14},{3,15},{4,8},{5,9},{6,10},{7,11},{8,4},{9,5},... | collective-permute-start | bytes 12296 | tf_op jit(solution)/shard_map/ppermute | solution.py:592
  137.6 4.5 %collective-permute-start.29 = (f32[1,8,128]{2,1,0:T(8,128)S(1)}, f32[1,8,128]{2,1,0:T(8,128)S(1)}, u32[]{:S(2)}, u32[]{:S(2)}) collective-permute-start(f32[1,8,128]{2,1,0:T(8,128)S(1)} %get-tuple-element.78), channel_id=1, source_target_pairs={{0,8},{1,9},{2,10},{3,11},{4,12},{5,13},{6,14},{7,15},{8,0},{9,1},... | collective-permute-start | bytes 12296 | tf_op jit(solution)/shard_map/ppermute | solution.py:592
  137.7 4.4 %collective-permute-start.28 = (f32[1,8,128]{2,1,0:T(8,128)S(1)}, f32[1,8,128]{2,1,0:T(8,128)S(1)}, u32[]{:S(2)}, u32[]{:S(2)}) collective-permute-start(f32[1,8,128]{2,1,0:T(8,128)S(1)} %get-tuple-element.78), channel_id=1, source_target_pairs={{0,4},{1,5},{2,6},{3,7},{4,0},{5,1},{6,2},{7,3},{8,12},{9,13},{10,... | collective-permute-start | bytes 12296 | tf_op jit(solution)/shard_map/ppermute | solution.py:592
  142.1 3.7 %collective-permute-start.31 = (f32[4,1,8,128]{3,2,1,0:T(8,128)S(1)}, f32[4,1,8,128]{3,2,1,0:T(8,128)S(1)}, u32[]{:S(2)}, u32[]{:S(2)}) collective-permute-start(f32[4,1,8,128]{3,2,1,0:T(8,128)S(1)} %pad_maximum_fusion.5), channel_id=1, source_target_pairs={{0,2},{1,3},{2,0},{3,1},{4,6},{5,7},{6,4},{7,5},{8,10},{9,11},{10,... | collective-permute-start | bytes 49160 | tf_op jit(solution)/shard_map/ppermute | solution.py:592
  145.8 1.2 collective-permute-start.32

commit v3 on v2

--- a/solution.py
+++ b/solution.py
@@ -108,6 +108,10 @@
         return carry
 
     lax.fori_loop(0, count // step, run, 0)
+
+
+def sum_step(blocks):
+    return min(4 * TILE, blocks)
 
 
 def sum_rows(count, step, body, terms, poles):
@@ -235,8 +239,8 @@
     for first, slot in ((0, 2), (blocks - NYB, 1)):
 
         def step(group, carry, first=first, slot=slot):
-            for index in range(4):
-                pair = first // 2 + 4 * group + index
+            for index in range(8):
+                pair = first // 2 + 8 * group + index
                 for q in range(2):
                     b = 2 * pair + q
                     pieces = [
@@ -247,7 +251,7 @@
                     image[b] = image[b] + combine(z, product)
             return carry
 
-        lax.fori_loop(0, NYB // 8, step, 0)
+        lax.fori_loop(0, NYB // 16, step, 0)
 
 
 def contact_part(spots, wide, sigma, mats, sem, acc, image):
@@ -409,10 +413,10 @@
     contact_part(spots, wide, sigma, mats, sems[2], acc, image)
 
     def terms(s):
-        b, v = own[pl.ds(s, 2 * TILE)], image[pl.ds(s, 2 * TILE)]
+        b, v = own[pl.ds(s, sum_step(blocks))], image[pl.ds(s, sum_step(blocks))]
         return (b * b, *inner_terms(b, v), v * v)
 
-    bb, bv_re, bv_im, vv = sum_rows(blocks, 2 * TILE, terms, 4, poles)
+    bb, bv_re, bv_im, vv = sum_rows(blocks, sum_step(blocks), terms, 4, poles)
     store_chunk(
         chunk, edge_a, edge_b, me_ref[0], spots, image, pack_columns([lane_sum(bb), *inner_pair(bv_re, bv_im), lane_sum(vv)])
     )
@@ -445,12 +449,12 @@
     apply_operator(near, spots, z, wide, ham, ovl, sigma, mats, sems, acc, turned)
 
     def terms(s):
-        b = rhs_ext[pl.ds(NYB + s, 2 * TILE)]
-        h = half_ext[pl.ds(NYB + s, 2 * TILE)]
-        t = turned[pl.ds(s, 2 * TILE)]
+        b = rhs_ext[pl.ds(NYB + s, sum_step(blocks))]
+        h = half_ext[pl.ds(NYB + s, sum_step(blocks))]
+        t = turned[pl.ds(s, sum_step(blocks))]
         return (*inner_terms(t, h), t * t, h * h, *inner_terms(b, h), *inner_terms(b, t))
 
-    th_re, th_im, tt, hh, bh_re, bh_im, bt_re, bt_im = sum_rows(blocks, 2 * TILE, terms, 8, poles)
+    th_re, th_im, tt, hh, bh_re, bh_im, bt_re, bt_im = sum_rows(blocks, sum_step(blocks), terms, 8, poles)
     columns = [
         *inner_pair(th_re, th_im), lane_sum(tt), lane_sum(hh),
         *inner_pair(bh_re, bh_im), *inner_pair(bt_re, bt_im),
@@ -513,10 +517,10 @@
     apply_operator(near, spots, z, wide, ham, ovl, sigma, mats, sems, acc, image)
 
     def terms(s):
-        b, v = rhs_ext[pl.ds(NYB + s, 2 * TILE)], image[pl.ds(s, 2 * TILE)]
+        b, v = rhs_ext[pl.ds(NYB + s, sum_step(blocks))], image[pl.ds(s, sum_step(blocks))]
         return (*inner_terms(b, v), v * v)
 
-    bv_re, bv_im, vv = sum_rows(blocks, 2 * TILE, terms, 3, poles)
+    bv_re, bv_im, vv = sum_rows(blocks, sum_step(blocks), terms, 3, poles)
     store_chunk(chunk, edge_a, edge_b, me_ref[0], spots, image, pack_columns([*inner_pair(bv_re, bv_im), lane_sum(vv)]))
 
 
@@ -557,10 +561,10 @@
     apply_operator(near, spots, z, wide, ham, ovl, sigma, mats, sems, acc, turned)
 
     def terms(s):
-        h, t = half_own[pl.ds(s, 2 * TILE)], turned[pl.ds(s, 2 * TILE)]
+        h, t = half_own[pl.ds(s, sum_step(blocks))], turned[pl.ds(s, sum_step(blocks))]
         return (*inner_terms(t, h), t * t)
 
-    th_re, th_im, tt = sum_rows(blocks, 2 * TILE, terms, 3, poles)
+    th_re, th_im, tt = sum_rows(blocks, sum_step(blocks), terms, 3, poles)
     sums_out[0] = pack_columns([*inner_pair(th_re, th_im), lane_sum(tt)])
 
 

time: 149 us -> 148 us (level)
  no operation moved by 1% of the time
where the time goes in v3:
time: 148 us
  Pallas kernels  73.1 us (49%)
  starting transfers between devices  43.6 us (29%)
  waiting for transfers between devices  24.9 us (17%)
  local copies, waits for them, and re-layouts  4.46 us (3%)
    pallas_call x4, Pallas kernels, call(): pl.pallas_call(kernel, in_specs=[SMEM] * 5 + [VMEM] * (len(inputs) - 5) +...  60.1 us
    ppermute x29, starting transfers between devices, flip(): return lax.ppermute(value, 'gx', [(i, i ^ mask) for i in range(count)])  35.6 us
    ppermute x29, waiting for transfers between devices, flip(): return lax.ppermute(value, 'gx', [(i, i ^ mask) for i in range(count)])  24.9 us
    pallas_call x1, Pallas kernels, own_part(): pl.pallas_call(functools.partial(own_kernel, 0), in_specs=[SMEM] * 3 + [V...  10.5 us
    ppermute x4, starting transfers between devices, exchange(): far = (lax.ppermute(edges[1], 'gx', other),)  8.09 us
    unnamed x32, local copies, waits for them, and re-layouts  4.11 us
  transfers between devices with their start and end apart: 33, of which 15 were waited for; matrix products, arithmetic and copies ran while one was open for 1% of the time, Pallas kernels for 7%

profile of v3, /device:TPU:0, one launch (start us, length us, event | category | flops | bytes accessed | tf_op | source)
XLA Modules:
  0.0 147.7 jit_solution(12489563915083373283)
XLA Ops:
  0.6 0.0 copy-start
  0.6 1.0 copy-done
  1.7 0.7 copy-done.6
  2.3 0.9 prepare.1
  3.2 5.1 %collective-permute-start.3 = (f32[9,8,128]{2,1,0:T(8,128)S(1)}, f32[9,8,128]{2,1,0:T(8,128)S(1)}, u32[]{:S(2)}, u32[]{:S(2)}) collective-permute-start(f32[9,8,128]{2,1,0:T(8,128)S(1)} %get-tuple-element.43), channel_id=1, source_target_pairs={{0,12},{1,13},{2,14},{3,15},{4,8},{5,9},{6,10},{7,11},{8,4},{9,5},... | collective-permute-start | bytes 110600 | tf_op jit(solution)/shard_map/ppermute | solution.py:596
  8.3 0.0 collective-permute-start.2
  8.3 0.6 collective-permute-start.1
  9.0 0.7 add_select_fusion
  9.7 0.1 copy.10
  9.8 0.2 reshape.17.near
  10.0 0.3 collective-permute-done.3
  10.3 2.9 %collective-permute-done.2 = f32[9,8,128]{2,1,0:T(8,128)S(1)} collective-permute-done((f32[9,8,128]{2,1,0:T(8,128)S(1)}, f32[9,8,128]{2,1,0:T(8,128)S(1)}, u32[]{:S(2)}, u32[]{:S(2)}) %collective-permute-start.2) | collective-permute-done | bytes 36896 | tf_op jit(solution)/shard_map/ppermute | solution.py:596
  13.2 1.6 %collective-permute-start.4 = (f32[4,9,8,128]{3,2,1,0:T(8,128)S(1)}, f32[4,9,8,128]{3,2,1,0:T(8,128)S(1)}, u32[]{:S(2)}, u32[]{:S(2)}) collective-permute-start(f32[4,9,8,128]{3,2,1,0:T(8,128)S(1)} %pad_maximum_fusion.1), channel_id=1, source_target_pairs={{0,2},{1,3},{2,0},{3,1},{4,6},{5,7},{6,4},{7,5},{8,10},{9,11},{10,... | collective-permute-start | bytes 442376 | tf_op jit(solution)/shard_map/ppermute | solution.py:596
  14.8 0.0 collective-permute-start
  14.8 1.0 copy-done.1
  15.9 0.7 copy-done.2
  16.5 0.7 copy-done.4
  17.2 10.5 %own.3.image_in = f32[128,8,128]{2,1,0:T(8,128)S(1)} custom-call(s32[640]{0:T(1024)S(1)} %reshape.17.near, f32[8]{0:T(128)S(1)} %copy-done.2, f32[8]{0:T(128)S(1)} %copy-done.4, f32[128,8,128]{2,1,0:T(8,128)S(1)} %copy-done.1, bf16[320,128,128]{2,1,0:T(8,128)(2,1)} %bitcast.44, bf16[320,128,128]{2,1,0:T(8,128)(2,1)} %bitcast.49), custom_call_target="tpu_custom_call" | custom-call | flops 335544320 | bytes 20971520 | tf_op jit(solution)/shard_map/own/pallas_call | solution.py:653
  27.7 0.7 collective-permute-start.6
  28.4 0.1 collective-permute-start.5
  28.5 1.2 collective-permute-done.5.partner
  29.7 10.5 %first.1 = (f32[288,8,128]{2,1,0:T(8,128)S(1)}, f32[128,8,128]{2,1,0:T(8,128)S(1)}, f32[9,8,128]{2,1,0:T(8,128)S(1)}, f32[16,8,128]{2,1,0:T(8,128)S(1)}, f32[16,8,128]{2,1,0:T(8,128)S(1)}) custom-call(s32[1]{0:T(128)} %bitcast.me_ref, s32[640]{0:T(1024)S(1)} %reshape.17.near, s32[8]{0:T(128)S(1)} %copy-done.7, f32[8]{0:T(128)S(1)} %copy-done.2, ...), custom_call_target="tpu_custom_call" | custom-call | tf_op jit(solution)/shard_map/first/pallas_call | solution.py:633
  40.2 1.5 %collective-permute-start.11 = (f32[9,8,128]{2,1,0:T(8,128)S(1)}, f32[9,8,128]{2,1,0:T(8,128)S(1)}, u32[]{:S(2)}, u32[]{:S(2)}) collective-permute-start(f32[9,8,128]{2,1,0:T(8,128)S(1)} %get-tuple-element.54), channel_id=1, source_target_pairs={{0,12},{1,13},{2,14},{3,15},{4,8},{5,9},{6,10},{7,11},{8,4},{9,5},... | collective-permute-start | bytes 110600 | tf_op jit(solution)/shard_map/ppermute | solution.py:596
  41.7 0.6 collective-permute-start.10
  42.4 2.3 %collective-permute-start.9 = (f32[9,8,128]{2,1,0:T(8,128)S(1)}, f32[9,8,128]{2,1,0:T(8,128)S(1)}, u32[]{:S(2)}, u32[]{:S(2)}) collective-permute-start(f32[9,8,128]{2,1,0:T(8,128)S(1)} %get-tuple-element.54), channel_id=1, source_target_pairs={{0,4},{1,5},{2,6},{3,7},{4,0},{5,1},{6,2},{7,3},{8,12},{9,13},{10,... | collective-permute-start | bytes 110600 | tf_op jit(solution)/shard_map/ppermute | solution.py:596
  44.7 3.3 %collective-permute-start.8 = (f32[16,8,128]{2,1,0:T(8,128)S(1)}, f32[16,8,128]{2,1,0:T(8,128)S(1)}, u32[]{:S(2)}, u32[]{:S(2)}) collective-permute-start(f32[16,8,128]{2,1,0:T(8,128)S(1)} %get-tuple-element.53), channel_id=1, source_target_pairs={{0,15},{1,2},{2,1},{3,4},{4,3},{5,6},{6,5},{7,8},{8,7},{9,10},{10,... | collective-permute-start | bytes 196616 | tf_op jit(solution)/shard_map/ppermute | solution.py:603
  48.0 2.0 %collective-permute-start.12 = (f32[4,9,8,128]{3,2,1,0:T(8,128)S(1)}, f32[4,9,8,128]{3,2,1,0:T(8,128)S(1)}, u32[]{:S(2)}, u32[]{:S(2)}) collective-permute-start(f32[4,9,8,128]{3,2,1,0:T(8,128)S(1)} %pad_maximum_fusion.2), channel_id=1, source_target_pairs={{0,2},{1,3},{2,0},{3,1},{4,6},{5,7},{6,4},{7,5},{8,10},{9,11},{10,... | collective-permute-start | bytes 442376 | tf_op jit(solution)/shard_map/ppermute | solution.py:596
  50.0 3.7 %collective-permute-done.12 = f32[4,9,8,128]{3,2,1,0:T(8,128)S(1)} collective-permute-done((f32[4,9,8,128]{3,2,1,0:T(8,128)S(1)}, f32[4,9,8,128]{3,2,1,0:T(8,128)S(1)}, u32[]{:S(2)}, u32[]{:S(2)}) %collective-permute-start.12) | collective-permute-done | bytes 147488 | tf_op jit(solution)/shard_map/ppermute | solution.py:596
  53.8 0.1 collective-permute-start.13
  53.8 0.5 collective-permute-start.7
  54.3 1.2 collective-permute-done.7.partner
  55.5 16.6 %second.1 = (f32[288,8,128]{2,1,0:T(8,128)S(1)}, f32[288,8,128]{2,1,0:T(8,128)S(1)}, f32[128,8,128]{2,1,0:T(8,128)S(1)}, f32[9,8,128]{2,1,0:T(8,128)S(1)}, f32[1...) custom-call(s32[1]{0:T(128)} %bitcast.me_ref, s32[640]{0:T(1024)S(1)} %reshape.17.near, ...), custom_call_target="tpu_custom_call" | custom-call | tf_op jit(solution)/shard_map/second/pallas_call | solution.py:633
  72.1 1.7 %collective-permute-start.18 = (f32[9,8,128]{2,1,0:T(8,128)S(1)}, f32[9,8,128]{2,1,0:T(8,128)S(1)}, u32[]{:S(2)}, u32[]{:S(2)}) collective-permute-start(f32[9,8,128]{2,1,0:T(8,128)S(1)} %get-tuple-element.63), channel_id=1, source_target_pairs={{0,12},{1,13},{2,14},{3,15},{4,8},{5,9},{6,10},{7,11},{8,4},{9,5},... | collective-permute-start | bytes 110600 | tf_op jit(solution)/shard_map/ppermute | solution.py:596
  73.9 0.2 collective-permute-start.17
  74.1 2.5 %collective-permute-start.16 = (f32[9,8,128]{2,1,0:T(8,128)S(1)}, f32[9,8,128]{2,1,0:T(8,128)S(1)}, u32[]{:S(2)}, u32[]{:S(2)}) collective-permute-start(f32[9,8,128]{2,1,0:T(8,128)S(1)} %get-tuple-element.63), channel_id=1, source_target_pairs={{0,4},{1,5},{2,6},{3,7},{4,0},{5,1},{6,2},{7,3},{8,12},{9,13},{10,... | collective-permute-start | bytes 110600 | tf_op jit(solution)/shard_map/ppermute | solution.py:596
  76.6 2.1 %collective-permute-start.15 = (f32[16,8,128]{2,1,0:T(8,128)S(1)}, f32[16,8,128]{2,1,0:T(8,128)S(1)}, u32[]{:S(2)}, u32[]{:S(2)}) collective-permute-start(f32[16,8,128]{2,1,0:T(8,128)S(1)} %get-tuple-element.62), channel_id=1, source_target_pairs={{0,15},{1,2},{2,1},{3,4},{4,3},{5,6},{6,5},{7,8},{8,7},{9,10},{10,... | collective-permute-start | bytes 196616 | tf_op jit(solution)/shard_map/ppermute | solution.py:603
  78.7 0.4 collective-permute-done.17
  79.1 0.1 collective-permute-done.16
  79.2 2.1 %collective-permute-start.19 = (f32[4,9,8,128]{3,2,1,0:T(8,128)S(1)}, f32[4,9,8,128]{3,2,1,0:T(8,128)S(1)}, u32[]{:S(2)}, u32[]{:S(2)}) collective-permute-start(f32[4,9,8,128]{3,2,1,0:T(8,128)S(1)} %pad_maximum_fusion.3), channel_id=1, source_target_pairs={{0,2},{1,3},{2,0},{3,1},{4,6},{5,7},{6,4},{7,5},{8,10},{9,11},{10,... | collective-permute-start | bytes 442376 | tf_op jit(solution)/shard_map/ppermute | solution.py:596
  81.4 3.7 %collective-permute-done.19 = f32[4,9,8,128]{3,2,1,0:T(8,128)S(1)} collective-permute-done((f32[4,9,8,128]{3,2,1,0:T(8,128)S(1)}, f32[4,9,8,128]{3,2,1,0:T(8,128)S(1)}, u32[]{:S(2)}, u32[]{:S(2)}) %collective-permute-start.19) | collective-permute-done | bytes 147488 | tf_op jit(solution)/shard_map/ppermute | solution.py:596
  85.1 0.1 collective-permute-start.20
  85.2 0.5 collective-permute-start.14
  85.7 1.2 collective-permute-done.14.partner
  86.9 16.6 %third.1 = (f32[128,8,128]{2,1,0:T(8,128)S(1)}, f32[128,8,128]{2,1,0:T(8,128)S(1)}, f32[160,8,128]{2,1,0:T(8,128)S(1)}, f32[160,8,128]{2,1,0:T(8,128)S(1)}, f32[...) custom-call(s32[1]{0:T(128)} %bitcast.me_ref, ...), custom_call_target="tpu_custom_call" | custom-call | tf_op jit(solution)/shard_map/third/pallas_call | solution.py:633
  103.5 2.2 %collective-permute-start.25 = (f32[9,8,128]{2,1,0:T(8,128)S(1)}, f32[9,8,128]{2,1,0:T(8,128)S(1)}, u32[]{:S(2)}, u32[]{:S(2)}) collective-permute-start(f32[9,8,128]{2,1,0:T(8,128)S(1)} %get-tuple-element.75), channel_id=1, source_target_pairs={{0,12},{1,13},{2,14},{3,15},{4,8},{5,9},{6,10},{7,11},{8,4},{9,5},... | collective-permute-start | bytes 110600 | tf_op jit(solution)/shard_map/ppermute | solution.py:596
  105.7 0.0 collective-permute-start.24
  105.7 2.3 %collective-permute-start.23 = (f32[9,8,128]{2,1,0:T(8,128)S(1)}, f32[9,8,128]{2,1,0:T(8,128)S(1)}, u32[]{:S(2)}, u32[]{:S(2)}) collective-permute-start(f32[9,8,128]{2,1,0:T(8,128)S(1)} %get-tuple-element.75), channel_id=1, source_target_pairs={{0,4},{1,5},{2,6},{3,7},{4,0},{5,1},{6,2},{7,3},{8,12},{9,13},{10,... | collective-permute-start | bytes 110600 | tf_op jit(solution)/shard_map/ppermute | solution.py:596
  108.0 2.6 %collective-permute-start.22 = (f32[16,8,128]{2,1,0:T(8,128)S(1)}, f32[16,8,128]{2,1,0:T(8,128)S(1)}, u32[]{:S(2)}, u32[]{:S(2)}) collective-permute-start(f32[16,8,128]{2,1,0:T(8,128)S(1)} %get-tuple-element.74), channel_id=1, source_target_pairs={{0,15},{1,2},{2,1},{3,4},{4,3},{5,6},{6,5},{7,8},{8,7},{9,10},{10,... | collective-permute-start | bytes 196616 | tf_op jit(solution)/shard_map/ppermute | solution.py:603
  110.6 0.0 collective-permute-done.23
  110.7 2.2 %collective-permute-start.26 = (f32[4,9,8,128]{3,2,1,0:T(8,128)S(1)}, f32[4,9,8,128]{3,2,1,0:T(8,128)S(1)}, u32[]{:S(2)}, u32[]{:S(2)}) collective-permute-start(f32[4,9,8,128]{3,2,1,0:T(8,128)S(1)} %pad_maximum_fusion.4), channel_id=1, source_target_pairs={{0,2},{1,3},{2,0},{3,1},{4,6},{5,7},{6,4},{7,5},{8,10},{9,11},{10,... | collective-permute-start | bytes 442376 | tf_op jit(solution)/shard_map/ppermute | solution.py:596
  112.9 3.7 %collective-permute-done.26 = f32[4,9,8,128]{3,2,1,0:T(8,128)S(1)} collective-permute-done((f32[4,9,8,128]{3,2,1,0:T(8,128)S(1)}, f32[4,9,8,128]{3,2,1,0:T(8,128)S(1)}, u32[]{:S(2)}, u32[]{:S(2)}) %collective-permute-start.26) | collective-permute-done | bytes 147488 | tf_op jit(solution)/shard_map/ppermute | solution.py:596
  116.6 0.1 collective-permute-start.27
  116.7 0.5 collective-permute-start.21
  117.2 1.2 collective-permute-done.21.partner
  118.3 16.4 %fourth.1 = (f32[128,8,128]{2,1,0:T(8,128)S(1)}, f32[128,8,128]{2,1,0:T(8,128)S(1)}, f32[128,8,128]{2,1,0:T(8,128)S(1)}, f32[1,8,128]{2,1,0:T(8,128)S(1)}) custom-call(s32[1]{0:T(128)} %bitcast.me_ref, s32[640]{0:T(1024)S(1)} %reshape.17.near, s32[8]{0:T(128)S(1)} %copy-done.7, f32[8]{0:T(128)S(1)} %copy-done.3, f32[8]{0:T(128)S(1)} %copy-done.5, ...), custom_call_target="tpu_custom_call" | custom-call | tf_op jit(solution)/shard_map/fourth/pallas_call | solution.py:633
  134.8 1.9 %collective-permute-start.30 = (f32[1,8,128]{2,1,0:T(8,128)S(1)}, f32[1,8,128]{2,1,0:T(8,128)S(1)}, u32[]{:S(2)}, u32[]{:S(2)}) collective-permute-start(f32[1,8,128]{2,1,0:T(8,128)S(1)} %get-tuple-element.78), channel_id=1, source_target_pairs={{0,12},{1,13},{2,14},{3,15},{4,8},{5,9},{6,10},{7,11},{8,4},{9,5},... | collective-permute-start | bytes 12296 | tf_op jit(solution)/shard_map/ppermute | solution.py:596
  136.7 0.2 collective-permute-start.29
  136.9 2.3 %collective-permute-start.28 = (f32[1,8,128]{2,1,0:T(8,128)S(1)}, f32[1,8,128]{2,1,0:T(8,128)S(1)}, u32[]{:S(2)}, u32[]{:S(2)}) collective-permute-start(f32[1,8,128]{2,1,0:T(8,128)S(1)} %get-tuple-element.78), channel_id=1, source_target_pairs={{0,4},{1,5},{2,6},{3,7},{4,0},{5,1},{6,2},{7,3},{8,12},{9,13},{10,... | collective-permute-start | bytes 12296 | tf_op jit(solution)/shard_map/ppermute | solution.py:596
  139.2 1.0 collective-permute-done.30
  140.3 1.0 collective-permute-done.29
  141.2 1.7 %collective-permute-start.31 = (f32[4,1,8,128]{3,2,1,0:T(8,128)S(1)}, f32[4,1,8,128]{3,2,1,0:T(8,128)S(1)}, u32[]{:S(2)}, u32[]{:S(2)}) collective-permute-start(f32[4,1,8,128]{3,2,1,0:T(8,128)S(1)} %pad_maximum_fusion.5), channel_id=1, source_target_pairs={{0,2},{1,3},{2,0},{3,1},{4,6},{5,7},{6,4},{7,5},{8,10},{9,11},{10,... | collective-permute-start | bytes 49160 | tf_op jit(solution)/shard_map/ppermute | solution.py:596
  142.9 2.1 %collective-permute-done.31 = f32[4,1,8,128]{3,2,1,0:T(8,128)S(1)} collective-permute-done((f32[4,1,8,128]{3,2,1,0:T(8,128)S(1)}, f32[4,1,8,128]{3,2,1,0:T(8,128)S(1)}, u32[]{:S(2)}, u32[]{:S(2)}) %collective-permute-start.31) | collective-permute-done | bytes 16416 | tf_op jit(solution)/shard_map/ppermute | solution.py:596
  145.0 1.2 collective-permute-done.32.far_side
  146.2 1.6 %last.1 = (f32[128,8,128]{2,1,0:T(8,128)}, f32[128,8,128]{2,1,0:T(8,128)}) custom-call(f32[8,1,8,128]{3,2,1,0:T(8,128)S(1)} %constant_dynamic-update-slice_fusion.15.near_side, f32[8,1,8,128]{3,2,1,0:T(8,128)S(1)} %collective-permute-done.32.far_side, f32[128,8,128]{2,1,0:T(8,128)S(1)} %get-tuple-element.79.half_own, ...), custom_call_target="tpu_custom_call" | custom-call | tf_op jit(solution)/shard_map/last/pallas_call | solution.py:686
  (54 shorter events, 0.2 us)
Async XLA Ops:
  0.6 1.0 copy-start
  1.7 0.7 copy-start.6
  3.2 7.1 %collective-permute-start.3 = (f32[9,8,128]{2,1,0:T(8,128)S(1)}, f32[9,8,128]{2,1,0:T(8,128)S(1)}, u32[]{:S(2)}, u32[]{:S(2)}) collective-permute-start(f32[9,8,128]{2,1,0:T(8,128)S(1)} %get-tuple-element.43), channel_id=1, source_target_pairs={{0,12},{1,13},{2,14},{3,15},{4,8},{5,9},{6,10},{7,11},{8,4},{9,5},... | collective-permute-start | bytes 110600 | tf_op jit(solution)/shard_map/ppermute | solution.py:596
  8.3 4.9 %collective-permute-start.2 = (f32[9,8,128]{2,1,0:T(8,128)S(1)}, f32[9,8,128]{2,1,0:T(8,128)S(1)}, u32[]{:S(2)}, u32[]{:S(2)}) collective-permute-start(f32[9,8,128]{2,1,0:T(8,128)S(1)} %get-tuple-element.43), channel_id=1, source_target_pairs={{0,8},{1,9},{2,10},{3,11},{4,12},{5,13},{6,14},{7,15},{8,0},{9,1},... | collective-permute-start | bytes 110600 | tf_op jit(solution)/shard_map/ppermute | solution.py:596
  8.3 4.9 %collective-permute-start.1 = (f32[9,8,128]{2,1,0:T(8,128)S(1)}, f32[9,8,128]{2,1,0:T(8,128)S(1)}, u32[]{:S(2)}, u32[]{:S(2)}) collective-permute-start(f32[9,8,128]{2,1,0:T(8,128)S(1)} %get-tuple-element.43), channel_id=1, source_target_pairs={{0,4},{1,5},{2,6},{3,7},{4,0},{5,1},{6,2},{7,3},{8,12},{9,13},{10,... | collective-permute-start | bytes 110600 | tf_op jit(solution)/shard_map/ppermute | solution.py:596
  13.2 14.5 %collective-permute-start.4 = (f32[4,9,8,128]{3,2,1,0:T(8,128)S(1)}, f32[4,9,8,128]{3,2,1,0:T(8,128)S(1)}, u32[]{:S(2)}, u32[]{:S(2)}) collective-permute-start(f32[4,9,8,128]{3,2,1,0:T(8,128)S(1)} %pad_maximum_fusion.1), channel_id=1, source_target_pairs={{0,2},{1,3},{2,0},{3,1},{4,6},{5,7},{6,4},{7,5},{8,10},{9,11},{10,... | collective-permute-start | bytes 442376 | tf_op jit(solution)/shard_map/ppermute | solution.py:596
  14.8 12.9 %collective-permute-start = (f32[16,8,128]{2,1,0:T(8,128)S(1)}, f32[16,8,128]{2,1,0:T(8,128)S(1)}, u32[]{:S(2)}, u32[]{:S(2)}) collective-permute-start(f32[16,8,128]{2,1,0:T(8,128)S(1)} %get-tuple-element.42), channel_id=1, source_target_pairs={{0,15},{1,2},{2,1},{3,4},{4,3},{5,6},{6,5},{7,8},{8,7},{9,10},{10,... | collective-permute-start | bytes 196616 | tf_op jit(solution)/shard_map/ppermute | solution.py:603
  14.8 1.0 copy-start.1
  15.9 0.7 copy-start.2
  16.5 0.7 copy-start.4
  17.2 12.6 %copy-start.7 = (s32[8]{0:T(128)S(1)}, s32[8]{0:T(128)}, u32[]{:S(2)}) copy-start(s32[8]{0:T(128)} %contact.9) | copy-start | bytes 100
  27.7 2.0 %collective-permute-start.6 = (f32[8,9,8,128]{3,2,1,0:T(8,128)S(1)}, f32[8,9,8,128]{3,2,1,0:T(8,128)S(1)}, u32[]{:S(2)}, u32[]{:S(2)}) collective-permute-start(f32[8,9,8,128]{3,2,1,0:T(8,128)S(1)} %pad_maximum_fusion.near_side), channel_id=1, source_target_pairs={{0,1},{1,0},{2,3},{3,2},{4,5},{5,4},{6,7},{7,6},{8,9},{9,8},{10,11... | collective-permute-start | bytes 884744 | tf_op jit(solution)/shard_map/ppermute | solution.py:596
  28.4 1.3 collective-permute-start.5
  40.2 7.8 %collective-permute-start.11 = (f32[9,8,128]{2,1,0:T(8,128)S(1)}, f32[9,8,128]{2,1,0:T(8,128)S(1)}, u32[]{:S(2)}, u32[]{:S(2)}) collective-permute-start(f32[9,8,128]{2,1,0:T(8,128)S(1)} %get-tuple-element.54), channel_id=1, source_target_pairs={{0,12},{1,13},{2,14},{3,15},{4,8},{5,9},{6,10},{7,11},{8,4},{9,5},... | collective-permute-start | bytes 110600 | tf_op jit(solution)/shard_map/ppermute | solution.py:596
  41.7 6.3 %collective-permute-start.10 = (f32[9,8,128]{2,1,0:T(8,128)S(1)}, f32[9,8,128]{2,1,0:T(8,128)S(1)}, u32[]{:S(2)}, u32[]{:S(2)}) collective-permute-start(f32[9,8,128]{2,1,0:T(8,128)S(1)} %get-tuple-element.54), channel_id=1, source_target_pairs={{0,8},{1,9},{2,10},{3,11},{4,12},{5,13},{6,14},{7,15},{8,0},{9,1},... | collective-permute-start | bytes 110600 | tf_op jit(solution)/shard_map/ppermute | solution.py:596
  42.4 5.6 %collective-permute-start.9 = (f32[9,8,128]{2,1,0:T(8,128)S(1)}, f32[9,8,128]{2,1,0:T(8,128)S(1)}, u32[]{:S(2)}, u32[]{:S(2)}) collective-permute-start(f32[9,8,128]{2,1,0:T(8,128)S(1)} %get-tuple-element.54), channel_id=1, source_target_pairs={{0,4},{1,5},{2,6},{3,7},{4,0},{5,1},{6,2},{7,3},{8,12},{9,13},{10,... | collective-permute-start | bytes 110600 | tf_op jit(solution)/shard_map/ppermute | solution.py:596
  44.7 9.1 %collective-permute-start.8 = (f32[16,8,128]{2,1,0:T(8,128)S(1)}, f32[16,8,128]{2,1,0:T(8,128)S(1)}, u32[]{:S(2)}, u32[]{:S(2)}) collective-permute-start(f32[16,8,128]{2,1,0:T(8,128)S(1)} %get-tuple-element.53), channel_id=1, source_target_pairs={{0,15},{1,2},{2,1},{3,4},{4,3},{5,6},{6,5},{7,8},{8,7},{9,10},{10,... | collective-permute-start | bytes 196616 | tf_op jit(solution)/shard_map/ppermute | solution.py:603
  48.0 5.7 %collective-permute-start.12 = (f32[4,9,8,128]{3,2,1,0:T(8,128)S(1)}, f32[4,9,8,128]{3,2,1,0:T(8,128)S(1)}, u32[]{:S(2)}, u32[]{:S(2)}) collective-permute-start(f32[4,9,8,128]{3,2,1,0:T(8,128)S(1)} %pad_maximum_fusion.2), channel_id=1, source_target_pairs={{0,2},{1,3},{2,0},{3,1},{4,6},{5,7},{6,4},{7,5},{8,10},{9,11},{10,... | collective-permute-start | bytes 442376 | tf_op jit(solution)/shard_map/ppermute | solution.py:596
  53.8 1.7 %collective-permute-start.13 = (f32[8,9,8,128]{3,2,1,0:T(8,128)S(1)}, f32[8,9,8,128]{3,2,1,0:T(8,128)S(1)}, u32[]{:S(2)}, u32[]{:S(2)}) collective-permute-start(f32[8,9,8,128]{3,2,1,0:T(8,128)S(1)} %constant_dynamic-update-slice_fusion.near_side), channel_id=1, source_target_pairs={{0,1},{1,0},{2,3},{3,2},{4,5},{5,4},{6,7},{7,6},{8,9},{9,8},{10,11... | collective-permute-start | bytes 884744 | tf_op jit(solution)/shard_map/ppermute | solution.py:596
  53.8 1.7 %collective-permute-start.7 = (f32[16,8,128]{2,1,0:T(8,128)S(1)}, f32[16,8,128]{2,1,0:T(8,128)S(1)}, u32[]{:S(2)}, u32[]{:S(2)}) collective-permute-start(f32[16,8,128]{2,1,0:T(8,128)S(1)} %get-tuple-element.52), channel_id=1, source_target_pairs={{0,1},{1,0},{2,3},{3,2},{4,5},{5,4},{6,7},{7,6},{8,9},{9,8},{10,11... | collective-permute-start | bytes 196616 | tf_op jit(solution)/shard_map/ppermute | solution.py:596
  55.5 31.4 %copy-start.3 = (f32[8]{0:T(128)S(1)}, f32[8]{0:T(128)}, u32[]{:S(2)}) copy-start(f32[8]{0:T(128)} %pole_re.9) | copy-start | bytes 100
  55.5 31.4 %copy-start.5 = (f32[8]{0:T(128)S(1)}, f32[8]{0:T(128)}, u32[]{:S(2)}) copy-start(f32[8]{0:T(128)} %pole_im.9) | copy-start | bytes 100
  72.1 6.6 %collective-permute-start.18 = (f32[9,8,128]{2,1,0:T(8,128)S(1)}, f32[9,8,128]{2,1,0:T(8,128)S(1)}, u32[]{:S(2)}, u32[]{:S(2)}) collective-permute-start(f32[9,8,128]{2,1,0:T(8,128)S(1)} %get-tuple-element.63), channel_id=1, source_target_pairs={{0,12},{1,13},{2,14},{3,15},{4,8},{5,9},{6,10},{7,11},{8,4},{9,5},... | collective-permute-start | bytes 110600 | tf_op jit(solution)/shard_map/ppermute | solution.py:596
  73.9 5.3 %collective-permute-start.17 = (f32[9,8,128]{2,1,0:T(8,128)S(1)}, f32[9,8,128]{2,1,0:T(8,128)S(1)}, u32[]{:S(2)}, u32[]{:S(2)}) collective-permute-start(f32[9,8,128]{2,1,0:T(8,128)S(1)} %get-tuple-element.63), channel_id=1, source_target_pairs={{0,8},{1,9},{2,10},{3,11},{4,12},{5,13},{6,14},{7,15},{8,0},{9,1},... | collective-permute-start | bytes 110600 | tf_op jit(solution)/shard_map/ppermute | solution.py:596
  74.1 5.1 %collective-permute-start.16 = (f32[9,8,128]{2,1,0:T(8,128)S(1)}, f32[9,8,128]{2,1,0:T(8,128)S(1)}, u32[]{:S(2)}, u32[]{:S(2)}) collective-permute-start(f32[9,8,128]{2,1,0:T(8,128)S(1)} %get-tuple-element.63), channel_id=1, source_target_pairs={{0,4},{1,5},{2,6},{3,7},{4,0},{5,1},{6,2},{7,3},{8,12},{9,13},{10,... | collective-permute-start | bytes 110600 | tf_op jit(solution)/shard_map/ppermute | solution.py:596
  76.6 8.5 %collective-permute-start.15 = (f32[16,8,128]{2,1,0:T(8,128)S(1)}, f32[16,8,128]{2,1,0:T(8,128)S(1)}, u32[]{:S(2)}, u32[]{:S(2)}) collective-permute-start(f32[16,8,128]{2,1,0:T(8,128)S(1)} %get-tuple-element.62), channel_id=1, source_target_pairs={{0,15},{1,2},{2,1},{3,4},{4,3},{5,6},{6,5},{7,8},{8,7},{9,10},{10,... | collective-permute-start | bytes 196616 | tf_op jit(solution)/shard_map/ppermute | solution.py:603
  79.2 5.9 %collective-permute-start.19 = (f32[4,9,8,128]{3,2,1,0:T(8,128)S(1)}, f32[4,9,8,128]{3,2,1,0:T(8,128)S(1)}, u32[]{:S(2)}, u32[]{:S(2)}) collective-permute-start(f32[4,9,8,128]{3,2,1,0:T(8,128)S(1)} %pad_maximum_fusion.3), channel_id=1, source_target_pairs={{0,2},{1,3},{2,0},{3,1},{4,6},{5,7},{6,4},{7,5},{8,10},{9,11},{10,... | collective-permute-start | bytes 442376 | tf_op jit(solution)/shard_map/ppermute | solution.py:596
  85.1 1.7 %collective-permute-start.20 = (f32[8,9,8,128]{3,2,1,0:T(8,128)S(1)}, f32[8,9,8,128]{3,2,1,0:T(8,128)S(1)}, u32[]{:S(2)}, u32[]{:S(2)}) collective-permute-start(f32[8,9,8,128]{3,2,1,0:T(8,128)S(1)} %constant_dynamic-update-slice_fusion.5.near_side), channel_id=1, source_target_pairs={{0,1},{1,0},{2,3},{3,2},{4,5},{5,4},{6,7},{7,6},{8,9},{9,8},{10,11... | collective-permute-start | bytes 884744 | tf_op jit(solution)/shard_map/ppermute | solution.py:596
  85.2 1.7 %collective-permute-start.14 = (f32[16,8,128]{2,1,0:T(8,128)S(1)}, f32[16,8,128]{2,1,0:T(8,128)S(1)}, u32[]{:S(2)}, u32[]{:S(2)}) collective-permute-start(f32[16,8,128]{2,1,0:T(8,128)S(1)} %get-tuple-element.61), channel_id=1, source_target_pairs={{0,1},{1,0},{2,3},{3,2},{4,5},{5,4},{6,7},{7,6},{8,9},{9,8},{10,11... | collective-permute-start | bytes 196616 | tf_op jit(solution)/shard_map/ppermute | solution.py:596
  103.5 7.1 %collective-permute-start.25 = (f32[9,8,128]{2,1,0:T(8,128)S(1)}, f32[9,8,128]{2,1,0:T(8,128)S(1)}, u32[]{:S(2)}, u32[]{:S(2)}) collective-permute-start(f32[9,8,128]{2,1,0:T(8,128)S(1)} %get-tuple-element.75), channel_id=1, source_target_pairs={{0,12},{1,13},{2,14},{3,15},{4,8},{5,9},{6,10},{7,11},{8,4},{9,5},... | collective-permute-start | bytes 110600 | tf_op jit(solution)/shard_map/ppermute | solution.py:596
  105.7 4.9 %collective-permute-start.24 = (f32[9,8,128]{2,1,0:T(8,128)S(1)}, f32[9,8,128]{2,1,0:T(8,128)S(1)}, u32[]{:S(2)}, u32[]{:S(2)}) collective-permute-start(f32[9,8,128]{2,1,0:T(8,128)S(1)} %get-tuple-element.75), channel_id=1, source_target_pairs={{0,8},{1,9},{2,10},{3,11},{4,12},{5,13},{6,14},{7,15},{8,0},{9,1},... | collective-permute-start | bytes 110600 | tf_op jit(solution)/shard_map/ppermute | solution.py:596
  105.7 4.9 %collective-permute-start.23 = (f32[9,8,128]{2,1,0:T(8,128)S(1)}, f32[9,8,128]{2,1,0:T(8,128)S(1)}, u32[]{:S(2)}, u32[]{:S(2)}) collective-permute-start(f32[9,8,128]{2,1,0:T(8,128)S(1)} %get-tuple-element.75), channel_id=1, source_target_pairs={{0,4},{1,5},{2,6},{3,7},{4,0},{5,1},{6,2},{7,3},{8,12},{9,13},{10,... | collective-permute-start | bytes 110600 | tf_op jit(solution)/shard_map/ppermute | solution.py:596
  108.0 8.6 %collective-permute-start.22 = (f32[16,8,128]{2,1,0:T(8,128)S(1)}, f32[16,8,128]{2,1,0:T(8,128)S(1)}, u32[]{:S(2)}, u32[]{:S(2)}) collective-permute-start(f32[16,8,128]{2,1,0:T(8,128)S(1)} %get-tuple-element.74), channel_id=1, source_target_pairs={{0,15},{1,2},{2,1},{3,4},{4,3},{5,6},{6,5},{7,8},{8,7},{9,10},{10,... | collective-permute-start | bytes 196616 | tf_op jit(solution)/shard_map/ppermute | solution.py:603
  110.7 5.9 %collective-permute-start.26 = (f32[4,9,8,128]{3,2,1,0:T(8,128)S(1)}, f32[4,9,8,128]{3,2,1,0:T(8,128)S(1)}, u32[]{:S(2)}, u32[]{:S(2)}) collective-permute-start(f32[4,9,8,128]{3,2,1,0:T(8,128)S(1)} %pad_maximum_fusion.4), channel_id=1, source_target_pairs={{0,2},{1,3},{2,0},{3,1},{4,6},{5,7},{6,4},{7,5},{8,10},{9,11},{10,... | collective-permute-start | bytes 442376 | tf_op jit(solution)/shard_map/ppermute | solution.py:596
  116.6 1.7 %collective-permute-start.27 = (f32[8,9,8,128]{3,2,1,0:T(8,128)S(1)}, f32[8,9,8,128]{3,2,1,0:T(8,128)S(1)}, u32[]{:S(2)}, u32[]{:S(2)}) collective-permute-start(f32[8,9,8,128]{3,2,1,0:T(8,128)S(1)} %constant_dynamic-update-slice_fusion.10.near_side), channel_id=1, source_target_pairs={{0,1},{1,0},{2,3},{3,2},{4,5},{5,4},{6,7},{7,6},{8,9},{9,8},{10,11... | collective-permute-start | bytes 884744 | tf_op jit(solution)/shard_map/ppermute | solution.py:596
  116.7 1.7 %collective-permute-start.21 = (f32[16,8,128]{2,1,0:T(8,128)S(1)}, f32[16,8,128]{2,1,0:T(8,128)S(1)}, u32[]{:S(2)}, u32[]{:S(2)}) collective-permute-start(f32[16,8,128]{2,1,0:T(8,128)S(1)} %get-tuple-element.73), channel_id=1, source_target_pairs={{0,1},{1,0},{2,3},{3,2},{4,5},{5,4},{6,7},{7,6},{8,9},{9,8},{10,11... | collective-permute-start | bytes 196616 | tf_op jit(solution)/shard_map/ppermute | solution.py:596
  134.8 5.5 %collective-permute-start.30 = (f32[1,8,128]{2,1,0:T(8,128)S(1)}, f32[1,8,128]{2,1,0:T(8,128)S(1)}, u32[]{:S(2)}, u32[]{:S(2)}) collective-permute-start(f32[1,8,128]{2,1,0:T(8,128)S(1)} %get-tuple-element.78), channel_id=1, source_target_pairs={{0,12},{1,13},{2,14},{3,15},{4,8},{5,9},{6,10},{7,11},{8,4},{9,5},... | collective-permute-start | bytes 12296 | tf_op jit(solution)/shard_map/ppermute | solution.py:596
  136.7 4.5 %collective-permute-start.29 = (f32[1,8,128]{2,1,0:T(8,128)S(1)}, f32[1,8,128]{2,1,0:T(8,128)S(1)}, u32[]{:S(2)}, u32[]{:S(2)}) collective-permute-start(f32[1,8,128]{2,1,0:T(8,128)S(1)} %get-tuple-element.78), channel_id=1, source_target_pairs={{0,8},{1,9},{2,10},{3,11},{4,12},{5,13},{6,14},{7,15},{8,0},{9,1},... | collective-permute-start | bytes 12296 | tf_op jit(solution)/shard_map/ppermute | solution.py:596
  136.9 4.3 %collective-permute-start.28 = (f32[1,8,128]{2,1,0:T(8,128)S(1)}, f32[1,8,128]{2,1,0:T(8,128)S(1)}, u32[]{:S(2)}, u32[]{:S(2)}) collective-permute-start(f32[1,8,128]{2,1,0:T(8,128)S(1)} %get-tuple-element.78), channel_id=1, source_target_pairs={{0,4},{1,5},{2,6},{3,7},{4,0},{5,1},{6,2},{7,3},{8,12},{9,13},{10,... | collective-permute-start | bytes 12296 | tf_op jit(solution)/shard_map/ppermute | solution.py:596
  141.2 3.7 %collective-permute-start.31 = (f32[4,1,8,128]{3,2,1,0:T(8,128)S(1)}, f32[4,1,8,128]{3,2,1,0:T(8,128)S(1)}, u32[]{:S(2)}, u32[]{:S(2)}) collective-permute-start(f32[4,1,8,128]{3,2,1,0:T(8,128)S(1)} %pad_maximum_fusion.5), channel_id=1, source_target_pairs={{0,2},{1,3},{2,0},{3,1},{4,6},{5,7},{6,4},{7,5},{8,10},{9,11},{10,... | collective-permute-start | bytes 49160 | tf_op jit(solution)/shard_map/ppermute | solution.py:596
  145.0 1.2 collective-permute-start.32

commit v4 on v3

--- a/solution.py
+++ b/solution.py
@@ -146,12 +146,12 @@
     place_gathered(ext, 2 * NYB + blocks, me, near_side, far_side, cols)
 
 
-def pole_factor(values):
-    poles = values.shape[0]
+def pole_factor(values, part):
+    poles = values.shape[0] // 2
     row = lax.broadcasted_iota(jnp.int32, (poles, LANES), 0)
     factor = jnp.zeros((poles, LANES), F32)
     for pole in range(poles):
-        factor = jnp.where(row == pole, values[pole], factor)
+        factor = jnp.where(row == pole, values[part * poles + pole], factor)
     return factor
 
 
@@ -340,8 +340,8 @@
         copy.wait()
 
 
-def own_kernel(first, near, pole_re, pole_im, own, ham, ovl, image, wide, mats, *sems):
-    z = (pole_factor(pole_re), pole_factor(pole_im))
+def own_kernel(first, near, pole_ref, own, ham, ovl, image, wide, mats, *sems):
+    z = (pole_factor(pole_ref, 0), pole_factor(pole_ref, 1))
     blocks = own.shape[0]
     parts = sems[0].shape[0]
     size = image.shape[0] // parts
@@ -380,11 +380,11 @@
 
 
 def first_kernel(
-    me_ref, near, contact, pole_re, pole_im, own, image_in, partner, other, near_side, far_side, ham, ovl, sigma,
+    me_ref, near, contact, pole_ref, own, image_in, partner, other, near_side, far_side, ham, ovl, sigma,
     rhs_ext, image, chunk, edge_a, edge_b, wide, acc, mats, *sems,
 ):
     blocks, poles = own.shape[0], own.shape[1]
-    z = (pole_factor(pole_re), pole_factor(pole_im))
+    z = (pole_factor(pole_ref, 0), pole_factor(pole_ref, 1))
     spots = contact_spots(contact, me_ref[0], blocks)
     edge_slabs = NYB * NNZ // 2
     edges = []
@@ -423,13 +423,13 @@
 
 
 def second_kernel(
-    me_ref, near, contact, pole_re, pole_im, rhs_ext, own, partner, other, near_side, far_side, ham, ovl, sigma,
+    me_ref, near, contact, pole_ref, rhs_ext, own, partner, other, near_side, far_side, ham, ovl, sigma,
     image_ext, half_ext, turned, chunk, edge_a, edge_b, scalars, wide, acc, mats,
     *sems,
 ):
     start_matrices(ham, ovl, sigma, mats, sems)
     blocks, poles = own.shape[0], own.shape[1]
-    z = (pole_factor(pole_re), pole_factor(pole_im))
+    z = (pole_factor(pole_ref, 0), pole_factor(pole_ref, 1))
     spots = contact_spots(contact, me_ref[0], blocks)
     cols = len(spots)
     fill_extended(image_ext, partner, own, other, me_ref[0], near_side, far_side, cols)
@@ -463,14 +463,14 @@
 
 
 def third_kernel(
-    me_ref, near, contact, pole_re, pole_im, scalars, rhs_ext, image_ext, half_ext, own, partner, other,
+    me_ref, near, contact, pole_ref, scalars, rhs_ext, image_ext, half_ext, own, partner, other,
     near_side, far_side, ham, ovl, sigma,
     residual_own, direction_own, residual_rem, direction_rem, iterate, image, chunk, edge_a,
     edge_b, rho_out, turned_ext, wide, acc, mats, *sems,
 ):
     start_matrices(ham, ovl, sigma, mats, sems)
     blocks, poles = own.shape[0], own.shape[1]
-    z = (pole_factor(pole_re), pole_factor(pole_im))
+    z = (pole_factor(pole_ref, 0), pole_factor(pole_ref, 1))
     spots = contact_spots(contact, me_ref[0], blocks)
     cols = len(spots)
     fill_extended(turned_ext, partner, own, other, me_ref[0], near_side, far_side, cols)
@@ -525,13 +525,13 @@
 
 
 def fourth_kernel(
-    me_ref, near, contact, pole_re, pole_im, rho_in, residual_own, direction_own, residual_rem,
+    me_ref, near, contact, pole_ref, rho_in, residual_own, direction_own, residual_rem,
     direction_rem, iterate_in, own, partner, other, near_side, far_side, ham, ovl, sigma,
     half_own, turned, iterate, sums_out, contact_image, wide, acc, mats, *sems,
 ):
     start_matrices(ham, ovl, sigma, mats, sems)
     blocks, poles = own.shape[0], own.shape[1]
-    z = (pole_factor(pole_re), pole_factor(pole_im))
+    z = (pole_factor(pole_ref, 0), pole_factor(pole_ref, 1))
     spots = contact_spots(contact, me_ref[0], blocks)
     cols = len(spots)
     place_gathered(contact_image, 0, me_ref[0], near_side, far_side, cols)
@@ -624,7 +624,8 @@
     parts = max(2, blocks // 32)
     sems = [pltpu.SemaphoreType.DMA((p,)) for p in (parts, parts, max(1, sigma.shape[0] // 128))]
     hbm = pl.BlockSpec(memory_space=pl.ANY)
-    fixed = (me_ref, near, contact, pole_real, pole_imag)
+    pole_parts = jnp.concatenate([pole_real, pole_imag])
+    fixed = (me_ref, near, contact, pole_parts)
     remote = 2 * NYB + CONTACT
     rows = cols + 1
 
@@ -632,7 +633,7 @@
         scratch = [pltpu.VMEM((r, poles, LANES), F32) for r in scratch]
         return pl.pallas_call(
             kernel,
-            in_specs=[SMEM] * 5 + [VMEM] * (len(inputs) - 5) + [hbm] * 3,
+            in_specs=[SMEM] * 4 + [VMEM] * (len(inputs) - 4) + [hbm] * 3,
             out_specs=[VMEM] * len(out_rows),
             out_shape=[vec_shape(r) for r in out_rows],
             scratch_shapes=[*scratch, wide, acc, held, *sems],
@@ -652,7 +653,7 @@
     def own_part(near):
         return pl.pallas_call(
             functools.partial(own_kernel, 0),
-            in_specs=[SMEM] * 3 + [VMEM] + [hbm] * 2,
+            in_specs=[SMEM] * 2 + [VMEM] + [hbm] * 2,
             out_specs=VMEM,
             out_shape=vec_shape(blocks),
             scratch_shapes=[wide, held, *([pltpu.SemaphoreType.DMA((parts,))] * 2)],
@@ -661,7 +662,7 @@
                 flops=4 * ham.size * 2 * poles, bytes_accessed=4 * ham.size, transcendentals=0
             ),
             name="own",
-        )(near, pole_real, pole_imag, rhs, *slabs[:2])
+        )(near, pole_parts, rhs, *slabs[:2])
 
     rhs_ext, image, chunk, edge_a, edge_b = call(
         first_kernel, (*fixed, rhs, *exchange(chunk, edges, own_part)),

time: 148 us -> 147 us (level)
    unnamed x32 -> x24, local copies, waits for them, and re-layouts: 4.11 us -> 2.79 us
where the time goes in v4:
time: 147 us
  Pallas kernels  73 us (50%)
  starting transfers between devices  43.6 us (30%)
  waiting for transfers between devices  25 us (17%)
  local copies, waits for them, and re-layouts  3.14 us (2%)
  other arithmetic  1.52 us (1%)
    pallas_call x4, Pallas kernels, call(): pl.pallas_call(kernel, in_specs=[SMEM] * 4 + [VMEM] * (len(inputs) - 4) +...  60.1 us
    ppermute x29, starting transfers between devices, flip(): return lax.ppermute(value, 'gx', [(i, i ^ mask) for i in range(count)])  35.4 us
    ppermute x29, waiting for transfers between devices, flip(): return lax.ppermute(value, 'gx', [(i, i ^ mask) for i in range(count)])  25 us
    pallas_call x1, Pallas kernels, own_part(): pl.pallas_call(functools.partial(own_kernel, 0), in_specs=[SMEM] * 2 + [V...  10.5 us
    ppermute x4, starting transfers between devices, exchange(): far = (lax.ppermute(edges[1], 'gx', other),)  8.15 us
  transfers between devices with their start and end apart: 33, of which 15 were waited for; matrix products, arithmetic and copies ran while one was open for 1% of the time, Pallas kernels for 7%

profile of v4, /device:TPU:0, one launch (start us, length us, event | category | flops | bytes accessed | tf_op | source)
XLA Modules:
  0.0 147.1 jit_solution(9621230042960338609)
XLA Ops:
  0.6 0.0 copy-start
  0.6 1.0 copy-done
  1.7 0.7 copy-done.2
  2.3 0.9 prepare.1
  3.2 5.1 %collective-permute-start.3 = (f32[9,8,128]{2,1,0:T(8,128)S(1)}, f32[9,8,128]{2,1,0:T(8,128)S(1)}, u32[]{:S(2)}, u32[]{:S(2)}) collective-permute-start(f32[9,8,128]{2,1,0:T(8,128)S(1)} %get-tuple-element.43), channel_id=1, source_target_pairs={{0,12},{1,13},{2,14},{3,15},{4,8},{5,9},{6,10},{7,11},{8,4},{9,5},... | collective-permute-start | bytes 110600 | tf_op jit(solution)/shard_map/ppermute | solution.py:596
  8.3 0.6 collective-permute-start.1
  9.0 0.7 add_select_fusion
  9.7 0.1 copy.10
  9.8 0.2 reshape.17.near
  10.0 0.3 collective-permute-done.3
  10.3 2.9 %collective-permute-done.2 = f32[9,8,128]{2,1,0:T(8,128)S(1)} collective-permute-done((f32[9,8,128]{2,1,0:T(8,128)S(1)}, f32[9,8,128]{2,1,0:T(8,128)S(1)}, u32[]{:S(2)}, u32[]{:S(2)}) %collective-permute-start.2) | collective-permute-done | bytes 36896 | tf_op jit(solution)/shard_map/ppermute | solution.py:596
  13.2 1.6 %collective-permute-start.4 = (f32[4,9,8,128]{3,2,1,0:T(8,128)S(1)}, f32[4,9,8,128]{3,2,1,0:T(8,128)S(1)}, u32[]{:S(2)}, u32[]{:S(2)}) collective-permute-start(f32[4,9,8,128]{3,2,1,0:T(8,128)S(1)} %pad_maximum_fusion.1), channel_id=1, source_target_pairs={{0,2},{1,3},{2,0},{3,1},{4,6},{5,7},{6,4},{7,5},{8,10},{9,11},{10,... | collective-permute-start | bytes 442376 | tf_op jit(solution)/shard_map/ppermute | solution.py:596
  14.8 0.0 collective-permute-start
  14.8 0.7 pad_maximum_fusion.6.pole_ref
  15.6 1.0 copy-done.1
  16.6 10.5 %own.3.image_in = f32[128,8,128]{2,1,0:T(8,128)S(1)} custom-call(s32[640]{0:T(1024)S(1)} %reshape.17.near, f32[16]{0:T(128)S(1)} %pad_maximum_fusion.6.pole_ref, f32[128,8,128]{2,1,0:T(8,128)S(1)} %copy-done.1, bf16[320,128,128]{2,1,0:T(8,128)(2,1)} %bitcast.44, bf16[320,128,128]{2,1,0:T(8,128)(2,1)} %bitcast.49), custom_call_target="tpu_custom_call" | custom-call | flops 335544320 | bytes 20971520 | tf_op jit(solution)/shard_map/own/pallas_call | solution.py:654
  27.1 0.0 collective-permute-done.4
  27.1 0.0 collective-permute-done.other
  27.2 0.7 collective-permute-start.6
  27.8 0.1 collective-permute-start.5
  27.9 1.2 collective-permute-done.5.partner
  29.1 10.4 %first.1 = (f32[288,8,128]{2,1,0:T(8,128)S(1)}, f32[128,8,128]{2,1,0:T(8,128)S(1)}, f32[9,8,128]{2,1,0:T(8,128)S(1)}, f32[16,8,128]{2,1,0:T(8,128)S(1)}, f32[16,8,128]{2,1,0:T(8,128)S(1)}) custom-call(s32[1]{0:T(128)} %bitcast.me_ref, s32[640]{0:T(1024)S(1)} %reshape.17.near, s32[8]{0:T(128)S(1)} %copy-done.3, f32[16]{0:T(128)S(1)} %pad_maximum_fusion.6.pole_ref, ...), custom_call_target="tpu_custom_call" | custom-call | tf_op jit(solution)/shard_map/first/pallas_call | solution.py:634
  39.6 1.5 %collective-permute-start.11 = (f32[9,8,128]{2,1,0:T(8,128)S(1)}, f32[9,8,128]{2,1,0:T(8,128)S(1)}, u32[]{:S(2)}, u32[]{:S(2)}) collective-permute-start(f32[9,8,128]{2,1,0:T(8,128)S(1)} %get-tuple-element.54), channel_id=1, source_target_pairs={{0,12},{1,13},{2,14},{3,15},{4,8},{5,9},{6,10},{7,11},{8,4},{9,5},... | collective-permute-start | bytes 110600 | tf_op jit(solution)/shard_map/ppermute | solution.py:596
  41.1 0.6 collective-permute-start.10
  41.8 2.3 %collective-permute-start.9 = (f32[9,8,128]{2,1,0:T(8,128)S(1)}, f32[9,8,128]{2,1,0:T(8,128)S(1)}, u32[]{:S(2)}, u32[]{:S(2)}) collective-permute-start(f32[9,8,128]{2,1,0:T(8,128)S(1)} %get-tuple-element.54), channel_id=1, source_target_pairs={{0,4},{1,5},{2,6},{3,7},{4,0},{5,1},{6,2},{7,3},{8,12},{9,13},{10,... | collective-permute-start | bytes 110600 | tf_op jit(solution)/shard_map/ppermute | solution.py:596
  44.1 3.3 %collective-permute-start.8 = (f32[16,8,128]{2,1,0:T(8,128)S(1)}, f32[16,8,128]{2,1,0:T(8,128)S(1)}, u32[]{:S(2)}, u32[]{:S(2)}) collective-permute-start(f32[16,8,128]{2,1,0:T(8,128)S(1)} %get-tuple-element.53), channel_id=1, source_target_pairs={{0,15},{1,2},{2,1},{3,4},{4,3},{5,6},{6,5},{7,8},{8,7},{9,10},{10,... | collective-permute-start | bytes 196616 | tf_op jit(solution)/shard_map/ppermute | solution.py:603
  47.4 2.0 %collective-permute-start.12 = (f32[4,9,8,128]{3,2,1,0:T(8,128)S(1)}, f32[4,9,8,128]{3,2,1,0:T(8,128)S(1)}, u32[]{:S(2)}, u32[]{:S(2)}) collective-permute-start(f32[4,9,8,128]{3,2,1,0:T(8,128)S(1)} %pad_maximum_fusion.2), channel_id=1, source_target_pairs={{0,2},{1,3},{2,0},{3,1},{4,6},{5,7},{6,4},{7,5},{8,10},{9,11},{10,... | collective-permute-start | bytes 442376 | tf_op jit(solution)/shard_map/ppermute | solution.py:596
  49.4 3.7 %collective-permute-done.12 = f32[4,9,8,128]{3,2,1,0:T(8,128)S(1)} collective-permute-done((f32[4,9,8,128]{3,2,1,0:T(8,128)S(1)}, f32[4,9,8,128]{3,2,1,0:T(8,128)S(1)}, u32[]{:S(2)}, u32[]{:S(2)}) %collective-permute-start.12) | collective-permute-done | bytes 147488 | tf_op jit(solution)/shard_map/ppermute | solution.py:596
  53.2 0.1 collective-permute-start.13
  53.3 0.5 collective-permute-start.7
  53.8 1.2 collective-permute-done.7.partner
  54.9 16.6 %second.1 = (f32[288,8,128]{2,1,0:T(8,128)S(1)}, f32[288,8,128]{2,1,0:T(8,128)S(1)}, f32[128,8,128]{2,1,0:T(8,128)S(1)}, f32[9,8,128]{2,1,0:T(8,128)S(1)}, f32[1...) custom-call(s32[1]{0:T(128)} %bitcast.me_ref, s32[640]{0:T(1024)S(1)} %reshape.17.near, ...), custom_call_target="tpu_custom_call" | custom-call | tf_op jit(solution)/shard_map/second/pallas_call | solution.py:634
  71.5 1.7 %collective-permute-start.18 = (f32[9,8,128]{2,1,0:T(8,128)S(1)}, f32[9,8,128]{2,1,0:T(8,128)S(1)}, u32[]{:S(2)}, u32[]{:S(2)}) collective-permute-start(f32[9,8,128]{2,1,0:T(8,128)S(1)} %get-tuple-element.63), channel_id=1, source_target_pairs={{0,12},{1,13},{2,14},{3,15},{4,8},{5,9},{6,10},{7,11},{8,4},{9,5},... | collective-permute-start | bytes 110600 | tf_op jit(solution)/shard_map/ppermute | solution.py:596
  73.3 0.2 collective-permute-start.17
  73.5 2.5 %collective-permute-start.16 = (f32[9,8,128]{2,1,0:T(8,128)S(1)}, f32[9,8,128]{2,1,0:T(8,128)S(1)}, u32[]{:S(2)}, u32[]{:S(2)}) collective-permute-start(f32[9,8,128]{2,1,0:T(8,128)S(1)} %get-tuple-element.63), channel_id=1, source_target_pairs={{0,4},{1,5},{2,6},{3,7},{4,0},{5,1},{6,2},{7,3},{8,12},{9,13},{10,... | collective-permute-start | bytes 110600 | tf_op jit(solution)/shard_map/ppermute | solution.py:596
  76.0 2.1 %collective-permute-start.15 = (f32[16,8,128]{2,1,0:T(8,128)S(1)}, f32[16,8,128]{2,1,0:T(8,128)S(1)}, u32[]{:S(2)}, u32[]{:S(2)}) collective-permute-start(f32[16,8,128]{2,1,0:T(8,128)S(1)} %get-tuple-element.62), channel_id=1, source_target_pairs={{0,15},{1,2},{2,1},{3,4},{4,3},{5,6},{6,5},{7,8},{8,7},{9,10},{10,... | collective-permute-start | bytes 196616 | tf_op jit(solution)/shard_map/ppermute | solution.py:603
  78.2 0.4 collective-permute-done.17
  78.5 0.1 collective-permute-done.16
  78.6 2.1 %collective-permute-start.19 = (f32[4,9,8,128]{3,2,1,0:T(8,128)S(1)}, f32[4,9,8,128]{3,2,1,0:T(8,128)S(1)}, u32[]{:S(2)}, u32[]{:S(2)}) collective-permute-start(f32[4,9,8,128]{3,2,1,0:T(8,128)S(1)} %pad_maximum_fusion.3), channel_id=1, source_target_pairs={{0,2},{1,3},{2,0},{3,1},{4,6},{5,7},{6,4},{7,5},{8,10},{9,11},{10,... | collective-permute-start | bytes 442376 | tf_op jit(solution)/shard_map/ppermute | solution.py:596
  80.8 3.7 %collective-permute-done.19 = f32[4,9,8,128]{3,2,1,0:T(8,128)S(1)} collective-permute-done((f32[4,9,8,128]{3,2,1,0:T(8,128)S(1)}, f32[4,9,8,128]{3,2,1,0:T(8,128)S(1)}, u32[]{:S(2)}, u32[]{:S(2)}) %collective-permute-start.19) | collective-permute-done | bytes 147488 | tf_op jit(solution)/shard_map/ppermute | solution.py:596
  84.5 0.1 collective-permute-start.20
  84.6 0.5 collective-permute-start.14
  85.1 1.2 collective-permute-done.14.partner
  86.3 16.6 %third.1 = (f32[128,8,128]{2,1,0:T(8,128)S(1)}, f32[128,8,128]{2,1,0:T(8,128)S(1)}, f32[160,8,128]{2,1,0:T(8,128)S(1)}, f32[160,8,128]{2,1,0:T(8,128)S(1)}, f32[...) custom-call(s32[1]{0:T(128)} %bitcast.me_ref, ...), custom_call_target="tpu_custom_call" | custom-call | tf_op jit(solution)/shard_map/third/pallas_call | solution.py:634
  102.9 2.2 %collective-permute-start.25 = (f32[9,8,128]{2,1,0:T(8,128)S(1)}, f32[9,8,128]{2,1,0:T(8,128)S(1)}, u32[]{:S(2)}, u32[]{:S(2)}) collective-permute-start(f32[9,8,128]{2,1,0:T(8,128)S(1)} %get-tuple-element.75), channel_id=1, source_target_pairs={{0,12},{1,13},{2,14},{3,15},{4,8},{5,9},{6,10},{7,11},{8,4},{9,5},... | collective-permute-start | bytes 110600 | tf_op jit(solution)/shard_map/ppermute | solution.py:596
  105.1 0.0 collective-permute-start.24
  105.1 2.3 %collective-permute-start.23 = (f32[9,8,128]{2,1,0:T(8,128)S(1)}, f32[9,8,128]{2,1,0:T(8,128)S(1)}, u32[]{:S(2)}, u32[]{:S(2)}) collective-permute-start(f32[9,8,128]{2,1,0:T(8,128)S(1)} %get-tuple-element.75), channel_id=1, source_target_pairs={{0,4},{1,5},{2,6},{3,7},{4,0},{5,1},{6,2},{7,3},{8,12},{9,13},{10,... | collective-permute-start | bytes 110600 | tf_op jit(solution)/shard_map/ppermute | solution.py:596
  107.4 2.7 %collective-permute-start.22 = (f32[16,8,128]{2,1,0:T(8,128)S(1)}, f32[16,8,128]{2,1,0:T(8,128)S(1)}, u32[]{:S(2)}, u32[]{:S(2)}) collective-permute-start(f32[16,8,128]{2,1,0:T(8,128)S(1)} %get-tuple-element.74), channel_id=1, source_target_pairs={{0,15},{1,2},{2,1},{3,4},{4,3},{5,6},{6,5},{7,8},{8,7},{9,10},{10,... | collective-permute-start | bytes 196616 | tf_op jit(solution)/shard_map/ppermute | solution.py:603
  110.0 0.0 collective-permute-done.23
  110.1 2.2 %collective-permute-start.26 = (f32[4,9,8,128]{3,2,1,0:T(8,128)S(1)}, f32[4,9,8,128]{3,2,1,0:T(8,128)S(1)}, u32[]{:S(2)}, u32[]{:S(2)}) collective-permute-start(f32[4,9,8,128]{3,2,1,0:T(8,128)S(1)} %pad_maximum_fusion.4), channel_id=1, source_target_pairs={{0,2},{1,3},{2,0},{3,1},{4,6},{5,7},{6,4},{7,5},{8,10},{9,11},{10,... | collective-permute-start | bytes 442376 | tf_op jit(solution)/shard_map/ppermute | solution.py:596
  112.3 3.6 %collective-permute-done.26 = f32[4,9,8,128]{3,2,1,0:T(8,128)S(1)} collective-permute-done((f32[4,9,8,128]{3,2,1,0:T(8,128)S(1)}, f32[4,9,8,128]{3,2,1,0:T(8,128)S(1)}, u32[]{:S(2)}, u32[]{:S(2)}) %collective-permute-start.26) | collective-permute-done | bytes 147488 | tf_op jit(solution)/shard_map/ppermute | solution.py:596
  115.9 0.1 collective-permute-start.27
  116.0 0.5 collective-permute-start.21
  116.5 1.2 collective-permute-done.21.partner
  117.7 16.4 %fourth.1 = (f32[128,8,128]{2,1,0:T(8,128)S(1)}, f32[128,8,128]{2,1,0:T(8,128)S(1)}, f32[128,8,128]{2,1,0:T(8,128)S(1)}, f32[1,8,128]{2,1,0:T(8,128)S(1)}) custom-call(s32[1]{0:T(128)} %bitcast.me_ref, s32[640]{0:T(1024)S(1)} %reshape.17.near, s32[8]{0:T(128)S(1)} %copy-done.3, f32[16]{0:T(128)S(1)} %pad_maximum_fusion.6.pole_ref, ...), custom_call_target="tpu_custom_call" | custom-call | tf_op jit(solution)/shard_map/fourth/pallas_call | solution.py:634
  134.1 2.0 %collective-permute-start.30 = (f32[1,8,128]{2,1,0:T(8,128)S(1)}, f32[1,8,128]{2,1,0:T(8,128)S(1)}, u32[]{:S(2)}, u32[]{:S(2)}) collective-permute-start(f32[1,8,128]{2,1,0:T(8,128)S(1)} %get-tuple-element.78), channel_id=1, source_target_pairs={{0,12},{1,13},{2,14},{3,15},{4,8},{5,9},{6,10},{7,11},{8,4},{9,5},... | collective-permute-start | bytes 12296 | tf_op jit(solution)/shard_map/ppermute | solution.py:596
  136.1 0.2 collective-permute-start.29
  136.3 2.3 %collective-permute-start.28 = (f32[1,8,128]{2,1,0:T(8,128)S(1)}, f32[1,8,128]{2,1,0:T(8,128)S(1)}, u32[]{:S(2)}, u32[]{:S(2)}) collective-permute-start(f32[1,8,128]{2,1,0:T(8,128)S(1)} %get-tuple-element.78), channel_id=1, source_target_pairs={{0,4},{1,5},{2,6},{3,7},{4,0},{5,1},{6,2},{7,3},{8,12},{9,13},{10,... | collective-permute-start | bytes 12296 | tf_op jit(solution)/shard_map/ppermute | solution.py:596
  138.6 1.0 collective-permute-done.30
  139.6 1.0 collective-permute-done.29
  140.6 1.5 %collective-permute-start.31 = (f32[4,1,8,128]{3,2,1,0:T(8,128)S(1)}, f32[4,1,8,128]{3,2,1,0:T(8,128)S(1)}, u32[]{:S(2)}, u32[]{:S(2)}) collective-permute-start(f32[4,1,8,128]{3,2,1,0:T(8,128)S(1)} %pad_maximum_fusion.5), channel_id=1, source_target_pairs={{0,2},{1,3},{2,0},{3,1},{4,6},{5,7},{6,4},{7,5},{8,10},{9,11},{10,... | collective-permute-start | bytes 49160 | tf_op jit(solution)/shard_map/ppermute | solution.py:596
  142.1 2.2 %collective-permute-done.31 = f32[4,1,8,128]{3,2,1,0:T(8,128)S(1)} collective-permute-done((f32[4,1,8,128]{3,2,1,0:T(8,128)S(1)}, f32[4,1,8,128]{3,2,1,0:T(8,128)S(1)}, u32[]{:S(2)}, u32[]{:S(2)}) %collective-permute-start.31) | collective-permute-done | bytes 16416 | tf_op jit(solution)/shard_map/ppermute | solution.py:596
  144.4 1.2 collective-permute-done.32.far_side
  145.6 1.6 %last.1 = (f32[128,8,128]{2,1,0:T(8,128)}, f32[128,8,128]{2,1,0:T(8,128)}) custom-call(f32[8,1,8,128]{3,2,1,0:T(8,128)S(1)} %constant_dynamic-update-slice_fusion.15.near_side, f32[8,1,8,128]{3,2,1,0:T(8,128)S(1)} %collective-permute-done.32.far_side, f32[128,8,128]{2,1,0:T(8,128)S(1)} %get-tuple-element.79.half_own, ...), custom_call_target="tpu_custom_call" | custom-call | tf_op jit(solution)/shard_map/last/pallas_call | solution.py:687
  (47 shorter events, 0.2 us)
Async XLA Ops:
  0.6 1.0 copy-start
  1.7 0.7 copy-start.2
  3.2 7.1 %collective-permute-start.3 = (f32[9,8,128]{2,1,0:T(8,128)S(1)}, f32[9,8,128]{2,1,0:T(8,128)S(1)}, u32[]{:S(2)}, u32[]{:S(2)}) collective-permute-start(f32[9,8,128]{2,1,0:T(8,128)S(1)} %get-tuple-element.43), channel_id=1, source_target_pairs={{0,12},{1,13},{2,14},{3,15},{4,8},{5,9},{6,10},{7,11},{8,4},{9,5},... | collective-permute-start | bytes 110600 | tf_op jit(solution)/shard_map/ppermute | solution.py:596
  8.3 4.9 %collective-permute-start.2 = (f32[9,8,128]{2,1,0:T(8,128)S(1)}, f32[9,8,128]{2,1,0:T(8,128)S(1)}, u32[]{:S(2)}, u32[]{:S(2)}) collective-permute-start(f32[9,8,128]{2,1,0:T(8,128)S(1)} %get-tuple-element.43), channel_id=1, source_target_pairs={{0,8},{1,9},{2,10},{3,11},{4,12},{5,13},{6,14},{7,15},{8,0},{9,1},... | collective-permute-start | bytes 110600 | tf_op jit(solution)/shard_map/ppermute | solution.py:596
  8.3 4.9 %collective-permute-start.1 = (f32[9,8,128]{2,1,0:T(8,128)S(1)}, f32[9,8,128]{2,1,0:T(8,128)S(1)}, u32[]{:S(2)}, u32[]{:S(2)}) collective-permute-start(f32[9,8,128]{2,1,0:T(8,128)S(1)} %get-tuple-element.43), channel_id=1, source_target_pairs={{0,4},{1,5},{2,6},{3,7},{4,0},{5,1},{6,2},{7,3},{8,12},{9,13},{10,... | collective-permute-start | bytes 110600 | tf_op jit(solution)/shard_map/ppermute | solution.py:596
  13.2 13.9 %collective-permute-start.4 = (f32[4,9,8,128]{3,2,1,0:T(8,128)S(1)}, f32[4,9,8,128]{3,2,1,0:T(8,128)S(1)}, u32[]{:S(2)}, u32[]{:S(2)}) collective-permute-start(f32[4,9,8,128]{3,2,1,0:T(8,128)S(1)} %pad_maximum_fusion.1), channel_id=1, source_target_pairs={{0,2},{1,3},{2,0},{3,1},{4,6},{5,7},{6,4},{7,5},{8,10},{9,11},{10,... | collective-permute-start | bytes 442376 | tf_op jit(solution)/shard_map/ppermute | solution.py:596
  14.8 12.3 %collective-permute-start = (f32[16,8,128]{2,1,0:T(8,128)S(1)}, f32[16,8,128]{2,1,0:T(8,128)S(1)}, u32[]{:S(2)}, u32[]{:S(2)}) collective-permute-start(f32[16,8,128]{2,1,0:T(8,128)S(1)} %get-tuple-element.42), channel_id=1, source_target_pairs={{0,15},{1,2},{2,1},{3,4},{4,3},{5,6},{6,5},{7,8},{8,7},{9,10},{10,... | collective-permute-start | bytes 196616 | tf_op jit(solution)/shard_map/ppermute | solution.py:603
  15.6 1.0 copy-start.1
  16.6 12.5 %copy-start.3 = (s32[8]{0:T(128)S(1)}, s32[8]{0:T(128)}, u32[]{:S(2)}) copy-start(s32[8]{0:T(128)} %contact.9) | copy-start | bytes 100
  27.2 2.0 %collective-permute-start.6 = (f32[8,9,8,128]{3,2,1,0:T(8,128)S(1)}, f32[8,9,8,128]{3,2,1,0:T(8,128)S(1)}, u32[]{:S(2)}, u32[]{:S(2)}) collective-permute-start(f32[8,9,8,128]{3,2,1,0:T(8,128)S(1)} %pad_maximum_fusion.near_side), channel_id=1, source_target_pairs={{0,1},{1,0},{2,3},{3,2},{4,5},{5,4},{6,7},{7,6},{8,9},{9,8},{10,11... | collective-permute-start | bytes 884744 | tf_op jit(solution)/shard_map/ppermute | solution.py:596
  27.8 1.3 collective-permute-start.5
  39.6 7.8 %collective-permute-start.11 = (f32[9,8,128]{2,1,0:T(8,128)S(1)}, f32[9,8,128]{2,1,0:T(8,128)S(1)}, u32[]{:S(2)}, u32[]{:S(2)}) collective-permute-start(f32[9,8,128]{2,1,0:T(8,128)S(1)} %get-tuple-element.54), channel_id=1, source_target_pairs={{0,12},{1,13},{2,14},{3,15},{4,8},{5,9},{6,10},{7,11},{8,4},{9,5},... | collective-permute-start | bytes 110600 | tf_op jit(solution)/shard_map/ppermute | solution.py:596
  41.1 6.3 %collective-permute-start.10 = (f32[9,8,128]{2,1,0:T(8,128)S(1)}, f32[9,8,128]{2,1,0:T(8,128)S(1)}, u32[]{:S(2)}, u32[]{:S(2)}) collective-permute-start(f32[9,8,128]{2,1,0:T(8,128)S(1)} %get-tuple-element.54), channel_id=1, source_target_pairs={{0,8},{1,9},{2,10},{3,11},{4,12},{5,13},{6,14},{7,15},{8,0},{9,1},... | collective-permute-start | bytes 110600 | tf_op jit(solution)/shard_map/ppermute | solution.py:596
  41.8 5.6 %collective-permute-start.9 = (f32[9,8,128]{2,1,0:T(8,128)S(1)}, f32[9,8,128]{2,1,0:T(8,128)S(1)}, u32[]{:S(2)}, u32[]{:S(2)}) collective-permute-start(f32[9,8,128]{2,1,0:T(8,128)S(1)} %get-tuple-element.54), channel_id=1, source_target_pairs={{0,4},{1,5},{2,6},{3,7},{4,0},{5,1},{6,2},{7,3},{8,12},{9,13},{10,... | collective-permute-start | bytes 110600 | tf_op jit(solution)/shard_map/ppermute | solution.py:596
  44.1 9.1 %collective-permute-start.8 = (f32[16,8,128]{2,1,0:T(8,128)S(1)}, f32[16,8,128]{2,1,0:T(8,128)S(1)}, u32[]{:S(2)}, u32[]{:S(2)}) collective-permute-start(f32[16,8,128]{2,1,0:T(8,128)S(1)} %get-tuple-element.53), channel_id=1, source_target_pairs={{0,15},{1,2},{2,1},{3,4},{4,3},{5,6},{6,5},{7,8},{8,7},{9,10},{10,... | collective-permute-start | bytes 196616 | tf_op jit(solution)/shard_map/ppermute | solution.py:603
  47.4 5.7 %collective-permute-start.12 = (f32[4,9,8,128]{3,2,1,0:T(8,128)S(1)}, f32[4,9,8,128]{3,2,1,0:T(8,128)S(1)}, u32[]{:S(2)}, u32[]{:S(2)}) collective-permute-start(f32[4,9,8,128]{3,2,1,0:T(8,128)S(1)} %pad_maximum_fusion.2), channel_id=1, source_target_pairs={{0,2},{1,3},{2,0},{3,1},{4,6},{5,7},{6,4},{7,5},{8,10},{9,11},{10,... | collective-permute-start | bytes 442376 | tf_op jit(solution)/shard_map/ppermute | solution.py:596
  53.2 1.7 %collective-permute-start.13 = (f32[8,9,8,128]{3,2,1,0:T(8,128)S(1)}, f32[8,9,8,128]{3,2,1,0:T(8,128)S(1)}, u32[]{:S(2)}, u32[]{:S(2)}) collective-permute-start(f32[8,9,8,128]{3,2,1,0:T(8,128)S(1)} %constant_dynamic-update-slice_fusion.near_side), channel_id=1, source_target_pairs={{0,1},{1,0},{2,3},{3,2},{4,5},{5,4},{6,7},{7,6},{8,9},{9,8},{10,11... | collective-permute-start | bytes 884744 | tf_op jit(solution)/shard_map/ppermute | solution.py:596
  53.3 1.7 %collective-permute-start.7 = (f32[16,8,128]{2,1,0:T(8,128)S(1)}, f32[16,8,128]{2,1,0:T(8,128)S(1)}, u32[]{:S(2)}, u32[]{:S(2)}) collective-permute-start(f32[16,8,128]{2,1,0:T(8,128)S(1)} %get-tuple-element.52), channel_id=1, source_target_pairs={{0,1},{1,0},{2,3},{3,2},{4,5},{5,4},{6,7},{7,6},{8,9},{9,8},{10,11... | collective-permute-start | bytes 196616 | tf_op jit(solution)/shard_map/ppermute | solution.py:596
  71.5 6.6 %collective-permute-start.18 = (f32[9,8,128]{2,1,0:T(8,128)S(1)}, f32[9,8,128]{2,1,0:T(8,128)S(1)}, u32[]{:S(2)}, u32[]{:S(2)}) collective-permute-start(f32[9,8,128]{2,1,0:T(8,128)S(1)} %get-tuple-element.63), channel_id=1, source_target_pairs={{0,12},{1,13},{2,14},{3,15},{4,8},{5,9},{6,10},{7,11},{8,4},{9,5},... | collective-permute-start | bytes 110600 | tf_op jit(solution)/shard_map/ppermute | solution.py:596
  73.3 5.3 %collective-permute-start.17 = (f32[9,8,128]{2,1,0:T(8,128)S(1)}, f32[9,8,128]{2,1,0:T(8,128)S(1)}, u32[]{:S(2)}, u32[]{:S(2)}) collective-permute-start(f32[9,8,128]{2,1,0:T(8,128)S(1)} %get-tuple-element.63), channel_id=1, source_target_pairs={{0,8},{1,9},{2,10},{3,11},{4,12},{5,13},{6,14},{7,15},{8,0},{9,1},... | collective-permute-start | bytes 110600 | tf_op jit(solution)/shard_map/ppermute | solution.py:596
  73.5 5.1 %collective-permute-start.16 = (f32[9,8,128]{2,1,0:T(8,128)S(1)}, f32[9,8,128]{2,1,0:T(8,128)S(1)}, u32[]{:S(2)}, u32[]{:S(2)}) collective-permute-start(f32[9,8,128]{2,1,0:T(8,128)S(1)} %get-tuple-element.63), channel_id=1, source_target_pairs={{0,4},{1,5},{2,6},{3,7},{4,0},{5,1},{6,2},{7,3},{8,12},{9,13},{10,... | collective-permute-start | bytes 110600 | tf_op jit(solution)/shard_map/ppermute | solution.py:596
  76.0 8.5 %collective-permute-start.15 = (f32[16,8,128]{2,1,0:T(8,128)S(1)}, f32[16,8,128]{2,1,0:T(8,128)S(1)}, u32[]{:S(2)}, u32[]{:S(2)}) collective-permute-start(f32[16,8,128]{2,1,0:T(8,128)S(1)} %get-tuple-element.62), channel_id=1, source_target_pairs={{0,15},{1,2},{2,1},{3,4},{4,3},{5,6},{6,5},{7,8},{8,7},{9,10},{10,... | collective-permute-start | bytes 196616 | tf_op jit(solution)/shard_map/ppermute | solution.py:603
  78.6 5.9 %collective-permute-start.19 = (f32[4,9,8,128]{3,2,1,0:T(8,128)S(1)}, f32[4,9,8,128]{3,2,1,0:T(8,128)S(1)}, u32[]{:S(2)}, u32[]{:S(2)}) collective-permute-start(f32[4,9,8,128]{3,2,1,0:T(8,128)S(1)} %pad_maximum_fusion.3), channel_id=1, source_target_pairs={{0,2},{1,3},{2,0},{3,1},{4,6},{5,7},{6,4},{7,5},{8,10},{9,11},{10,... | collective-permute-start | bytes 442376 | tf_op jit(solution)/shard_map/ppermute | solution.py:596
  84.5 1.7 %collective-permute-start.20 = (f32[8,9,8,128]{3,2,1,0:T(8,128)S(1)}, f32[8,9,8,128]{3,2,1,0:T(8,128)S(1)}, u32[]{:S(2)}, u32[]{:S(2)}) collective-permute-start(f32[8,9,8,128]{3,2,1,0:T(8,128)S(1)} %constant_dynamic-update-slice_fusion.5.near_side), channel_id=1, source_target_pairs={{0,1},{1,0},{2,3},{3,2},{4,5},{5,4},{6,7},{7,6},{8,9},{9,8},{10,11... | collective-permute-start | bytes 884744 | tf_op jit(solution)/shard_map/ppermute | solution.py:596
  84.6 1.7 %collective-permute-start.14 = (f32[16,8,128]{2,1,0:T(8,128)S(1)}, f32[16,8,128]{2,1,0:T(8,128)S(1)}, u32[]{:S(2)}, u32[]{:S(2)}) collective-permute-start(f32[16,8,128]{2,1,0:T(8,128)S(1)} %get-tuple-element.61), channel_id=1, source_target_pairs={{0,1},{1,0},{2,3},{3,2},{4,5},{5,4},{6,7},{7,6},{8,9},{9,8},{10,11... | collective-permute-start | bytes 196616 | tf_op jit(solution)/shard_map/ppermute | solution.py:596
  102.9 7.1 %collective-permute-start.25 = (f32[9,8,128]{2,1,0:T(8,128)S(1)}, f32[9,8,128]{2,1,0:T(8,128)S(1)}, u32[]{:S(2)}, u32[]{:S(2)}) collective-permute-start(f32[9,8,128]{2,1,0:T(8,128)S(1)} %get-tuple-element.75), channel_id=1, source_target_pairs={{0,12},{1,13},{2,14},{3,15},{4,8},{5,9},{6,10},{7,11},{8,4},{9,5},... | collective-permute-start | bytes 110600 | tf_op jit(solution)/shard_map/ppermute | solution.py:596
  105.1 4.9 %collective-permute-start.24 = (f32[9,8,128]{2,1,0:T(8,128)S(1)}, f32[9,8,128]{2,1,0:T(8,128)S(1)}, u32[]{:S(2)}, u32[]{:S(2)}) collective-permute-start(f32[9,8,128]{2,1,0:T(8,128)S(1)} %get-tuple-element.75), channel_id=1, source_target_pairs={{0,8},{1,9},{2,10},{3,11},{4,12},{5,13},{6,14},{7,15},{8,0},{9,1},... | collective-permute-start | bytes 110600 | tf_op jit(solution)/shard_map/ppermute | solution.py:596
  105.1 4.9 %collective-permute-start.23 = (f32[9,8,128]{2,1,0:T(8,128)S(1)}, f32[9,8,128]{2,1,0:T(8,128)S(1)}, u32[]{:S(2)}, u32[]{:S(2)}) collective-permute-start(f32[9,8,128]{2,1,0:T(8,128)S(1)} %get-tuple-element.75), channel_id=1, source_target_pairs={{0,4},{1,5},{2,6},{3,7},{4,0},{5,1},{6,2},{7,3},{8,12},{9,13},{10,... | collective-permute-start | bytes 110600 | tf_op jit(solution)/shard_map/ppermute | solution.py:596
  107.4 8.6 %collective-permute-start.22 = (f32[16,8,128]{2,1,0:T(8,128)S(1)}, f32[16,8,128]{2,1,0:T(8,128)S(1)}, u32[]{:S(2)}, u32[]{:S(2)}) collective-permute-start(f32[16,8,128]{2,1,0:T(8,128)S(1)} %get-tuple-element.74), channel_id=1, source_target_pairs={{0,15},{1,2},{2,1},{3,4},{4,3},{5,6},{6,5},{7,8},{8,7},{9,10},{10,... | collective-permute-start | bytes 196616 | tf_op jit(solution)/shard_map/ppermute | solution.py:603
  110.1 5.9 %collective-permute-start.26 = (f32[4,9,8,128]{3,2,1,0:T(8,128)S(1)}, f32[4,9,8,128]{3,2,1,0:T(8,128)S(1)}, u32[]{:S(2)}, u32[]{:S(2)}) collective-permute-start(f32[4,9,8,128]{3,2,1,0:T(8,128)S(1)} %pad_maximum_fusion.4), channel_id=1, source_target_pairs={{0,2},{1,3},{2,0},{3,1},{4,6},{5,7},{6,4},{7,5},{8,10},{9,11},{10,... | collective-permute-start | bytes 442376 | tf_op jit(solution)/shard_map/ppermute | solution.py:596
  115.9 1.7 %collective-permute-start.27 = (f32[8,9,8,128]{3,2,1,0:T(8,128)S(1)}, f32[8,9,8,128]{3,2,1,0:T(8,128)S(1)}, u32[]{:S(2)}, u32[]{:S(2)}) collective-permute-start(f32[8,9,8,128]{3,2,1,0:T(8,128)S(1)} %constant_dynamic-update-slice_fusion.10.near_side), channel_id=1, source_target_pairs={{0,1},{1,0},{2,3},{3,2},{4,5},{5,4},{6,7},{7,6},{8,9},{9,8},{10,11... | collective-permute-start | bytes 884744 | tf_op jit(solution)/shard_map/ppermute | solution.py:596
  116.0 1.7 %collective-permute-start.21 = (f32[16,8,128]{2,1,0:T(8,128)S(1)}, f32[16,8,128]{2,1,0:T(8,128)S(1)}, u32[]{:S(2)}, u32[]{:S(2)}) collective-permute-start(f32[16,8,128]{2,1,0:T(8,128)S(1)} %get-tuple-element.73), channel_id=1, source_target_pairs={{0,1},{1,0},{2,3},{3,2},{4,5},{5,4},{6,7},{7,6},{8,9},{9,8},{10,11... | collective-permute-start | bytes 196616 | tf_op jit(solution)/shard_map/ppermute | solution.py:596
  134.1 5.5 %collective-permute-start.30 = (f32[1,8,128]{2,1,0:T(8,128)S(1)}, f32[1,8,128]{2,1,0:T(8,128)S(1)}, u32[]{:S(2)}, u32[]{:S(2)}) collective-permute-start(f32[1,8,128]{2,1,0:T(8,128)S(1)} %get-tuple-element.78), channel_id=1, source_target_pairs={{0,12},{1,13},{2,14},{3,15},{4,8},{5,9},{6,10},{7,11},{8,4},{9,5},... | collective-permute-start | bytes 12296 | tf_op jit(solution)/shard_map/ppermute | solution.py:596
  136.1 4.5 %collective-permute-start.29 = (f32[1,8,128]{2,1,0:T(8,128)S(1)}, f32[1,8,128]{2,1,0:T(8,128)S(1)}, u32[]{:S(2)}, u32[]{:S(2)}) collective-permute-start(f32[1,8,128]{2,1,0:T(8,128)S(1)} %get-tuple-element.78), channel_id=1, source_target_pairs={{0,8},{1,9},{2,10},{3,11},{4,12},{5,13},{6,14},{7,15},{8,0},{9,1},... | collective-permute-start | bytes 12296 | tf_op jit(solution)/shard_map/ppermute | solution.py:596
  136.3 4.3 %collective-permute-start.28 = (f32[1,8,128]{2,1,0:T(8,128)S(1)}, f32[1,8,128]{2,1,0:T(8,128)S(1)}, u32[]{:S(2)}, u32[]{:S(2)}) collective-permute-start(f32[1,8,128]{2,1,0:T(8,128)S(1)} %get-tuple-element.78), channel_id=1, source_target_pairs={{0,4},{1,5},{2,6},{3,7},{4,0},{5,1},{6,2},{7,3},{8,12},{9,13},{10,... | collective-permute-start | bytes 12296 | tf_op jit(solution)/shard_map/ppermute | solution.py:596
  140.6 3.7 %collective-permute-start.31 = (f32[4,1,8,128]{3,2,1,0:T(8,128)S(1)}, f32[4,1,8,128]{3,2,1,0:T(8,128)S(1)}, u32[]{:S(2)}, u32[]{:S(2)}) collective-permute-start(f32[4,1,8,128]{3,2,1,0:T(8,128)S(1)} %pad_maximum_fusion.5), channel_id=1, source_target_pairs={{0,2},{1,3},{2,0},{3,1},{4,6},{5,7},{6,4},{7,5},{8,10},{9,11},{10,... | collective-permute-start | bytes 49160 | tf_op jit(solution)/shard_map/ppermute | solution.py:596
  144.4 1.2 collective-permute-start.32
